TPU v7x, 32 devices: a whole 2x2x4 slice. The times are simulated.
32 devices in a mesh: lsec: 4 (over z), rsec: 2 (over y), mpo: 4 (over x, core).
Axes of the slice: x: 2, y: 2, z: 4, core: 2. Of those that a mesh axis runs over, the one named last changes fastest.
Arguments:
- wavefunction: bfloat16 [64, 128, 128], P(('lsec', 'rsec')), may hold values from -6 to 6
- left_env: bfloat16 [40, 16, 128, 128], P('mpo', 'lsec'), may hold values from -0.5 to 0.5
- right_env: bfloat16 [40, 8, 128, 128], P('mpo', 'rsec'), may hold values from -0.125 to 0.125
- left_sizes: int32 [16], P('lsec'), may hold values from 64 to 128
- right_sizes: int32 [8], P('rsec'), may hold values from 64 to 128
- tile_left: int32 [64], P(('lsec', 'rsec')), may hold values from 0 to 3
- tile_right: int32 [64], P(('lsec', 'rsec')), may hold values from 0 to 3
- send_slot: int32 [40, 64], P('mpo', ('lsec', 'rsec')), may hold values from 0 to 8, as said below
- recv_tile: int32 [4, 64], P('mpo', ('lsec', 'rsec')), may hold values from 0 to 8, as said below
Outputs:
- hpsi: bfloat16 [64, 128, 128], P(('lsec', 'rsec', 'mpo'))
Inputs may be any that keep to these rules, and one draw needn't show every extreme that they name: `send_slot`: the value 8 means that the MPO bond index has no block on the tile; any other value q is a device pair index l * (devices along rsec) + r. `recv_tile`: entry [m, q * 8 + s] is the tile on pair q into which pair s adds its slot for q under mpo index m, and 8 exactly where no entry of send_slot of pair s in group m names q.
All inputs are finite; a program needn't handle non-finite values.
Results may differ from a plain program's by a relative error of at most 0.0075.
Values may be sent and summed in bfloat16 or wider, within the bound.
No kernel may reach another device: no remote copies, remote signals or barrier semaphores. Data moves between devices by JAX's collectives and lax.ppermute only.
A program may use at most 64 MiB of HBM per device.

v0:
```python
import jax
import jax.numpy as jnp
from jax import lax
from jax.sharding import PartitionSpec as P


def per_device(
    wavefunction,
    left_env,
    right_env,
    left_sizes,
    right_sizes,
    tile_left,
    tile_right,
    send_slot,
    recv_tile,
):
    tile_dev = wavefunction.shape[0]
    states = wavefunction.shape[1]
    left_count = left_env.shape[1]
    right_count = right_env.shape[1]
    peer_count = lax.axis_size(("lsec", "rsec"))
    left_pick = (tile_left[:, None] == jnp.arange(left_count, dtype=jnp.int32)[None, :]).astype(
        jnp.int32
    )
    right_pick = (tile_right[:, None] == jnp.arange(right_count, dtype=jnp.int32)[None, :]).astype(
        jnp.int32
    )
    live_rows = jnp.sum(left_pick * left_sizes[None, :], axis=1)
    live_cols = jnp.sum(right_pick * right_sizes[None, :], axis=1)
    position = jnp.arange(states, dtype=jnp.int32)
    inside = (position[None, :, None] < live_rows[:, None, None]) & (
        position[None, None, :] < live_cols[:, None, None]
    )
    masked = jnp.where(inside, wavefunction, jnp.zeros_like(wavefunction))
    left_blocks = jnp.take(left_env, tile_left, axis=1)
    right_blocks = jnp.take(right_env, tile_right, axis=1)
    right_done = jnp.einsum(
        "tpq,atrq->atpr", masked, right_blocks, preferred_element_type=jnp.float32
    ).astype(jnp.bfloat16)
    coupled = jnp.einsum(
        "atop,atpr->ator", left_blocks, right_done, preferred_element_type=jnp.float32
    )
    slot_ids = send_slot.reshape(-1)
    buffer = jax.ops.segment_sum(
        coupled.reshape(-1, states, states), slot_ids, num_segments=peer_count + 1
    )
    outgoing = buffer[:peer_count].astype(jnp.bfloat16)
    received = lax.all_to_all(outgoing, ("lsec", "rsec"), split_axis=0, concat_axis=0, tiled=True)
    chooser = (recv_tile[0][None, :] == jnp.arange(tile_dev, dtype=jnp.int32)[:, None]).astype(
        jnp.bfloat16
    )
    partial_sum = jnp.dot(
        chooser, received.reshape(peer_count, states * states), preferred_element_type=jnp.float32
    )
    partial_sum = partial_sum.reshape(tile_dev, states, states)
    my_share = lax.psum_scatter(
        partial_sum.astype(jnp.bfloat16), "mpo", scatter_dimension=0, tiled=True
    ).astype(jnp.float32)
    my_count = my_share.shape[0]
    my_start = lax.axis_index("mpo") * my_count
    inside_share = lax.dynamic_slice_in_dim(inside, my_start, my_count, 0)
    return jnp.where(inside_share, my_share, jnp.zeros_like(my_share)).astype(jnp.bfloat16)


def solution(mesh):
    placed = (
        P(("lsec", "rsec"), None, None),
        P("mpo", "lsec", None, None),
        P("mpo", "rsec", None, None),
        P("lsec"),
        P("rsec"),
        P(("lsec", "rsec")),
        P(("lsec", "rsec")),
        P("mpo", ("lsec", "rsec")),
        P("mpo", ("lsec", "rsec")),
    )
    return jax.shard_map(
        per_device,
        mesh=mesh,
        in_specs=placed,
        out_specs=P(("lsec", "rsec", "mpo"), None, None),
        check_vma=False,
    )
```

profile of v0, /device:TPU:0, one launch (start us, length us, event | category | flops | bytes accessed | tf_op | source)
XLA Modules:
  0.0 85.0 jit_solution(117284969057569916)
XLA Ops:
  6.5 0.0 copy-start
  6.5 0.0 reduce-scatter.2.cloned.1.call-start
  6.5 0.8 compare_select_fusion
  7.3 0.7 compare_and_fusion
  8.0 0.7 compare_select_fusion.1
  8.6 0.7 compare_and_fusion.1
  9.3 0.8 select_reduce_fusion
  10.0 0.8 select_reduce_fusion.1
  10.8 0.8 copy.23
  11.6 0.1 reshape.83
  11.7 0.1 iota_compare_fusion.1
  11.7 0.0 copy-done
  11.7 0.0 copy-start.1
  11.8 2.4 %gather_fusion = bf16[8,10,128,128]{3,2,1,0:T(8,128)(2,1)} fusion(bf16[10,4,128,128]{3,2,1,0:T(8,128)(2,1)S(1)} %copy-done, s32[1024]{0:T(1024)S(1)} %pad_clamp_fusion.1), kind=kCustom, calls=%fused_computation.clone | custom fusion | bytes 5242912 | tf_op jit(solution)/shard_map/jit(_take)/gather | solution.py:36
  14.1 0.0 copy-done.1
  14.1 2.4 %gather_fusion.1 = bf16[8,10,128,128]{3,2,1,0:T(8,128)(2,1)} fusion(bf16[10,4,128,128]{3,2,1,0:T(8,128)(2,1)S(1)} %copy-done.1, s32[1024]{0:T(1024)S(1)} %pad_clamp_fusion), kind=kCustom, calls=%fused_computation.1.clone | custom fusion | bytes 5242912 | tf_op jit(solution)/shard_map/jit(_take)/gather | solution.py:37
  16.6 0.0 copy-start.2
  16.6 5.4 %select_bitcast_fusion = (bf16[10,8,128,128]{3,2,0,1:T(8,128)(2,1)}, bf16[10,8,128,128]{3,2,0,1:T(8,128)(2,1)}) fusion(bf16[8,10,128,128]{3,2,1,0:T(8,128)(2,1)} %gather_fusion.1, pred[8]{0:T(512)(128)(4,1)S(1)} %compare_and_fusion, bf16[8,10,128,128]{3,2,1,0:T(8,128)(2,1)} %gather_fusion, pred[8]{0:T(512)(128)(4,1)S(1)} %compare_and_fusion.1), kind=kLoop, calls=%fused_computation.8 | loop fusion | flops 2621440 | bytes 10485776 | tf_op jit(solution)/shard_map/jit(_take)/select_n | solution.py:37
  22.0 0.0 copy-done.2
  22.0 7.5 %fusion = f32[10,8,128,128]{3,2,1,0:T(8,128)} fusion(bf16[10,8,128,128]{3,2,0,1:T(8,128)(2,1)} %get-tuple-element.7, bf16[10,8,128,128]{3,2,0,1:T(8,128)(2,1)} %get-tuple-element.6, bf16[8,128,128]{2,1,0:T(8,128)(2,1)S(1)} %copy-done.2, pred[8,128]{1,0:T(8,128)(4,1)S(1)} %get-tuple-element.8, pred[8,128]{1,0:T(8,128)(4,1)S(1)} %get-tuple-element.9), kind=kOutput, calls=%fused_computation.3 | convolution fusion | flops 672661504 | bytes 10749952 | tf_op jit(solution)/shard_map/atop,atpr->ator/dot_general | solution.py:41
  29.6 0.0 copy-start.3
  29.6 10.8 %scatter_fusion = f32[9,128,128]{2,1,0:T(8,128)S(1)} fusion(f32[9,128,128]{2,1,0:T(8,128)S(1)} %broadcast_in_dim.12, s32[80]{0:T(128)S(1)} %reshape.83, f32[80,128,128]{2,1,0:T(8,128)} %bitcast.25), kind=kCustom, calls=%fused_computation.2 | custom fusion | flops 1310720 | bytes 15728960 | tf_op jit(solution)/shard_map/scatter-add | solution.py:45
  40.5 16.0 %all_to_all.5 = bf16[8,128,128]{2,1,0:T(8,128)(2,1)S(1)} all-to-all(bf16[8,128,128]{2,1,0:T(8,128)(2,1)S(1)} %slice.11), channel_id=1, replica_groups=mesh['lsec'=4,'rsec'=2,'mpo'=4] {'lsec','rsec'}, dimensions={0} | all-to-all | bytes 524288 | tf_op jit(solution)/shard_map/all_to_all | solution.py:49
  56.5 0.0 copy-done.3
  56.5 0.3 convolution_convert_fusion
  56.8 0.7 copy.27
  57.5 0.0 reduce-scatter.2.cloned.1.call-update
  57.5 0.2 broadcast_and_fusion
  57.7 19.0 %reduce-scatter.2.cloned.1.call-done = bf16[2,128,128]{2,1,0:T(8,128)(2,1)} async-done(((bf16[8,128,128]{2,1,0:T(8,128)(2,1)}), bf16[2,128,128]{2,1,0:T(8,128)(2,1)}) %reduce-scatter.2.cloned.1.call-update) | async-done | bytes 65552 | tf_op jit(solution)/shard_map/reduce_scatter | solution.py:57
  76.7 1.5 %select_convert_fusion = bf16[2,128,128]{2,1,0:T(8,128)(2,1)} fusion(bf16[2,128,128]{2,1,0:T(8,128)(2,1)} %reduce-scatter.2.cloned.1.call-done, pred[8,128,128]{2,1,0:T(8,128)(4,1)S(1)} %broadcast_and_fusion, s32[]{:T(128)S(6)} %select_n.18), kind=kLoop, calls=%fused_computation.18 | loop fusion | flops 98304 | bytes 163844 | tf_op jit(solution)/shard_map/convert_element_type | solution.py:63
  (4 shorter events, 0.1 us)
Async XLA Ops:
  6.5 5.2 %copy-start = (bf16[10,4,128,128]{3,2,1,0:T(8,128)(2,1)S(1)}, bf16[10,4,128,128]{3,2,1,0:T(8,128)(2,1)}, u32[]{:S(2)}) copy-start(bf16[10,4,128,128]{3,2,1,0:T(8,128)(2,1)} %param.12) | copy-start | bytes 3932164
  6.5 70.2 %reduce-scatter.2.cloned.1.call-start = ((), (), s32[]{:S(2)}) async-start(), calls=%async_computation.2 | async-start | bytes 327680 | tf_op jit(solution)/shard_map/reduce_scatter | solution.py:57
  11.7 2.4 %copy-start.1 = (bf16[10,4,128,128]{3,2,1,0:T(8,128)(2,1)S(1)}, bf16[10,4,128,128]{3,2,1,0:T(8,128)(2,1)}, u32[]{:S(2)}) copy-start(bf16[10,4,128,128]{3,2,1,0:T(8,128)(2,1)} %param.13) | copy-start | bytes 3932164
  16.6 5.4 %copy-start.2 = (bf16[8,128,128]{2,1,0:T(8,128)(2,1)S(1)}, bf16[8,128,128]{2,1,0:T(8,128)(2,1)}, u32[]{:S(2)}) copy-start(bf16[8,128,128]{2,1,0:T(8,128)(2,1)} %param.11) | copy-start | bytes 786436
  29.6 26.9 %copy-start.3 = (s32[1,8]{1,0:T(1,128)S(1)}, s32[1,8]{1,0:T(1,128)}, u32[]{:S(2)}) copy-start(s32[1,8]{1,0:T(1,128)} %param.19) | copy-start | bytes 100
Sparse Core Ops, SparseCore 0:
  57.6 19.0 reduce-scatter.1
where the time goes:
time: 85.5 us; the launch traced here: 85 us
  other arithmetic  22.3 us (26%)
  waiting for transfers between devices  19 us (22%)
  blocking collectives  16 us (19%)
  between operations  13.5 us (16%)
  matrix products  7.79 us (9%)
  local copies, waits for them, and re-layouts  6.52 us (8%)
    reduce_scatter x1, waiting for transfers between devices, per_device(): lax.psum_scatter(partial_sum.astype(jnp.bfloat16), 'mpo', scatter_dimensi...  19 us
    all_to_all x1, blocking collectives, per_device(): lax.all_to_all(outgoing, ('lsec', 'rsec'), split_axis=0, concat_axis=0, t...  16 us
    scatter-add x1, other arithmetic, per_device(): jax.ops.segment_sum(coupled.reshape(-1, states, states), slot_ids, num_se...  10.8 us
    dot_general x1, matrix products, per_device(): jnp.einsum('atop,atpr->ator', left_blocks, right_done, preferred_element_...  7.53 us
    select_n x2, other arithmetic, per_device(): right_blocks = jnp.take(right_env, tile_right, axis=1)  6.18 us
    gather x1, local copies, waits for them, and re-layouts, per_device(): right_blocks = jnp.take(right_env, tile_right, axis=1)  2.45 us
    gather x1, local copies, waits for them, and re-layouts, per_device(): left_blocks = jnp.take(left_env, tile_left, axis=1)  2.39 us
  transfers between devices with their start and end apart: 1, of which 1 were waited for; matrix products, arithmetic and copies ran while one was open for 0% of the time, Pallas kernels for 0%

commit v1 on v0

v1 whole, which is shorter than its diff:
```python
import functools

import jax
import jax.numpy as jnp
from jax import lax
from jax.experimental import pallas as pl
from jax.experimental.pallas import tpu as pltpu
from jax.sharding import PartitionSpec as P

SMEM = pl.BlockSpec(memory_space=pltpu.SMEM)
VMEM = pl.BlockSpec(memory_space=pltpu.VMEM)
ANY = pl.BlockSpec(memory_space=pl.ANY)


def inside(states, rows, cols):
    at_row = lax.broadcasted_iota(jnp.int32, (states, states), 0)
    at_col = lax.broadcasted_iota(jnp.int32, (states, states), 1)
    return (at_row < rows) & (at_col < cols)


def couple_kernel(
    groups,
    tile_left,
    tile_right,
    left_sizes,
    right_sizes,
    send_slot,
    wave_hbm,
    left_hbm,
    right_hbm,
    *rest,
):
    outs = rest[: len(groups)]
    wave, left, right, masked, done, total, wave_sem, left_sem, right_sem = rest[len(groups) :]
    bonds, tiles, states = left.shape[0], wave.shape[0], wave.shape[1]
    wave_copy = pltpu.make_async_copy(wave_hbm, wave, wave_sem)
    wave_copy.start()

    def copies(a):
        return (
            pltpu.make_async_copy(right_hbm.at[a], right.at[a], right_sem.at[a]),
            pltpu.make_async_copy(left_hbm.at[a], left.at[a], left_sem.at[a]),
        )

    for a in range(bonds):
        for copy in copies(a):
            copy.start()
    total[...] = jnp.zeros_like(total)
    wave_copy.wait()
    for g in range(tiles):
        keep = inside(states, left_sizes[tile_left[g]], right_sizes[tile_right[g]])
        tile = wave[g].astype(jnp.float32)
        masked[g] = jnp.where(keep, tile, 0.0).astype(jnp.bfloat16)

    @pl.loop(0, bonds)
    def _(a):
        for copy in copies(a):
            copy.wait()
        for g in range(tiles):
            done[g] = lax.dot_general(
                masked[g],
                right[a, tile_right[g]],
                (((1,), (1,)), ((), ())),
                preferred_element_type=jnp.float32,
            ).astype(jnp.bfloat16)
        for g in range(tiles):
            q = send_slot[g, a]
            total[q] += jnp.dot(
                left[a, tile_left[g]], done[g], preferred_element_type=jnp.float32
            )

    for out, order in zip(outs, groups):
        for j, q in enumerate(order()):
            out[j] = total[q].astype(jnp.bfloat16)


def couple(groups, peers, tile_left, tile_right, left_sizes, right_sizes, send_slot, wave, left, right):
    tiles, states = wave.shape[0], wave.shape[1]
    bonds = left.shape[0]
    return pl.pallas_call(
        functools.partial(couple_kernel, [g for g, _ in groups]),
        out_shape=[
            jax.ShapeDtypeStruct((count, states, states), jnp.bfloat16) for _, count in groups
        ],
        in_specs=[SMEM] * 5 + [ANY] * 3,
        out_specs=[VMEM] * len(groups),
        scratch_shapes=[
            pltpu.VMEM(wave.shape, jnp.bfloat16),
            pltpu.VMEM(left.shape, jnp.bfloat16),
            pltpu.VMEM(right.shape, jnp.bfloat16),
            pltpu.VMEM(wave.shape, jnp.bfloat16),
            pltpu.VMEM(wave.shape, jnp.bfloat16),
            pltpu.VMEM((peers + 1, states, states), jnp.float32),
            pltpu.SemaphoreType.DMA,
            pltpu.SemaphoreType.DMA((bonds,)),
            pltpu.SemaphoreType.DMA((bonds,)),
        ],
        compiler_params=pltpu.CompilerParams(vmem_limit_bytes=40 * 1024 * 1024),
        name="couple",
    )(tile_left, tile_right, left_sizes, right_sizes, send_slot.T, wave, left, right)


def gather_kernel(n_left, own_table, other_table, *rest):
    received = rest[:n_left]
    give, keep, total = rest[n_left:]
    z, y = lax.axis_index("lsec"), lax.axis_index("rsec")
    c = lax.rem(lax.axis_index("mpo"), 2)
    total[...] = jnp.zeros_like(total)
    for k in range(n_left):
        source = 2 * jnp.bitwise_xor(z, k) + jnp.bitwise_xor(y, c)
        for j, table in enumerate((own_table, other_table)):
            t = table[0, source]
            total[t] += received[k][j].astype(jnp.float32)
    quarter = (total.shape[0] - 1) // 4
    for x in range(2):
        for j in range(quarter):
            give[x * quarter + j] = total[(2 * x + 1 - c) * quarter + j].astype(jnp.bfloat16)
            keep[x * quarter + j] = total[(2 * x + c) * quarter + j]


def gather(own_table, other_table, received, tiles):
    states = received[0].shape[1]
    return pl.pallas_call(
        functools.partial(gather_kernel, len(received)),
        out_shape=[
            jax.ShapeDtypeStruct((tiles // 2, states, states), jnp.bfloat16),
            jax.ShapeDtypeStruct((tiles // 2, states, states), jnp.float32),
        ],
        in_specs=[SMEM] * 2 + [VMEM] * len(received),
        out_specs=[VMEM] * 2,
        scratch_shapes=[pltpu.VMEM((tiles + 1, states, states), jnp.float32)],
        compiler_params=pltpu.CompilerParams(vmem_limit_bytes=16 * 1024 * 1024),
        name="gather",
    )(own_table, other_table, *received)


def cross_kernel(received, kept, give, keep):
    half = give.shape[0]
    x = lax.axis_index("mpo") // 2
    for j in range(half):
        away, here = (1 - x) * half + j, x * half + j
        give[j] = (kept[away] + received[away].astype(jnp.float32)).astype(jnp.bfloat16)
        keep[j] = kept[here] + received[here].astype(jnp.float32)


def cross(received, kept):
    half, states = kept.shape[0] // 2, kept.shape[1]
    return pl.pallas_call(
        cross_kernel,
        out_shape=[
            jax.ShapeDtypeStruct((half, states, states), jnp.bfloat16),
            jax.ShapeDtypeStruct((half, states, states), jnp.float32),
        ],
        in_specs=[VMEM] * 2,
        out_specs=[VMEM] * 2,
        compiler_params=pltpu.CompilerParams(vmem_limit_bytes=8 * 1024 * 1024),
        name="cross",
    )(received, kept)


def finish_kernel(tile_left, tile_right, left_sizes, right_sizes, received, kept, out):
    share, states = out.shape[0], out.shape[1]
    m = lax.axis_index("mpo")
    for j in range(share):
        h = m * share + j
        live = inside(states, left_sizes[tile_left[h]], right_sizes[tile_right[h]])
        out[j] = jnp.where(live, kept[j] + received[j].astype(jnp.float32), 0.0).astype(
            jnp.bfloat16
        )


def finish(tile_left, tile_right, left_sizes, right_sizes, received, kept):
    return pl.pallas_call(
        finish_kernel,
        out_shape=jax.ShapeDtypeStruct(kept.shape, jnp.bfloat16),
        in_specs=[SMEM] * 4 + [VMEM] * 2,
        out_specs=VMEM,
        compiler_params=pltpu.CompilerParams(vmem_limit_bytes=8 * 1024 * 1024),
        name="finish",
    )(tile_left, tile_right, left_sizes, right_sizes, received, kept)


def by_permutes(sizes, wave, left, right, left_sizes, right_sizes, tile_left, tile_right, send_slot, recv_tile):
    n_left, n_right, n_mpo = sizes
    axes = ("lsec", "rsec", "mpo")
    place = lambda z, y, m: (z * n_right + y) * n_mpo + m
    every = [(z, y, m) for z in range(n_left) for y in range(n_right) for m in range(n_mpo)]
    swap_core = [(m, m ^ 1) for m in range(n_mpo)]
    swap_chip = [(m, m ^ 2) for m in range(n_mpo)]
    other_table = lax.ppermute(recv_tile, "mpo", swap_core)

    def towards(flip):
        def order():
            z, y = lax.axis_index("lsec"), lax.axis_index("rsec")
            c = jnp.bitwise_xor(lax.rem(lax.axis_index("mpo"), 2), flip)
            return [
                jnp.bitwise_xor(z, k) * n_right + jnp.bitwise_xor(y, c) for k in range(n_left)
            ]

        return order

    give, keep = couple(
        [(towards(1), n_left), (towards(0), n_left)],
        n_left * n_right,
        tile_left, tile_right, left_sizes, right_sizes, send_slot, wave, left, right,
    )
    got = lax.ppermute(give, "mpo", swap_core)
    received = []
    for k in range(n_left):
        pair = jnp.stack([keep[k], got[k]])
        perm = [(place(z, y, m), place(z ^ k, y ^ (m % 2), m)) for z, y, m in every]
        received.append(lax.ppermute(pair, axes, perm))
    give, keep = gather(recv_tile, other_table, received, wave.shape[0])
    give, keep = cross(lax.ppermute(give, "mpo", swap_core), keep)
    return finish(
        tile_left, tile_right, left_sizes, right_sizes, lax.ppermute(give, "mpo", swap_chip), keep
    )


def by_exchange(sizes, wave, left, right, left_sizes, right_sizes, tile_left, tile_right, send_slot, recv_tile):
    peers = sizes[0] * sizes[1]
    tiles, states = wave.shape[0], wave.shape[1]
    (outgoing,) = couple(
        [(lambda: list(range(peers)), peers)],
        peers,
        tile_left, tile_right, left_sizes, right_sizes, send_slot, wave, left, right,
    )
    received = lax.all_to_all(outgoing, ("lsec", "rsec"), split_axis=0, concat_axis=0, tiled=True)
    chooser = (recv_tile[0][None, :] == jnp.arange(tiles, dtype=jnp.int32)[:, None]).astype(
        jnp.bfloat16
    )
    partial = jnp.dot(
        chooser, received.reshape(peers, states * states), preferred_element_type=jnp.float32
    )
    partial = partial.reshape(tiles, states, states).astype(jnp.bfloat16)
    share = lax.psum_scatter(partial, "mpo", scatter_dimension=0, tiled=True)
    start = lax.axis_index("mpo") * share.shape[0]
    at = lambda table, sizes_of: lax.dynamic_slice_in_dim(sizes_of[table], start, share.shape[0], 0)
    rows, cols = at(tile_left, left_sizes), at(tile_right, right_sizes)
    position = jnp.arange(states, dtype=jnp.int32)
    live = (position[None, :, None] < rows[:, None, None]) & (
        position[None, None, :] < cols[:, None, None]
    )
    return jnp.where(live, share, jnp.zeros_like(share))


def solution(mesh):
    sizes = tuple(mesh.shape[axis] for axis in ("lsec", "rsec", "mpo"))
    few = sizes[1] == 2 and sizes[2] == 4 and sizes[0] in (2, 4)
    placed = (
        P(("lsec", "rsec"), None, None),
        P("mpo", "lsec", None, None),
        P("mpo", "rsec", None, None),
        P("lsec"),
        P("rsec"),
        P(("lsec", "rsec")),
        P(("lsec", "rsec")),
        P("mpo", ("lsec", "rsec")),
        P("mpo", ("lsec", "rsec")),
    )
    return jax.shard_map(
        functools.partial(by_permutes if few else by_exchange, sizes),
        mesh=mesh,
        in_specs=placed,
        out_specs=P(("lsec", "rsec", "mpo"), None, None),
        check_vma=False,
    )
```

time: 85.5 us -> 40.8 us (0.48)
  other arithmetic: 22.3 us -> 0.03 us
  blocking collectives: 16 us -> 0 us
  starting transfers between devices: 0.01 us -> 14.2 us
  between operations: 13.5 us -> 0.08 us
  Pallas kernels: 0 us -> 11.4 us
  waiting for transfers between devices: 19 us -> 7.92 us
  matrix products: 7.79 us -> 0 us
    reduce_scatter x1 -> x0, waiting for transfers between devices: 19 us -> none  [per_device(): lax.psum_scatter(partial_sum.astype(jnp.bfloat16), 'mpo', scatter_dimensi...]
    all_to_all x1 -> x0, blocking collectives: 16 us -> none  [per_device(): lax.all_to_all(outgoing, ('lsec', 'rsec'), split_axis=0, concat_axis=0, t...]
    ppermute x0 -> x8, starting transfers between devices: none -> 14.2 us  [the longest x4 6.38 us: by_permutes(): received.append(lax.ppermute(pair, axes, perm))]
    pallas_call x0 -> x4, Pallas kernels: none -> 11.4 us  [the longest x1 9.5 us: couple(): pl.pallas_call(functools.partial(couple_kernel, [g for g, _ in groups]),...]
    scatter-add x1 -> x0, other arithmetic: 10.8 us -> none  [per_device(): jax.ops.segment_sum(coupled.reshape(-1, states, states), slot_ids, num_se...]
    ppermute x0 -> x8, waiting for transfers between devices: none -> 7.92 us  [the longest x1 2.86 us: by_permutes(): lax.ppermute(give, 'mpo', swap_chip)]
    dot_general x2 -> x0, matrix products: 7.79 us -> none  [the longest x1 7.53 us: per_device(): jnp.einsum('atop,atpr->ator', left_blocks, right_done, preferred_element_...]
    select_n x3 -> x0, other arithmetic: 6.84 us -> none  [the longest x2 6.18 us: per_device(): right_blocks = jnp.take(right_env, tile_right, axis=1)]
  transfers between devices with their start and end apart: 1 -> 8, of which waited for: 1 -> 5; matrix products, arithmetic and copies ran while one was open for 0% -> 0% of each run, Pallas kernels for 0% -> 0%
where the time goes in v1:
time: 40.8 us; the launch traced here: 40.5 us
  starting transfers between devices  14.2 us (35%)
  Pallas kernels  11.4 us (28%)
  waiting for transfers between devices  7.92 us (19%)
  local copies, waits for them, and re-layouts  6.91 us (17%)
    pallas_call x1, Pallas kernels, couple(): pl.pallas_call(functools.partial(couple_kernel, [g for g, _ in groups]),...  9.5 us
    unnamed x18, local copies, waits for them, and re-layouts  6.89 us
    ppermute x4, starting transfers between devices, by_permutes(): received.append(lax.ppermute(pair, axes, perm))  6.38 us
    ppermute x1, starting transfers between devices, by_permutes(): other_table = lax.ppermute(recv_tile, 'mpo', swap_core)  3.03 us
    ppermute x1, waiting for transfers between devices, by_permutes(): lax.ppermute(give, 'mpo', swap_chip)  2.86 us
    ppermute x1, starting transfers between devices, by_permutes(): give, keep = cross(lax.ppermute(give, 'mpo', swap_core), keep)  2.68 us
    ppermute x4, waiting for transfers between devices, by_permutes(): received.append(lax.ppermute(pair, axes, perm))  2.28 us
    ppermute x1, starting transfers between devices, by_permutes(): lax.ppermute(give, 'mpo', swap_chip)  1.57 us
  transfers between devices with their start and end apart: 8, of which 5 were waited for; matrix products, arithmetic and copies ran while one was open for 0% of the time, Pallas kernels for 0%

profile of v1, /device:TPU:0, one launch (start us, length us, event | category | flops | bytes accessed | tf_op | source)
XLA Modules:
  0.0 40.5 jit_solution(12087655137503940894)
XLA Ops:
  0.0 0.0 copy-start
  0.0 1.3 %copy-done = bf16[10,4,128,128]{3,2,1,0:T(8,128)(2,1)S(1)} copy-done((bf16[10,4,128,128]{3,2,1,0:T(8,128)(2,1)S(1)}, bf16[10,4,128,128]{3,2,1,0:T(8,128)(2,1)}, u32[]{:S(2)}) %copy-start) | copy-done | bytes 1310744
  1.3 0.0 copy-start.1
  1.3 1.3 %copy-done.1 = bf16[10,4,128,128]{3,2,1,0:T(8,128)(2,1)S(1)} copy-done((bf16[10,4,128,128]{3,2,1,0:T(8,128)(2,1)S(1)}, bf16[10,4,128,128]{3,2,1,0:T(8,128)(2,1)}, u32[]{:S(2)}) %copy-start.1) | copy-done | bytes 1310744
  2.6 0.0 copy-start.2
  2.6 0.9 %copy-done.2 = bf16[8,128,128]{2,1,0:T(8,128)(2,1)S(1)} copy-done((bf16[8,128,128]{2,1,0:T(8,128)(2,1)S(1)}, bf16[8,128,128]{2,1,0:T(8,128)(2,1)}, u32[]{:S(2)}) %copy-start.2) | copy-done | bytes 262168
  3.6 0.0 copy-start.3
  3.6 0.7 %copy-done.3 = s32[10,8]{0,1:T(8,128)S(1)} copy-done((s32[10,8]{0,1:T(8,128)S(1)}, s32[10,8]{0,1:T(8,128)}, u32[]{:S(2)}) %copy-start.3) | copy-done | bytes 344
  4.3 0.7 %copy-done.4 = s32[8]{0:T(128)S(1)} copy-done((s32[8]{0:T(128)S(1)}, s32[8]{0:T(128)}, u32[]{:S(2)}) %copy-start.4) | copy-done | bytes 56
  4.9 0.7 %copy-done.5 = s32[8]{0:T(128)S(1)} copy-done((s32[8]{0:T(128)S(1)}, s32[8]{0:T(128)}, u32[]{:S(2)}) %copy-start.5) | copy-done | bytes 56
  5.6 0.7 %copy-done.6 = s32[4]{0:T(128)S(1)} copy-done((s32[4]{0:T(128)S(1)}, s32[4]{0:T(128)}, u32[]{:S(2)}) %copy-start.6) | copy-done | bytes 40
  6.2 0.7 %copy-done.7 = s32[4]{0:T(128)S(1)} copy-done((s32[4]{0:T(128)S(1)}, s32[4]{0:T(128)}, u32[]{:S(2)}) %copy-start.7) | copy-done | bytes 40
  6.9 9.5 %couple.1 = (bf16[4,128,128]{2,1,0:T(8,128)(2,1)S(1)}, bf16[4,128,128]{2,1,0:T(8,128)(2,1)S(1)}) custom-call(s32[8]{0:T(128)S(1)} %copy-done.4, s32[8]{0:T(128)S(1)} %copy-done.5, s32[4]{0:T(128)S(1)} %copy-done.6, s32[4]{0:T(128)S(1)} %copy-done.7, s32[8,10]{1,0:T(8,128)S(1)} %bitcast.1, bf16[8,128,128]{2,1,0:T(8,128)(2,1)S(1)} %copy-done.2, ...), custom_call_target="tpu_custom_call" | custom-call | tf_op jit(solution)/shard_map/couple/pallas_call | solution.py:80
  16.4 0.5 %collective-permute-start.1 = (bf16[4,128,128]{2,1,0:T(8,128)(2,1)S(1)}, bf16[4,128,128]{2,1,0:T(8,128)(2,1)S(1)}, u32[]{:S(2)}, u32[]{:S(2)}) collective-permute-start(bf16[4,128,128]{2,1,0:T(8,128)(2,1)S(1)} %get-tuple-element.12), channel_id=1, source_target_pairs={{0,1},{1,0},{2,3},{3,2},{4,5},{5,4},{6,7},{7,6},{8,9},{9,8},{10,11... | collective-permute-start | bytes 393224 | tf_op jit(solution)/shard_map/ppermute | solution.py:207
  16.9 1.0 %collective-permute-done.1 = bf16[4,128,128]{2,1,0:T(8,128)(2,1)S(1)} collective-permute-done((bf16[4,128,128]{2,1,0:T(8,128)(2,1)S(1)}, bf16[4,128,128]{2,1,0:T(8,128)(2,1)S(1)}, u32[]{:S(2)}, u32[]{:S(2)}) %collective-permute-start.1) | collective-permute-done | bytes 131104 | tf_op jit(solution)/shard_map/ppermute | solution.py:207
  17.9 0.7 %collective-permute-start.2 = (bf16[2,128,128]{2,1,0:T(8,128)(2,1)S(1)}, bf16[2,128,128]{2,1,0:T(8,128)(2,1)S(1)}, u32[]{:S(2)}, u32[]{:S(2)}) collective-permute-start(bf16[2,128,128]{2,1,0:T(8,128)(2,1)S(1)} %pad_maximum_fusion), channel_id=1, source_target_pairs={{0,0},{1,5},{2,2},{3,7},{4,4},{5,1},{6,6},{7,3},{8,8},{9,13},{10,1... | collective-permute-start | bytes 196616 | tf_op jit(solution)/shard_map/ppermute | solution.py:212
  18.6 3.0 %collective-permute-start.3 = (bf16[2,128,128]{2,1,0:T(8,128)(2,1)S(1)}, bf16[2,128,128]{2,1,0:T(8,128)(2,1)S(1)}, u32[]{:S(2)}, u32[]{:S(2)}) collective-permute-start(bf16[2,128,128]{2,1,0:T(8,128)(2,1)S(1)} %pad_maximum_fusion.1), channel_id=1, source_target_pairs={{0,8},{1,13},{2,10},{3,15},{4,12},{5,9},{6,14},{7,11},{8,0},{9,5},... | collective-permute-start | bytes 196616 | tf_op jit(solution)/shard_map/ppermute | solution.py:212
  21.6 2.7 %collective-permute-start.4 = (bf16[2,128,128]{2,1,0:T(8,128)(2,1)S(1)}, bf16[2,128,128]{2,1,0:T(8,128)(2,1)S(1)}, u32[]{:S(2)}, u32[]{:S(2)}) collective-permute-start(bf16[2,128,128]{2,1,0:T(8,128)(2,1)S(1)} %pad_maximum_fusion.2), channel_id=1, source_target_pairs={{0,16},{1,21},{2,18},{3,23},{4,20},{5,17},{6,22},{7,19},{8,24},{9,... | collective-permute-start | bytes 196616 | tf_op jit(solution)/shard_map/ppermute | solution.py:212
  24.3 0.1 collective-permute-start.5
  24.4 0.0 copy-done.8
  24.4 3.0 %collective-permute-start = (s32[1,8]{1,0:T(1,128)S(1)}, s32[1,8]{1,0:T(1,128)S(1)}, u32[]{:S(2)}, u32[]{:S(2)}) collective-permute-start(s32[1,8]{1,0:T(1,128)S(1)} %copy-done.8), channel_id=1, source_target_pairs={{0,1},{1,0},{2,3},{3,2},{4,5},{5,4},{6,7},{7,6},{8,9},{9,8},{10,11... | collective-permute-start | bytes 104 | tf_op jit(solution)/shard_map/ppermute | solution.py:190
  27.4 0.8 %collective-permute-done.other_table = s32[1,8]{1,0:T(1,128)S(1)} collective-permute-done((s32[1,8]{1,0:T(1,128)S(1)}, s32[1,8]{1,0:T(1,128)S(1)}, u32[]{:S(2)}, u32[]{:S(2)}) %collective-permute-start) | collective-permute-done | bytes 64 | tf_op jit(solution)/shard_map/ppermute | solution.py:190
  28.2 0.0 collective-permute-done.2.rest_0_
  28.2 0.0 collective-permute-done.3.rest_1_
  28.2 0.0 collective-permute-done.4.rest_2_
  28.2 2.3 %collective-permute-done.5.rest_3_ = bf16[2,128,128]{2,1,0:T(8,128)(2,1)S(1)} collective-permute-done((bf16[2,128,128]{2,1,0:T(8,128)(2,1)S(1)}, bf16[2,128,128]{2,1,0:T(8,128)(2,1)S(1)}, u32[]{:S(2)}, u32[]{:S(2)}) %collective-permute-start.5) | collective-permute-done | bytes 65568 | tf_op jit(solution)/shard_map/ppermute | solution.py:212
  30.5 0.7 %gather.1 = (bf16[4,128,128]{2,1,0:T(8,128)(2,1)S(1)}, f32[4,128,128]{2,1,0:T(8,128)S(1)}) custom-call(s32[1,8]{1,0:T(1,128)S(1)} %copy-done.8, s32[1,8]{1,0:T(1,128)S(1)} %collective-permute-done.other_table, bf16[2,128,128]{2,1,0:T(8,128)(2,1)S(1)} %collective-permute-done.2.rest_0_, bf16[2,128,128]{2,1,0:T(8,128)(2,1)S(1)} %collective-permute-done.3.rest_1_, ...), custom_call_target="tpu_custom_call" | custom-call | tf_op jit(solution)/shard_map/gather/pallas_call | solution.py:123
  31.2 2.7 %collective-permute-start.6 = (bf16[4,128,128]{2,1,0:T(8,128)(2,1)S(1)}, bf16[4,128,128]{2,1,0:T(8,128)(2,1)S(1)}, u32[]{:S(2)}, u32[]{:S(2)}) collective-permute-start(bf16[4,128,128]{2,1,0:T(8,128)(2,1)S(1)} %get-tuple-element.13), channel_id=1, source_target_pairs={{0,1},{1,0},{2,3},{3,2},{4,5},{5,4},{6,7},{7,6},{8,9},{9,8},{10,11... | collective-permute-start | bytes 393224 | tf_op jit(solution)/shard_map/ppermute | solution.py:214
  33.9 1.0 %collective-permute-done.6.received = bf16[4,128,128]{2,1,0:T(8,128)(2,1)S(1)} collective-permute-done((bf16[4,128,128]{2,1,0:T(8,128)(2,1)S(1)}, bf16[4,128,128]{2,1,0:T(8,128)(2,1)S(1)}, u32[]{:S(2)}, u32[]{:S(2)}) %collective-permute-start.6) | collective-permute-done | bytes 131104 | tf_op jit(solution)/shard_map/ppermute | solution.py:214
  34.9 1.6 %collective-permute-start.7 = (bf16[2,128,128]{2,1,0:T(8,128)(2,1)S(1)}, bf16[2,128,128]{2,1,0:T(8,128)(2,1)S(1)}, u32[]{:S(2)}, u32[]{:S(2)}) collective-permute-start(bf16[2,128,128]{2,1,0:T(8,128)(2,1)S(1)} %get-tuple-element.15), channel_id=1, source_target_pairs={{0,2},{1,3},{2,0},{3,1},{4,6},{5,7},{6,4},{7,5},{8,10},{9,11},{10,... | collective-permute-start | bytes 196616 | tf_op jit(solution)/shard_map/ppermute | solution.py:216
  36.5 2.9 %collective-permute-done.7.received = bf16[2,128,128]{2,1,0:T(8,128)(2,1)S(1)} collective-permute-done((bf16[2,128,128]{2,1,0:T(8,128)(2,1)S(1)}, bf16[2,128,128]{2,1,0:T(8,128)(2,1)S(1)}, u32[]{:S(2)}, u32[]{:S(2)}) %collective-permute-start.7) | collective-permute-done | bytes 65568 | tf_op jit(solution)/shard_map/ppermute | solution.py:216
  39.3 1.2 %finish.1 = bf16[2,128,128]{2,1,0:T(8,128)(2,1)} custom-call(s32[8]{0:T(128)S(1)} %copy-done.4, s32[8]{0:T(128)S(1)} %copy-done.5, s32[4]{0:T(128)S(1)} %copy-done.6, s32[4]{0:T(128)S(1)} %copy-done.7, bf16[2,128,128]{2,1,0:T(8,128)(2,1)S(1)} %collective-permute-done.7.received, f32[2,128,128]{2,1,0:T(8,128)S(1)} %get-tuple-element.16.kept), custom_call_target="tpu_custom_call" | custom-call | tf_op jit(solution)/shard_map/finish/pallas_call | solution.py:173
  (12 shorter events, 0.1 us)
Async XLA Ops:
  0.0 1.3 %copy-start = (bf16[10,4,128,128]{3,2,1,0:T(8,128)(2,1)S(1)}, bf16[10,4,128,128]{3,2,1,0:T(8,128)(2,1)}, u32[]{:S(2)}) copy-start(bf16[10,4,128,128]{3,2,1,0:T(8,128)(2,1)} %left_hbm.1) | copy-start | bytes 3932164
  1.3 1.3 %copy-start.1 = (bf16[10,4,128,128]{3,2,1,0:T(8,128)(2,1)S(1)}, bf16[10,4,128,128]{3,2,1,0:T(8,128)(2,1)}, u32[]{:S(2)}) copy-start(bf16[10,4,128,128]{3,2,1,0:T(8,128)(2,1)} %right_hbm.1) | copy-start | bytes 3932164
  2.6 0.9 %copy-start.2 = (bf16[8,128,128]{2,1,0:T(8,128)(2,1)S(1)}, bf16[8,128,128]{2,1,0:T(8,128)(2,1)}, u32[]{:S(2)}) copy-start(bf16[8,128,128]{2,1,0:T(8,128)(2,1)} %wave_hbm.1) | copy-start | bytes 786436
  3.6 0.7 %copy-start.3 = (s32[10,8]{0,1:T(8,128)S(1)}, s32[10,8]{0,1:T(8,128)}, u32[]{:S(2)}) copy-start(s32[10,8]{0,1:T(8,128)} %param.16) | copy-start | bytes 964
  4.3 0.7 %copy-start.4 = (s32[8]{0:T(128)S(1)}, s32[8]{0:T(128)}, u32[]{:S(2)}) copy-start(s32[8]{0:T(128)} %tile_left.3) | copy-start | bytes 100
  4.9 0.7 %copy-start.5 = (s32[8]{0:T(128)S(1)}, s32[8]{0:T(128)}, u32[]{:S(2)}) copy-start(s32[8]{0:T(128)} %tile_right.3) | copy-start | bytes 100
  5.6 0.7 %copy-start.6 = (s32[4]{0:T(128)S(1)}, s32[4]{0:T(128)}, u32[]{:S(2)}) copy-start(s32[4]{0:T(128)} %left_sizes.3) | copy-start | bytes 52
  6.2 0.7 %copy-start.7 = (s32[4]{0:T(128)S(1)}, s32[4]{0:T(128)}, u32[]{:S(2)}) copy-start(s32[4]{0:T(128)} %right_sizes.3) | copy-start | bytes 52
  6.9 17.5 %copy-start.8 = (s32[1,8]{1,0:T(1,128)S(1)}, s32[1,8]{1,0:T(1,128)}, u32[]{:S(2)}) copy-start(s32[1,8]{1,0:T(1,128)} %own_table.1) | copy-start | bytes 100
  16.4 1.5 %collective-permute-start.1 = (bf16[4,128,128]{2,1,0:T(8,128)(2,1)S(1)}, bf16[4,128,128]{2,1,0:T(8,128)(2,1)S(1)}, u32[]{:S(2)}, u32[]{:S(2)}) collective-permute-start(bf16[4,128,128]{2,1,0:T(8,128)(2,1)S(1)} %get-tuple-element.12), channel_id=1, source_target_pairs={{0,1},{1,0},{2,3},{3,2},{4,5},{5,4},{6,7},{7,6},{8,9},{9,8},{10,11... | collective-permute-start | bytes 393224 | tf_op jit(solution)/shard_map/ppermute | solution.py:207
  17.9 10.3 %collective-permute-start.2 = (bf16[2,128,128]{2,1,0:T(8,128)(2,1)S(1)}, bf16[2,128,128]{2,1,0:T(8,128)(2,1)S(1)}, u32[]{:S(2)}, u32[]{:S(2)}) collective-permute-start(bf16[2,128,128]{2,1,0:T(8,128)(2,1)S(1)} %pad_maximum_fusion), channel_id=1, source_target_pairs={{0,0},{1,5},{2,2},{3,7},{4,4},{5,1},{6,6},{7,3},{8,8},{9,13},{10,1... | collective-permute-start | bytes 196616 | tf_op jit(solution)/shard_map/ppermute | solution.py:212
  18.6 9.6 %collective-permute-start.3 = (bf16[2,128,128]{2,1,0:T(8,128)(2,1)S(1)}, bf16[2,128,128]{2,1,0:T(8,128)(2,1)S(1)}, u32[]{:S(2)}, u32[]{:S(2)}) collective-permute-start(bf16[2,128,128]{2,1,0:T(8,128)(2,1)S(1)} %pad_maximum_fusion.1), channel_id=1, source_target_pairs={{0,8},{1,13},{2,10},{3,15},{4,12},{5,9},{6,14},{7,11},{8,0},{9,5},... | collective-permute-start | bytes 196616 | tf_op jit(solution)/shard_map/ppermute | solution.py:212
  21.6 6.6 %collective-permute-start.4 = (bf16[2,128,128]{2,1,0:T(8,128)(2,1)S(1)}, bf16[2,128,128]{2,1,0:T(8,128)(2,1)S(1)}, u32[]{:S(2)}, u32[]{:S(2)}) collective-permute-start(bf16[2,128,128]{2,1,0:T(8,128)(2,1)S(1)} %pad_maximum_fusion.2), channel_id=1, source_target_pairs={{0,16},{1,21},{2,18},{3,23},{4,20},{5,17},{6,22},{7,19},{8,24},{9,... | collective-permute-start | bytes 196616 | tf_op jit(solution)/shard_map/ppermute | solution.py:212
  24.3 6.2 %collective-permute-start.5 = (bf16[2,128,128]{2,1,0:T(8,128)(2,1)S(1)}, bf16[2,128,128]{2,1,0:T(8,128)(2,1)S(1)}, u32[]{:S(2)}, u32[]{:S(2)}) collective-permute-start(bf16[2,128,128]{2,1,0:T(8,128)(2,1)S(1)} %pad_maximum_fusion.3), channel_id=1, source_target_pairs={{0,24},{1,29},{2,26},{3,31},{4,28},{5,25},{6,30},{7,27},{8,16},{9,... | collective-permute-start | bytes 196616 | tf_op jit(solution)/shard_map/ppermute | solution.py:212
  24.4 3.9 %collective-permute-start = (s32[1,8]{1,0:T(1,128)S(1)}, s32[1,8]{1,0:T(1,128)S(1)}, u32[]{:S(2)}, u32[]{:S(2)}) collective-permute-start(s32[1,8]{1,0:T(1,128)S(1)} %copy-done.8), channel_id=1, source_target_pairs={{0,1},{1,0},{2,3},{3,2},{4,5},{5,4},{6,7},{7,6},{8,9},{9,8},{10,11... | collective-permute-start | bytes 104 | tf_op jit(solution)/shard_map/ppermute | solution.py:190
  31.2 3.7 %collective-permute-start.6 = (bf16[4,128,128]{2,1,0:T(8,128)(2,1)S(1)}, bf16[4,128,128]{2,1,0:T(8,128)(2,1)S(1)}, u32[]{:S(2)}, u32[]{:S(2)}) collective-permute-start(bf16[4,128,128]{2,1,0:T(8,128)(2,1)S(1)} %get-tuple-element.13), channel_id=1, source_target_pairs={{0,1},{1,0},{2,3},{3,2},{4,5},{5,4},{6,7},{7,6},{8,9},{9,8},{10,11... | collective-permute-start | bytes 393224 | tf_op jit(solution)/shard_map/ppermute | solution.py:214
  34.9 4.4 %collective-permute-start.7 = (bf16[2,128,128]{2,1,0:T(8,128)(2,1)S(1)}, bf16[2,128,128]{2,1,0:T(8,128)(2,1)S(1)}, u32[]{:S(2)}, u32[]{:S(2)}) collective-permute-start(bf16[2,128,128]{2,1,0:T(8,128)(2,1)S(1)} %get-tuple-element.15), channel_id=1, source_target_pairs={{0,2},{1,3},{2,0},{3,1},{4,6},{5,7},{6,4},{7,5},{8,10},{9,11},{10,... | collective-permute-start | bytes 196616 | tf_op jit(solution)/shard_map/ppermute | solution.py:216

commit v2 on v1

--- a/solution.py
+++ b/solution.py
@@ -9,7 +9,11 @@
 
 SMEM = pl.BlockSpec(memory_space=pltpu.SMEM)
 VMEM = pl.BlockSpec(memory_space=pltpu.VMEM)
-ANY = pl.BlockSpec(memory_space=pl.ANY)
+HBM = pl.BlockSpec(memory_space=pltpu.HBM)
+
+
+def in_hbm(*arrays):
+    return [pltpu.with_memory_space_constraint(x, pltpu.HBM) for x in arrays]
 
 
 def inside(states, rows, cols):
@@ -18,21 +22,20 @@
     return (at_row < rows) & (at_col < cols)
 
 
-def couple_kernel(
-    groups,
-    tile_left,
-    tile_right,
-    left_sizes,
-    right_sizes,
-    send_slot,
-    wave_hbm,
-    left_hbm,
-    right_hbm,
-    *rest,
-):
-    outs = rest[: len(groups)]
-    wave, left, right, masked, done, total, wave_sem, left_sem, right_sem = rest[len(groups) :]
+def couple_kernel(groups, share, *refs):
+    tables_hbm, (wave_hbm, left_hbm, right_hbm), rest = refs[:5], refs[5:8], refs[8:]
+    outs, live, rest = rest[: len(groups)], rest[len(groups)], rest[len(groups) + 1 :]
+    tables, rest = rest[:5], rest[5:]
+    wave, left, right, masked, done, total, table_sem, wave_sem, left_sem, right_sem = rest
+    tile_left, tile_right, left_sizes, right_sizes, send_slot = tables
     bonds, tiles, states = left.shape[0], wave.shape[0], wave.shape[1]
+    step = done.shape[0] // tiles
+    table_copies = [
+        pltpu.make_async_copy(src, dst, table_sem.at[i])
+        for i, (src, dst) in enumerate(zip(tables_hbm, tables))
+    ]
+    for copy in table_copies:
+        copy.start()
     wave_copy = pltpu.make_async_copy(wave_hbm, wave, wave_sem)
     wave_copy.start()
 
@@ -46,58 +49,73 @@
         for copy in copies(a):
             copy.start()
     total[...] = jnp.zeros_like(total)
+    for copy in table_copies:
+        copy.wait()
+    for j in range(live.shape[0]):
+        h = share() + j
+        keep = inside(states, left_sizes[tile_left[h]], right_sizes[tile_right[h]])
+        live[j] = jnp.where(keep, 1.0, 0.0).astype(jnp.bfloat16)
     wave_copy.wait()
     for g in range(tiles):
         keep = inside(states, left_sizes[tile_left[g]], right_sizes[tile_right[g]])
         tile = wave[g].astype(jnp.float32)
         masked[g] = jnp.where(keep, tile, 0.0).astype(jnp.bfloat16)
 
-    @pl.loop(0, bonds)
-    def _(a):
-        for copy in copies(a):
-            copy.wait()
+    @pl.loop(0, bonds // step)
+    def _(b):
+        for u in range(step):
+            for copy in copies(b * step + u):
+                copy.wait()
         for g in range(tiles):
-            done[g] = lax.dot_general(
+            blocks = jnp.concatenate([right[b * step + u, tile_right[g]] for u in range(step)], 0)
+            wide = lax.dot_general(
                 masked[g],
-                right[a, tile_right[g]],
+                blocks,
                 (((1,), (1,)), ((), ())),
                 preferred_element_type=jnp.float32,
             ).astype(jnp.bfloat16)
+            for u in range(step):
+                done[u * tiles + g] = wide[:, u * states : (u + 1) * states]
         for g in range(tiles):
-            q = send_slot[g, a]
-            total[q] += jnp.dot(
-                left[a, tile_left[g]], done[g], preferred_element_type=jnp.float32
-            )
+            for u in range(step):
+                total[send_slot[g, b * step + u]] += jnp.dot(
+                    left[b * step + u, tile_left[g]],
+                    done[u * tiles + g],
+                    preferred_element_type=jnp.float32,
+                )
 
     for out, order in zip(outs, groups):
         for j, q in enumerate(order()):
             out[j] = total[q].astype(jnp.bfloat16)
 
 
-def couple(groups, peers, tile_left, tile_right, left_sizes, right_sizes, send_slot, wave, left, right):
+def couple(groups, share, peers, tile_left, tile_right, left_sizes, right_sizes, send_slot, wave, left, right):
     tiles, states = wave.shape[0], wave.shape[1]
     bonds = left.shape[0]
+    step = max(d for d in range(1, 6) if bonds % d == 0)
+    counts = [count for _, count in groups] + [share[1]]
+    tables = (tile_left, tile_right, left_sizes, right_sizes, send_slot.T)
     return pl.pallas_call(
-        functools.partial(couple_kernel, [g for g, _ in groups]),
-        out_shape=[
-            jax.ShapeDtypeStruct((count, states, states), jnp.bfloat16) for _, count in groups
-        ],
-        in_specs=[SMEM] * 5 + [ANY] * 3,
-        out_specs=[VMEM] * len(groups),
-        scratch_shapes=[
+        functools.partial(couple_kernel, [g for g, _ in groups], share[0]),
+        out_shape=[jax.ShapeDtypeStruct((count, states, states), jnp.bfloat16) for count in counts],
+        in_specs=[HBM] * 8,
+        out_specs=[VMEM] * len(counts),
+        scratch_shapes=[pltpu.SMEM(table.shape, jnp.int32) for table in tables]
+        + [
             pltpu.VMEM(wave.shape, jnp.bfloat16),
             pltpu.VMEM(left.shape, jnp.bfloat16),
             pltpu.VMEM(right.shape, jnp.bfloat16),
             pltpu.VMEM(wave.shape, jnp.bfloat16),
-            pltpu.VMEM(wave.shape, jnp.bfloat16),
+            pltpu.VMEM((step * tiles, states, states), jnp.bfloat16),
             pltpu.VMEM((peers + 1, states, states), jnp.float32),
+            pltpu.SemaphoreType.DMA((len(tables),)),
             pltpu.SemaphoreType.DMA,
             pltpu.SemaphoreType.DMA((bonds,)),
             pltpu.SemaphoreType.DMA((bonds,)),
         ],
         compiler_params=pltpu.CompilerParams(vmem_limit_bytes=40 * 1024 * 1024),
         name="couple",
-    )(tile_left, tile_right, left_sizes, right_sizes, send_slot.T, wave, left, right)
+    )(*in_hbm(*tables, wave, left, right))
 
 
 def gather_kernel(n_left, own_table, other_table, *rest):
@@ -158,28 +176,6 @@
     )(received, kept)
 
 
-def finish_kernel(tile_left, tile_right, left_sizes, right_sizes, received, kept, out):
-    share, states = out.shape[0], out.shape[1]
-    m = lax.axis_index("mpo")
-    for j in range(share):
-        h = m * share + j
-        live = inside(states, left_sizes[tile_left[h]], right_sizes[tile_right[h]])
-        out[j] = jnp.where(live, kept[j] + received[j].astype(jnp.float32), 0.0).astype(
-            jnp.bfloat16
-        )
-
-
-def finish(tile_left, tile_right, left_sizes, right_sizes, received, kept):
-    return pl.pallas_call(
-        finish_kernel,
-        out_shape=jax.ShapeDtypeStruct(kept.shape, jnp.bfloat16),
-        in_specs=[SMEM] * 4 + [VMEM] * 2,
-        out_specs=VMEM,
-        compiler_params=pltpu.CompilerParams(vmem_limit_bytes=8 * 1024 * 1024),
-        name="finish",
-    )(tile_left, tile_right, left_sizes, right_sizes, received, kept)
-
-
 def by_permutes(sizes, wave, left, right, left_sizes, right_sizes, tile_left, tile_right, send_slot, recv_tile):
     n_left, n_right, n_mpo = sizes
     axes = ("lsec", "rsec", "mpo")
@@ -199,11 +195,14 @@
 
         return order
 
-    give, keep = couple(
+    share = wave.shape[0] // n_mpo
+    give, keep, live = couple(
         [(towards(1), n_left), (towards(0), n_left)],
+        (lambda: lax.axis_index("mpo") * share, share),
         n_left * n_right,
         tile_left, tile_right, left_sizes, right_sizes, send_slot, wave, left, right,
     )
+    give, other_table = lax.optimization_barrier((give, other_table))
     got = lax.ppermute(give, "mpo", swap_core)
     received = []
     for k in range(n_left):
@@ -212,16 +211,17 @@
         received.append(lax.ppermute(pair, axes, perm))
     give, keep = gather(recv_tile, other_table, received, wave.shape[0])
     give, keep = cross(lax.ppermute(give, "mpo", swap_core), keep)
-    return finish(
-        tile_left, tile_right, left_sizes, right_sizes, lax.ppermute(give, "mpo", swap_chip), keep
-    )
+    summed = keep + lax.ppermute(give, "mpo", swap_chip).astype(jnp.float32)
+    return jnp.where(live > 0, summed, 0.0).astype(jnp.bfloat16)
 
 
 def by_exchange(sizes, wave, left, right, left_sizes, right_sizes, tile_left, tile_right, send_slot, recv_tile):
     peers = sizes[0] * sizes[1]
     tiles, states = wave.shape[0], wave.shape[1]
-    (outgoing,) = couple(
+    share = tiles // sizes[2]
+    outgoing, live = couple(
         [(lambda: list(range(peers)), peers)],
+        (lambda: lax.axis_index("mpo") * share, share),
         peers,
         tile_left, tile_right, left_sizes, right_sizes, send_slot, wave, left, right,
     )
@@ -233,15 +233,8 @@
         chooser, received.reshape(peers, states * states), preferred_element_type=jnp.float32
     )
     partial = partial.reshape(tiles, states, states).astype(jnp.bfloat16)
-    share = lax.psum_scatter(partial, "mpo", scatter_dimension=0, tiled=True)
-    start = lax.axis_index("mpo") * share.shape[0]
-    at = lambda table, sizes_of: lax.dynamic_slice_in_dim(sizes_of[table], start, share.shape[0], 0)
-    rows, cols = at(tile_left, left_sizes), at(tile_right, right_sizes)
-    position = jnp.arange(states, dtype=jnp.int32)
-    live = (position[None, :, None] < rows[:, None, None]) & (
-        position[None, None, :] < cols[:, None, None]
-    )
-    return jnp.where(live, share, jnp.zeros_like(share))
+    mine = lax.psum_scatter(partial, "mpo", scatter_dimension=0, tiled=True)
+    return jnp.where(live > 0, mine, jnp.zeros_like(mine))
 
 
 def solution(mesh):

time: 40.8 us -> 28.2 us (0.69)
  local copies, waits for them, and re-layouts: 6.91 us -> 0.02 us
  Pallas kernels: 11.4 us -> 4.78 us
  waiting for transfers between devices: 7.92 us -> 11.2 us
  starting transfers between devices: 14.2 us -> 11.3 us
  other arithmetic: 0.03 us -> 0.69 us
    unnamed x18 -> x2, local copies, waits for them, and re-layouts: 6.89 us -> 0.01 us
    pallas_call x2 -> x1, Pallas kernels: 10.7 us -> 4.07 us  [couple(): pl.pallas_call(functools.partial(couple_kernel, [g for g, _ in groups], s...]
    ppermute x4, waiting for transfers between devices: 2.28 us -> 6.04 us  [by_permutes(): received.append(lax.ppermute(pair, axes, perm))]
    ppermute x1, starting transfers between devices: 3.03 us -> 0.45 us  [by_permutes(): other_table = lax.ppermute(recv_tile, 'mpo', swap_core)]
    ppermute x1, waiting for transfers between devices: 0.82 us -> 0.01 us  [by_permutes(): other_table = lax.ppermute(recv_tile, 'mpo', swap_core)]
    convert_element_type x0 -> x1, other arithmetic: none -> 0.66 us  [by_permutes(): return jnp.where(live > 0, summed, 0.0).astype(jnp.bfloat16)]
  transfers between devices with their start and end apart: 8 -> 8, of which waited for: 5 -> 5; matrix products, arithmetic and copies ran while one was open for 0% -> 0% of each run, Pallas kernels for 0% -> 15%
where the time goes in v2:
time: 28.2 us; the launch traced here: 28 us
  starting transfers between devices  11.3 us (40%)
  waiting for transfers between devices  11.2 us (40%)
  Pallas kernels  4.78 us (17%)
  other arithmetic  0.69 us (2%)
    ppermute x4, starting transfers between devices, by_permutes(): received.append(lax.ppermute(pair, axes, perm))  6.16 us
    ppermute x4, waiting for transfers between devices, by_permutes(): received.append(lax.ppermute(pair, axes, perm))  6.04 us
    pallas_call x1, Pallas kernels, couple(): pl.pallas_call(functools.partial(couple_kernel, [g for g, _ in groups], s...  4.07 us
    ppermute x1, starting transfers between devices, by_permutes(): give, keep = cross(lax.ppermute(give, 'mpo', swap_core), keep)  3 us
    ppermute x1, waiting for transfers between devices, by_permutes(): summed = keep + lax.ppermute(give, 'mpo', swap_chip).astype(jnp.float32)  2.85 us
    ppermute x1, starting transfers between devices, by_permutes(): summed = keep + lax.ppermute(give, 'mpo', swap_chip).astype(jnp.float32)  1.58 us
    ppermute x1, waiting for transfers between devices, by_permutes(): got = lax.ppermute(give, 'mpo', swap_core)  1.28 us
    ppermute x1, waiting for transfers between devices, by_permutes(): give, keep = cross(lax.ppermute(give, 'mpo', swap_core), keep)  0.99 us
  transfers between devices with their start and end apart: 8, of which 5 were waited for; matrix products, arithmetic and copies ran while one was open for 0% of the time, Pallas kernels for 15%

profile of v2, /device:TPU:0, one launch (start us, length us, event | category | flops | bytes accessed | tf_op | source)
XLA Modules:
  0.0 28.0 jit_solution(70744922000116682)
XLA Ops:
  0.0 0.5 %collective-permute-start = (s32[1,8]{1,0:T(1,128)}, s32[1,8]{1,0:T(1,128)S(1)}, u32[]{:S(2)}, u32[]{:S(2)}) collective-permute-start(s32[1,8]{1,0:T(1,128)} %own_table.1), channel_id=1, source_target_pairs={{0,1},{1,0},{2,3},{3,2},{4,5},{5,4},{6,7},{7,6},{8,9},{9,8},{10,11... | collective-permute-start | bytes 104 | tf_op jit(solution)/shard_map/ppermute | solution.py:186
  0.5 0.0 copy-start
  0.5 4.1 %couple.1 = (bf16[4,128,128]{2,1,0:T(8,128)(2,1)S(1)}, bf16[4,128,128]{2,1,0:T(8,128)(2,1)S(1)}, bf16[2,128,128]{2,1,0:T(8,128)(2,1)S(1)}) custom-call(s32[8]{0:T(128)} %refs_0_.1, s32[8]{0:T(128)} %refs_1_.1, s32[4]{0:T(128)} %refs_2_.1, s32[4]{0:T(128)} %refs_3_.1, s32[8,10]{1,0:T(8,128)} %bitcast.1, bf16[8,128,128]{2,1,0:T(8,128)(2,1)} %refs_5_.1, ...), custom_call_target="tpu_custom_call" | custom-call | tf_op jit(solution)/shard_map/couple/pallas_call | solution.py:98
  4.5 0.0 collective-permute-done.other_table
  4.5 0.1 collective-permute-start.1
  4.7 1.3 %collective-permute-done.1 = bf16[4,128,128]{2,1,0:T(8,128)(2,1)S(1)} collective-permute-done((bf16[4,128,128]{2,1,0:T(8,128)(2,1)S(1)}, bf16[4,128,128]{2,1,0:T(8,128)(2,1)S(1)}, u32[]{:S(2)}, u32[]{:S(2)}) %collective-permute-start.1) | collective-permute-done | bytes 131104 | tf_op jit(solution)/shard_map/ppermute | solution.py:206
  6.0 0.7 %collective-permute-start.2 = (bf16[2,128,128]{2,1,0:T(8,128)(2,1)S(1)}, bf16[2,128,128]{2,1,0:T(8,128)(2,1)S(1)}, u32[]{:S(2)}, u32[]{:S(2)}) collective-permute-start(bf16[2,128,128]{2,1,0:T(8,128)(2,1)S(1)} %pad_maximum_fusion), channel_id=1, source_target_pairs={{0,0},{1,5},{2,2},{3,7},{4,4},{5,1},{6,6},{7,3},{8,8},{9,13},{10,1... | collective-permute-start | bytes 196616 | tf_op jit(solution)/shard_map/ppermute | solution.py:211
  6.7 2.8 %collective-permute-start.3 = (bf16[2,128,128]{2,1,0:T(8,128)(2,1)S(1)}, bf16[2,128,128]{2,1,0:T(8,128)(2,1)S(1)}, u32[]{:S(2)}, u32[]{:S(2)}) collective-permute-start(bf16[2,128,128]{2,1,0:T(8,128)(2,1)S(1)} %pad_maximum_fusion.1), channel_id=1, source_target_pairs={{0,8},{1,13},{2,10},{3,15},{4,12},{5,9},{6,14},{7,11},{8,0},{9,5},... | collective-permute-start | bytes 196616 | tf_op jit(solution)/shard_map/ppermute | solution.py:211
  9.5 2.6 %collective-permute-start.4 = (bf16[2,128,128]{2,1,0:T(8,128)(2,1)S(1)}, bf16[2,128,128]{2,1,0:T(8,128)(2,1)S(1)}, u32[]{:S(2)}, u32[]{:S(2)}) collective-permute-start(bf16[2,128,128]{2,1,0:T(8,128)(2,1)S(1)} %pad_maximum_fusion.2), channel_id=1, source_target_pairs={{0,16},{1,21},{2,18},{3,23},{4,20},{5,17},{6,22},{7,19},{8,24},{9,... | collective-permute-start | bytes 196616 | tf_op jit(solution)/shard_map/ppermute | solution.py:211
  12.1 0.1 collective-permute-start.5
  12.2 0.0 collective-permute-done.2.rest_0_
  12.2 0.0 collective-permute-done.3.rest_1_
  12.2 3.2 %collective-permute-done.4.rest_2_ = bf16[2,128,128]{2,1,0:T(8,128)(2,1)S(1)} collective-permute-done((bf16[2,128,128]{2,1,0:T(8,128)(2,1)S(1)}, bf16[2,128,128]{2,1,0:T(8,128)(2,1)S(1)}, u32[]{:S(2)}, u32[]{:S(2)}) %collective-permute-start.4) | collective-permute-done | bytes 65568 | tf_op jit(solution)/shard_map/ppermute | solution.py:211
  15.4 2.9 %collective-permute-done.5.rest_3_ = bf16[2,128,128]{2,1,0:T(8,128)(2,1)S(1)} collective-permute-done((bf16[2,128,128]{2,1,0:T(8,128)(2,1)S(1)}, bf16[2,128,128]{2,1,0:T(8,128)(2,1)S(1)}, u32[]{:S(2)}, u32[]{:S(2)}) %collective-permute-start.5) | collective-permute-done | bytes 65568 | tf_op jit(solution)/shard_map/ppermute | solution.py:211
  18.3 0.0 copy-done
  18.3 0.7 %gather.1 = (bf16[4,128,128]{2,1,0:T(8,128)(2,1)S(1)}, f32[4,128,128]{2,1,0:T(8,128)S(1)}) custom-call(s32[1,8]{1,0:T(1,128)S(1)} %copy-done, s32[1,8]{1,0:T(1,128)S(1)} %collective-permute-done.other_table, bf16[2,128,128]{2,1,0:T(8,128)(2,1)S(1)} %collective-permute-done.2.rest_0_, bf16[2,128,128]{2,1,0:T(8,128)(2,1)S(1)} %collective-permute-done.3.rest_1_, ...), custom_call_target="tpu_custom_call" | custom-call | tf_op jit(solution)/shard_map/gather/pallas_call | solution.py:141
  18.9 3.0 %collective-permute-start.6 = (bf16[4,128,128]{2,1,0:T(8,128)(2,1)S(1)}, bf16[4,128,128]{2,1,0:T(8,128)(2,1)S(1)}, u32[]{:S(2)}, u32[]{:S(2)}) collective-permute-start(bf16[4,128,128]{2,1,0:T(8,128)(2,1)S(1)} %get-tuple-element.19), channel_id=1, source_target_pairs={{0,1},{1,0},{2,3},{3,2},{4,5},{5,4},{6,7},{7,6},{8,9},{9,8},{10,11... | collective-permute-start | bytes 393224 | tf_op jit(solution)/shard_map/ppermute | solution.py:213
  21.9 1.0 %collective-permute-done.6.received = bf16[4,128,128]{2,1,0:T(8,128)(2,1)S(1)} collective-permute-done((bf16[4,128,128]{2,1,0:T(8,128)(2,1)S(1)}, bf16[4,128,128]{2,1,0:T(8,128)(2,1)S(1)}, u32[]{:S(2)}, u32[]{:S(2)}) %collective-permute-start.6) | collective-permute-done | bytes 131104 | tf_op jit(solution)/shard_map/ppermute | solution.py:213
  23.0 1.6 %collective-permute-start.7 = (bf16[2,128,128]{2,1,0:T(8,128)(2,1)S(1)}, bf16[2,128,128]{2,1,0:T(8,128)(2,1)S(1)}, u32[]{:S(2)}, u32[]{:S(2)}) collective-permute-start(bf16[2,128,128]{2,1,0:T(8,128)(2,1)S(1)} %get-tuple-element.22), channel_id=1, source_target_pairs={{0,2},{1,3},{2,0},{3,1},{4,6},{5,7},{6,4},{7,5},{8,10},{9,11},{10,... | collective-permute-start | bytes 196616 | tf_op jit(solution)/shard_map/ppermute | solution.py:214
  24.5 2.8 %collective-permute-done.7 = bf16[2,128,128]{2,1,0:T(8,128)(2,1)S(1)} collective-permute-done((bf16[2,128,128]{2,1,0:T(8,128)(2,1)S(1)}, bf16[2,128,128]{2,1,0:T(8,128)(2,1)S(1)}, u32[]{:S(2)}, u32[]{:S(2)}) %collective-permute-start.7) | collective-permute-done | bytes 65568 | tf_op jit(solution)/shard_map/ppermute | solution.py:214
  27.4 0.7 %select_convert_fusion = bf16[2,128,128]{2,1,0:T(8,128)(2,1)} fusion(f32[2,128,128]{2,1,0:T(8,128)S(1)} %get-tuple-element.21, bf16[2,128,128]{2,1,0:T(8,128)(2,1)S(1)} %collective-permute-done.7, bf16[2,128,128]{2,1,0:T(8,128)(2,1)S(1)} %get-tuple-element.14), kind=kLoop, calls=%fused_computation | loop fusion | flops 163840 | bytes 327680 | tf_op jit(solution)/shard_map/convert_element_type | solution.py:215
  (7 shorter events, 0.1 us)
Async XLA Ops:
  0.0 4.5 %collective-permute-start = (s32[1,8]{1,0:T(1,128)}, s32[1,8]{1,0:T(1,128)S(1)}, u32[]{:S(2)}, u32[]{:S(2)}) collective-permute-start(s32[1,8]{1,0:T(1,128)} %own_table.1), channel_id=1, source_target_pairs={{0,1},{1,0},{2,3},{3,2},{4,5},{5,4},{6,7},{7,6},{8,9},{9,8},{10,11... | collective-permute-start | bytes 104 | tf_op jit(solution)/shard_map/ppermute | solution.py:186
  0.5 17.8 %copy-start = (s32[1,8]{1,0:T(1,128)S(1)}, s32[1,8]{1,0:T(1,128)}, u32[]{:S(2)}) copy-start(s32[1,8]{1,0:T(1,128)} %own_table.1) | copy-start | bytes 100
  4.5 1.4 %collective-permute-start.1 = (bf16[4,128,128]{2,1,0:T(8,128)(2,1)S(1)}, bf16[4,128,128]{2,1,0:T(8,128)(2,1)S(1)}, u32[]{:S(2)}, u32[]{:S(2)}) collective-permute-start(bf16[4,128,128]{2,1,0:T(8,128)(2,1)S(1)} %get-tuple-element.18), channel_id=1, source_target_pairs={{0,1},{1,0},{2,3},{3,2},{4,5},{5,4},{6,7},{7,6},{8,9},{9,8},{10,11... | collective-permute-start | bytes 393224 | tf_op jit(solution)/shard_map/ppermute | solution.py:206
  6.0 6.2 %collective-permute-start.2 = (bf16[2,128,128]{2,1,0:T(8,128)(2,1)S(1)}, bf16[2,128,128]{2,1,0:T(8,128)(2,1)S(1)}, u32[]{:S(2)}, u32[]{:S(2)}) collective-permute-start(bf16[2,128,128]{2,1,0:T(8,128)(2,1)S(1)} %pad_maximum_fusion), channel_id=1, source_target_pairs={{0,0},{1,5},{2,2},{3,7},{4,4},{5,1},{6,6},{7,3},{8,8},{9,13},{10,1... | collective-permute-start | bytes 196616 | tf_op jit(solution)/shard_map/ppermute | solution.py:211
  6.7 5.5 %collective-permute-start.3 = (bf16[2,128,128]{2,1,0:T(8,128)(2,1)S(1)}, bf16[2,128,128]{2,1,0:T(8,128)(2,1)S(1)}, u32[]{:S(2)}, u32[]{:S(2)}) collective-permute-start(bf16[2,128,128]{2,1,0:T(8,128)(2,1)S(1)} %pad_maximum_fusion.1), channel_id=1, source_target_pairs={{0,8},{1,13},{2,10},{3,15},{4,12},{5,9},{6,14},{7,11},{8,0},{9,5},... | collective-permute-start | bytes 196616 | tf_op jit(solution)/shard_map/ppermute | solution.py:211
  9.5 5.9 %collective-permute-start.4 = (bf16[2,128,128]{2,1,0:T(8,128)(2,1)S(1)}, bf16[2,128,128]{2,1,0:T(8,128)(2,1)S(1)}, u32[]{:S(2)}, u32[]{:S(2)}) collective-permute-start(bf16[2,128,128]{2,1,0:T(8,128)(2,1)S(1)} %pad_maximum_fusion.2), channel_id=1, source_target_pairs={{0,16},{1,21},{2,18},{3,23},{4,20},{5,17},{6,22},{7,19},{8,24},{9,... | collective-permute-start | bytes 196616 | tf_op jit(solution)/shard_map/ppermute | solution.py:211
  12.1 6.1 %collective-permute-start.5 = (bf16[2,128,128]{2,1,0:T(8,128)(2,1)S(1)}, bf16[2,128,128]{2,1,0:T(8,128)(2,1)S(1)}, u32[]{:S(2)}, u32[]{:S(2)}) collective-permute-start(bf16[2,128,128]{2,1,0:T(8,128)(2,1)S(1)} %pad_maximum_fusion.3), channel_id=1, source_target_pairs={{0,24},{1,29},{2,26},{3,31},{4,28},{5,25},{6,30},{7,27},{8,16},{9,... | collective-permute-start | bytes 196616 | tf_op jit(solution)/shard_map/ppermute | solution.py:211
  18.9 4.0 %collective-permute-start.6 = (bf16[4,128,128]{2,1,0:T(8,128)(2,1)S(1)}, bf16[4,128,128]{2,1,0:T(8,128)(2,1)S(1)}, u32[]{:S(2)}, u32[]{:S(2)}) collective-permute-start(bf16[4,128,128]{2,1,0:T(8,128)(2,1)S(1)} %get-tuple-element.19), channel_id=1, source_target_pairs={{0,1},{1,0},{2,3},{3,2},{4,5},{5,4},{6,7},{7,6},{8,9},{9,8},{10,11... | collective-permute-start | bytes 393224 | tf_op jit(solution)/shard_map/ppermute | solution.py:213
  23.0 4.4 %collective-permute-start.7 = (bf16[2,128,128]{2,1,0:T(8,128)(2,1)S(1)}, bf16[2,128,128]{2,1,0:T(8,128)(2,1)S(1)}, u32[]{:S(2)}, u32[]{:S(2)}) collective-permute-start(bf16[2,128,128]{2,1,0:T(8,128)(2,1)S(1)} %get-tuple-element.22), channel_id=1, source_target_pairs={{0,2},{1,3},{2,0},{3,1},{4,6},{5,7},{6,4},{7,5},{8,10},{9,11},{10,... | collective-permute-start | bytes 196616 | tf_op jit(solution)/shard_map/ppermute | solution.py:214

commit v3 on v2

--- a/solution.py
+++ b/solution.py
@@ -29,7 +29,6 @@
     wave, left, right, masked, done, total, table_sem, wave_sem, left_sem, right_sem = rest
     tile_left, tile_right, left_sizes, right_sizes, send_slot = tables
     bonds, tiles, states = left.shape[0], wave.shape[0], wave.shape[1]
-    step = done.shape[0] // tiles
     table_copies = [
         pltpu.make_async_copy(src, dst, table_sem.at[i])
         for i, (src, dst) in enumerate(zip(tables_hbm, tables))
@@ -38,19 +37,13 @@
         copy.start()
     wave_copy = pltpu.make_async_copy(wave_hbm, wave, wave_sem)
     wave_copy.start()
-
-    def copies(a):
-        return (
-            pltpu.make_async_copy(right_hbm.at[a], right.at[a], right_sem.at[a]),
-            pltpu.make_async_copy(left_hbm.at[a], left.at[a], left_sem.at[a]),
-        )
-
-    for a in range(bonds):
-        for copy in copies(a):
-            copy.start()
+    right_copy = pltpu.make_async_copy(right_hbm, right, right_sem)
+    right_copy.start()
     total[...] = jnp.zeros_like(total)
     for copy in table_copies:
         copy.wait()
+    left_copy = pltpu.make_async_copy(left_hbm, left, left_sem)
+    left_copy.start()
     for j in range(live.shape[0]):
         h = share() + j
         keep = inside(states, left_sizes[tile_left[h]], right_sizes[tile_right[h]])
@@ -60,29 +53,20 @@
         keep = inside(states, left_sizes[tile_left[g]], right_sizes[tile_right[g]])
         tile = wave[g].astype(jnp.float32)
         masked[g] = jnp.where(keep, tile, 0.0).astype(jnp.bfloat16)
-
-    @pl.loop(0, bonds // step)
-    def _(b):
-        for u in range(step):
-            for copy in copies(b * step + u):
-                copy.wait()
-        for g in range(tiles):
-            blocks = jnp.concatenate([right[b * step + u, tile_right[g]] for u in range(step)], 0)
-            wide = lax.dot_general(
-                masked[g],
-                blocks,
-                (((1,), (1,)), ((), ())),
-                preferred_element_type=jnp.float32,
-            ).astype(jnp.bfloat16)
-            for u in range(step):
-                done[u * tiles + g] = wide[:, u * states : (u + 1) * states]
-        for g in range(tiles):
-            for u in range(step):
-                total[send_slot[g, b * step + u]] += jnp.dot(
-                    left[b * step + u, tile_left[g]],
-                    done[u * tiles + g],
-                    preferred_element_type=jnp.float32,
-                )
+    right_copy.wait()
+    for g in range(tiles):
+        blocks = jnp.concatenate([right[a, tile_right[g]] for a in range(bonds)], 0)
+        wide = lax.dot_general(
+            masked[g], blocks, (((1,), (1,)), ((), ())), preferred_element_type=jnp.float32
+        ).astype(jnp.bfloat16)
+        for a in range(bonds):
+            done[a * tiles + g] = wide[:, a * states : (a + 1) * states]
+    left_copy.wait()
+    for g in range(tiles):
+        for a in range(bonds):
+            total[send_slot[g, a]] += jnp.dot(
+                left[a, tile_left[g]], done[a * tiles + g], preferred_element_type=jnp.float32
+            )
 
     for out, order in zip(outs, groups):
         for j, q in enumerate(order()):
@@ -92,7 +76,6 @@
 def couple(groups, share, peers, tile_left, tile_right, left_sizes, right_sizes, send_slot, wave, left, right):
     tiles, states = wave.shape[0], wave.shape[1]
     bonds = left.shape[0]
-    step = max(d for d in range(1, 6) if bonds % d == 0)
     counts = [count for _, count in groups] + [share[1]]
     tables = (tile_left, tile_right, left_sizes, right_sizes, send_slot.T)
     return pl.pallas_call(
@@ -106,50 +89,95 @@
             pltpu.VMEM(left.shape, jnp.bfloat16),
             pltpu.VMEM(right.shape, jnp.bfloat16),
             pltpu.VMEM(wave.shape, jnp.bfloat16),
-            pltpu.VMEM((step * tiles, states, states), jnp.bfloat16),
+            pltpu.VMEM((bonds * tiles, states, states), jnp.bfloat16),
             pltpu.VMEM((peers + 1, states, states), jnp.float32),
             pltpu.SemaphoreType.DMA((len(tables),)),
             pltpu.SemaphoreType.DMA,
-            pltpu.SemaphoreType.DMA((bonds,)),
-            pltpu.SemaphoreType.DMA((bonds,)),
+            pltpu.SemaphoreType.DMA,
+            pltpu.SemaphoreType.DMA,
         ],
         compiler_params=pltpu.CompilerParams(vmem_limit_bytes=40 * 1024 * 1024),
         name="couple",
     )(*in_hbm(*tables, wave, left, right))
 
 
-def gather_kernel(n_left, own_table, other_table, *rest):
-    received = rest[:n_left]
-    give, keep, total = rest[n_left:]
+SETS = (((3, 0), (2, 0), (1, 0)), ((2, 1), (1, 1), (0, 1)))
+FAR = (3, 1)
+
+
+def flipped(core, i):
     z, y = lax.axis_index("lsec"), lax.axis_index("rsec")
-    c = lax.rem(lax.axis_index("mpo"), 2)
+    dz, dy = (jnp.where(core == 0, SETS[0][i][d], SETS[1][i][d]) for d in range(2))
+    return jnp.bitwise_xor(z, dz) * 2 + jnp.bitwise_xor(y, dy)
+
+
+def fixed(dz, dy):
+    z, y = lax.axis_index("lsec"), lax.axis_index("rsec")
+    return jnp.bitwise_xor(z, dz) * 2 + jnp.bitwise_xor(y, dy)
+
+
+def first_kernel(own_table, other_table, received, held, part, chosen, total):
+    core = lax.rem(lax.axis_index("mpo"), 2)
+    quarter = (total.shape[0] - 1) // 4
     total[...] = jnp.zeros_like(total)
-    for k in range(n_left):
-        source = 2 * jnp.bitwise_xor(z, k) + jnp.bitwise_xor(y, c)
-        for j, table in enumerate((own_table, other_table)):
-            t = table[0, source]
-            total[t] += received[k][j].astype(jnp.float32)
-    quarter = (total.shape[0] - 1) // 4
-    for x in range(2):
-        for j in range(quarter):
-            give[x * quarter + j] = total[(2 * x + 1 - c) * quarter + j].astype(jnp.bfloat16)
-            keep[x * quarter + j] = total[(2 * x + c) * quarter + j]
-
-
-def gather(own_table, other_table, received, tiles):
-    states = received[0].shape[1]
+    total[own_table[0, fixed(0, 0)]] = held[0].astype(jnp.float32)
+    source = flipped(core, 0)
+    total[own_table[0, source]] += received[0].astype(jnp.float32)
+    total[other_table[0, source]] += received[1].astype(jnp.float32)
+    targets = [table[0, flipped(core, i)] for i in (1, 2) for table in (own_table, other_table)]
+    targets.append(own_table[0, fixed(*FAR)])
+    for side, half in enumerate((1 - core, core)):
+        for x in range(2):
+            for j in range(quarter):
+                at = (side * 2 + x) * quarter + j
+                tile = (2 * x + half) * quarter + j
+                part[at] = total[tile]
+                for s, target in enumerate(targets):
+                    one = jnp.where(target == tile, 1.0, 0.0)
+                    chosen[s, at] = jnp.full(chosen.shape[2:], one, jnp.float32)
+
+
+def second_kernel(part, chosen, near, nearest, far, give, keep):
+    slots = [near[0], near[1], nearest[0], nearest[1], far[0]]
+    half, states = give.shape[0], give.shape[1]
+    for at in range(2 * half):
+        tile = part[at].reshape(states // 8, 8, states)
+        for s, slot in enumerate(slots):
+            rows = slot.astype(jnp.float32).reshape(states // 8, 8, states)
+            tile += rows * chosen[s, at][None]
+        tile = tile.reshape(states, states)
+        if at < half:
+            give[at] = tile.astype(jnp.bfloat16)
+        else:
+            keep[at - half] = tile
+
+
+def gather(own_table, other_table, held, longest, near, nearest, far, tiles):
+    states = held.shape[1]
+    whole = (tiles, states, states)
+    part, chosen = pl.pallas_call(
+        first_kernel,
+        out_shape=[
+            jax.ShapeDtypeStruct(whole, jnp.float32),
+            jax.ShapeDtypeStruct((5, tiles, 8, states), jnp.float32),
+        ],
+        in_specs=[SMEM] * 2 + [VMEM] * 2,
+        out_specs=[VMEM] * 2,
+        scratch_shapes=[pltpu.VMEM((tiles + 1, states, states), jnp.float32)],
+        compiler_params=pltpu.CompilerParams(vmem_limit_bytes=16 * 1024 * 1024),
+        name="first_sums",
+    )(own_table, other_table, longest, held)
     return pl.pallas_call(
-        functools.partial(gather_kernel, len(received)),
+        second_kernel,
         out_shape=[
             jax.ShapeDtypeStruct((tiles // 2, states, states), jnp.bfloat16),
             jax.ShapeDtypeStruct((tiles // 2, states, states), jnp.float32),
         ],
-        in_specs=[SMEM] * 2 + [VMEM] * len(received),
+        in_specs=[VMEM] * 5,
         out_specs=[VMEM] * 2,
-        scratch_shapes=[pltpu.VMEM((tiles + 1, states, states), jnp.float32)],
         compiler_params=pltpu.CompilerParams(vmem_limit_bytes=16 * 1024 * 1024),
-        name="gather",
-    )(own_table, other_table, *received)
+        name="second_sums",
+    )(part, chosen, near, nearest, far)
 
 
 def cross_kernel(received, kept, give, keep):
@@ -185,31 +213,34 @@
     swap_chip = [(m, m ^ 2) for m in range(n_mpo)]
     other_table = lax.ppermute(recv_tile, "mpo", swap_core)
 
-    def towards(flip):
-        def order():
-            z, y = lax.axis_index("lsec"), lax.axis_index("rsec")
-            c = jnp.bitwise_xor(lax.rem(lax.axis_index("mpo"), 2), flip)
-            return [
-                jnp.bitwise_xor(z, k) * n_right + jnp.bitwise_xor(y, c) for k in range(n_left)
-            ]
-
-        return order
-
     share = wave.shape[0] // n_mpo
-    give, keep, live = couple(
-        [(towards(1), n_left), (towards(0), n_left)],
+    core = lambda flip: jnp.bitwise_xor(lax.rem(lax.axis_index("mpo"), 2), flip)
+    give, keep, far, held, live = couple(
+        [
+            (lambda: [flipped(core(1), i) for i in range(3)], 3),
+            (lambda: [flipped(core(0), i) for i in range(3)], 3),
+            (lambda: [fixed(*FAR)], 1),
+            (lambda: [fixed(0, 0)], 1),
+        ],
         (lambda: lax.axis_index("mpo") * share, share),
         n_left * n_right,
         tile_left, tile_right, left_sizes, right_sizes, send_slot, wave, left, right,
     )
+
+    def move(x, flips):
+        perm = [
+            (place(z, y, m), place(z ^ flips[m % 2][0], y ^ flips[m % 2][1], m))
+            for z, y, m in every
+        ]
+        return lax.ppermute(x, axes, perm)
+
     give, other_table = lax.optimization_barrier((give, other_table))
     got = lax.ppermute(give, "mpo", swap_core)
-    received = []
-    for k in range(n_left):
-        pair = jnp.stack([keep[k], got[k]])
-        perm = [(place(z, y, m), place(z ^ k, y ^ (m % 2), m)) for z, y, m in every]
-        received.append(lax.ppermute(pair, axes, perm))
-    give, keep = gather(recv_tile, other_table, received, wave.shape[0])
+    far = move(far, (FAR, FAR))
+    received = [
+        move(jnp.stack([keep[i], got[i]]), (SETS[0][i], SETS[1][i])) for i in range(3)
+    ]
+    give, keep = gather(recv_tile, other_table, held, *received, far, wave.shape[0])
     give, keep = cross(lax.ppermute(give, "mpo", swap_core), keep)
     summed = keep + lax.ppermute(give, "mpo", swap_chip).astype(jnp.float32)
     return jnp.where(live > 0, summed, 0.0).astype(jnp.bfloat16)
@@ -239,7 +270,7 @@
 
 def solution(mesh):
     sizes = tuple(mesh.shape[axis] for axis in ("lsec", "rsec", "mpo"))
-    few = sizes[1] == 2 and sizes[2] == 4 and sizes[0] in (2, 4)
+    few = sizes == (4, 2, 4)
     placed = (
         P(("lsec", "rsec"), None, None),
         P("mpo", "lsec", None, None),

time: 28.2 us -> 25.1 us (0.89)
  waiting for transfers between devices: 11.2 us -> 7.33 us
  starting transfers between devices: 11.3 us -> 12.6 us
  Pallas kernels: 4.78 us -> 4.28 us
    ppermute x4, starting transfers between devices: 6.16 us -> 10.3 us  [move(): return lax.ppermute(x, axes, perm)]
    ppermute x4, waiting for transfers between devices: 6.04 us -> 2.08 us  [move(): return lax.ppermute(x, axes, perm)]
    ppermute x1, starting transfers between devices: 3 us -> 0.18 us  [by_permutes(): give, keep = cross(lax.ppermute(give, 'mpo', swap_core), keep)]
    pallas_call x1, Pallas kernels: 4.07 us -> 3.41 us  [couple(): pl.pallas_call(functools.partial(couple_kernel, [g for g, _ in groups], s...]
    pallas_call x1 -> x2, Pallas kernels: 0.67 us -> 0.84 us  [the longest x1 0.65 us: gather(): pl.pallas_call(first_kernel, out_shape=[jax.ShapeDtypeStruct(whole, jnp.f...]
  transfers between devices with their start and end apart: 8 -> 8, of which waited for: 5 -> 4; matrix products, arithmetic and copies ran while one was open for 0% -> 0% of each run, Pallas kernels for 15% -> 16%
where the time goes in v3:
time: 25.1 us; the launch traced here: 24.9 us
  starting transfers between devices  12.6 us (50%)
  waiting for transfers between devices  7.33 us (29%)
  Pallas kernels  4.28 us (17%)
  other arithmetic  0.69 us (3%)
    ppermute x4, starting transfers between devices, move(): return lax.ppermute(x, axes, perm)  10.3 us
    pallas_call x1, Pallas kernels, couple(): pl.pallas_call(functools.partial(couple_kernel, [g for g, _ in groups], s...  3.41 us
    ppermute x1, waiting for transfers between devices, by_permutes(): summed = keep + lax.ppermute(give, 'mpo', swap_chip).astype(jnp.float32)  2.78 us
    ppermute x4, waiting for transfers between devices, move(): return lax.ppermute(x, axes, perm)  2.08 us
    ppermute x1, starting transfers between devices, by_permutes(): summed = keep + lax.ppermute(give, 'mpo', swap_chip).astype(jnp.float32)  1.55 us
    ppermute x1, waiting for transfers between devices, by_permutes(): got = lax.ppermute(give, 'mpo', swap_core)  1.24 us
    ppermute x1, waiting for transfers between devices, by_permutes(): give, keep = cross(lax.ppermute(give, 'mpo', swap_core), keep)  1.23 us
    convert_element_type x1, other arithmetic, by_permutes(): return jnp.where(live > 0, summed, 0.0).astype(jnp.bfloat16)  0.66 us
  transfers between devices with their start and end apart: 8, of which 4 were waited for; matrix products, arithmetic and copies ran while one was open for 0% of the time, Pallas kernels for 16%

profile of v3, /device:TPU:0, one launch (start us, length us, event | category | flops | bytes accessed | tf_op | source)
XLA Modules:
  0.0 24.9 jit_solution(16111106251260562576)
XLA Ops:
  0.0 0.5 %collective-permute-start = (s32[1,8]{1,0:T(1,128)}, s32[1,8]{1,0:T(1,128)S(1)}, u32[]{:S(2)}, u32[]{:S(2)}) collective-permute-start(s32[1,8]{1,0:T(1,128)} %own_table.1), channel_id=1, source_target_pairs={{0,1},{1,0},{2,3},{3,2},{4,5},{5,4},{6,7},{7,6},{8,9},{9,8},{10,11... | collective-permute-start | bytes 104 | tf_op jit(solution)/shard_map/ppermute | solution.py:214
  0.5 0.0 copy-start
  0.5 3.4 %couple.1 = (bf16[3,128,128]{2,1,0:T(8,128)(2,1)S(1)}, bf16[3,128,128]{2,1,0:T(8,128)(2,1)S(1)}, bf16[1,128,128]{2,1,0:T(8,128)(2,1)S(1)}, bf16[1,128,128]{2,1,0:T(8,128)(2,1)S(1)}, bf16[2,128,128]{2,1,0:T(8,128)(2,1)S(1)}) custom-call(s32[8]{0:T(128)} %refs_0_.1, s32[8]{0:T(128)} %refs_1_.1, s32[4]{0:T(128)} %refs_2_.1, s32[4]{0:T(128)} %refs_3_.1, ...), custom_call_target="tpu_custom_call" | custom-call | tf_op jit(solution)/shard_map/couple/pallas_call | solution.py:81
  3.9 0.0 collective-permute-done.other_table
  3.9 0.1 collective-permute-start.1
  4.0 1.2 %collective-permute-done.1 = bf16[3,128,128]{2,1,0:T(8,128)(2,1)S(1)} collective-permute-done((bf16[3,128,128]{2,1,0:T(8,128)(2,1)S(1)}, bf16[3,128,128]{2,1,0:T(8,128)(2,1)S(1)}, u32[]{:S(2)}, u32[]{:S(2)}) %collective-permute-start.1) | collective-permute-done | bytes 98336 | tf_op jit(solution)/shard_map/ppermute | solution.py:238
  5.3 4.8 %collective-permute-start.2 = (bf16[2,128,128]{2,1,0:T(8,128)(2,1)S(1)}, bf16[2,128,128]{2,1,0:T(8,128)(2,1)S(1)}, u32[]{:S(2)}, u32[]{:S(2)}) collective-permute-start(bf16[2,128,128]{2,1,0:T(8,128)(2,1)S(1)} %pad_maximum_fusion), channel_id=1, source_target_pairs={{0,24},{1,21},{2,26},{3,23},{4,28},{5,17},{6,30},{7,19},{8,16},{9,... | collective-permute-start | bytes 196616 | tf_op jit(solution)/shard_map/ppermute | solution.py:235
  10.1 0.1 collective-permute-start.3
  10.2 0.6 %collective-permute-start.4 = (bf16[2,128,128]{2,1,0:T(8,128)(2,1)S(1)}, bf16[2,128,128]{2,1,0:T(8,128)(2,1)S(1)}, u32[]{:S(2)}, u32[]{:S(2)}) collective-permute-start(bf16[2,128,128]{2,1,0:T(8,128)(2,1)S(1)} %pad_maximum_fusion.2), channel_id=1, source_target_pairs={{0,8},{1,5},{2,10},{3,7},{4,12},{5,1},{6,14},{7,3},{8,0},{9,13},{1... | collective-permute-start | bytes 196616 | tf_op jit(solution)/shard_map/ppermute | solution.py:235
  10.8 4.8 %collective-permute-start.5 = (bf16[1,128,128]{2,1,0:T(8,128)(2,1)S(1)}, bf16[1,128,128]{2,1,0:T(8,128)(2,1)S(1)}, u32[]{:S(2)}, u32[]{:S(2)}) collective-permute-start(bf16[1,128,128]{2,1,0:T(8,128)(2,1)S(1)} %get-tuple-element.26), channel_id=1, source_target_pairs={{0,28},{1,29},{2,30},{3,31},{4,24},{5,25},{6,26},{7,27},{8,20},{9,... | collective-permute-start | bytes 98312 | tf_op jit(solution)/shard_map/ppermute | solution.py:235
  15.6 0.0 collective-permute-done.2.received
  15.6 0.0 copy-done
  15.6 0.6 %first_sums.1 = (f32[8,128,128]{2,1,0:T(8,128)S(1)}, f32[5,8,8,128]{3,2,1,0:T(8,128)S(1)}) custom-call(s32[1,8]{1,0:T(1,128)S(1)} %copy-done, s32[1,8]{1,0:T(1,128)S(1)} %collective-permute-done.other_table, bf16[2,128,128]{2,1,0:T(8,128)(2,1)S(1)} %collective-permute-done.2.received, bf16[1,128,128]{2,1,0:T(8,128)(2,1)S(1)} %get-tuple-element.23.held), custom_call_target="tpu_custom_call" | custom-call | tf_op jit(solution)/shard_map/first_sums/pallas_call | solution.py:158
  16.2 2.1 %collective-permute-done.5.far = bf16[1,128,128]{2,1,0:T(8,128)(2,1)S(1)} collective-permute-done((bf16[1,128,128]{2,1,0:T(8,128)(2,1)S(1)}, bf16[1,128,128]{2,1,0:T(8,128)(2,1)S(1)}, u32[]{:S(2)}, u32[]{:S(2)}) %collective-permute-start.5) | collective-permute-done | bytes 32800 | tf_op jit(solution)/shard_map/ppermute | solution.py:235
  18.3 0.0 collective-permute-done.3.near
  18.3 0.0 collective-permute-done.4.nearest
  18.3 0.2 second_sums.1
  18.5 0.2 collective-permute-start.6
  18.7 1.2 %collective-permute-done.6.received = bf16[4,128,128]{2,1,0:T(8,128)(2,1)S(1)} collective-permute-done((bf16[4,128,128]{2,1,0:T(8,128)(2,1)S(1)}, bf16[4,128,128]{2,1,0:T(8,128)(2,1)S(1)}, u32[]{:S(2)}, u32[]{:S(2)}) %collective-permute-start.6) | collective-permute-done | bytes 131104 | tf_op jit(solution)/shard_map/ppermute | solution.py:244
  20.0 1.6 %collective-permute-start.7 = (bf16[2,128,128]{2,1,0:T(8,128)(2,1)S(1)}, bf16[2,128,128]{2,1,0:T(8,128)(2,1)S(1)}, u32[]{:S(2)}, u32[]{:S(2)}) collective-permute-start(bf16[2,128,128]{2,1,0:T(8,128)(2,1)S(1)} %get-tuple-element.30), channel_id=1, source_target_pairs={{0,2},{1,3},{2,0},{3,1},{4,6},{5,7},{6,4},{7,5},{8,10},{9,11},{10,... | collective-permute-start | bytes 196616 | tf_op jit(solution)/shard_map/ppermute | solution.py:245
  21.5 2.8 %collective-permute-done.7 = bf16[2,128,128]{2,1,0:T(8,128)(2,1)S(1)} collective-permute-done((bf16[2,128,128]{2,1,0:T(8,128)(2,1)S(1)}, bf16[2,128,128]{2,1,0:T(8,128)(2,1)S(1)}, u32[]{:S(2)}, u32[]{:S(2)}) %collective-permute-start.7) | collective-permute-done | bytes 65568 | tf_op jit(solution)/shard_map/ppermute | solution.py:245
  24.3 0.7 %select_convert_fusion = bf16[2,128,128]{2,1,0:T(8,128)(2,1)} fusion(f32[2,128,128]{2,1,0:T(8,128)S(1)} %get-tuple-element.29, bf16[2,128,128]{2,1,0:T(8,128)(2,1)S(1)} %collective-permute-done.7, bf16[2,128,128]{2,1,0:T(8,128)(2,1)S(1)} %get-tuple-element.18), kind=kLoop, calls=%fused_computation | loop fusion | flops 163840 | bytes 327680 | tf_op jit(solution)/shard_map/convert_element_type | solution.py:246
  (6 shorter events, 0.1 us)
Async XLA Ops:
  0.0 3.9 %collective-permute-start = (s32[1,8]{1,0:T(1,128)}, s32[1,8]{1,0:T(1,128)S(1)}, u32[]{:S(2)}, u32[]{:S(2)}) collective-permute-start(s32[1,8]{1,0:T(1,128)} %own_table.1), channel_id=1, source_target_pairs={{0,1},{1,0},{2,3},{3,2},{4,5},{5,4},{6,7},{7,6},{8,9},{9,8},{10,11... | collective-permute-start | bytes 104 | tf_op jit(solution)/shard_map/ppermute | solution.py:214
  0.5 15.1 %copy-start = (s32[1,8]{1,0:T(1,128)S(1)}, s32[1,8]{1,0:T(1,128)}, u32[]{:S(2)}) copy-start(s32[1,8]{1,0:T(1,128)} %own_table.1) | copy-start | bytes 100
  3.9 1.4 %collective-permute-start.1 = (bf16[3,128,128]{2,1,0:T(8,128)(2,1)S(1)}, bf16[3,128,128]{2,1,0:T(8,128)(2,1)S(1)}, u32[]{:S(2)}, u32[]{:S(2)}) collective-permute-start(bf16[3,128,128]{2,1,0:T(8,128)(2,1)S(1)} %get-tuple-element.22), channel_id=1, source_target_pairs={{0,1},{1,0},{2,3},{3,2},{4,5},{5,4},{6,7},{7,6},{8,9},{9,8},{10,11... | collective-permute-start | bytes 294920 | tf_op jit(solution)/shard_map/ppermute | solution.py:238
  5.3 10.3 %collective-permute-start.2 = (bf16[2,128,128]{2,1,0:T(8,128)(2,1)S(1)}, bf16[2,128,128]{2,1,0:T(8,128)(2,1)S(1)}, u32[]{:S(2)}, u32[]{:S(2)}) collective-permute-start(bf16[2,128,128]{2,1,0:T(8,128)(2,1)S(1)} %pad_maximum_fusion), channel_id=1, source_target_pairs={{0,24},{1,21},{2,26},{3,23},{4,28},{5,17},{6,30},{7,19},{8,16},{9,... | collective-permute-start | bytes 196616 | tf_op jit(solution)/shard_map/ppermute | solution.py:235
  10.1 8.2 %collective-permute-start.3 = (bf16[2,128,128]{2,1,0:T(8,128)(2,1)S(1)}, bf16[2,128,128]{2,1,0:T(8,128)(2,1)S(1)}, u32[]{:S(2)}, u32[]{:S(2)}) collective-permute-start(bf16[2,128,128]{2,1,0:T(8,128)(2,1)S(1)} %pad_maximum_fusion.1), channel_id=1, source_target_pairs={{0,16},{1,13},{2,18},{3,15},{4,20},{5,9},{6,22},{7,11},{8,24},{9,5... | collective-permute-start | bytes 196616 | tf_op jit(solution)/shard_map/ppermute | solution.py:235
  10.2 8.1 %collective-permute-start.4 = (bf16[2,128,128]{2,1,0:T(8,128)(2,1)S(1)}, bf16[2,128,128]{2,1,0:T(8,128)(2,1)S(1)}, u32[]{:S(2)}, u32[]{:S(2)}) collective-permute-start(bf16[2,128,128]{2,1,0:T(8,128)(2,1)S(1)} %pad_maximum_fusion.2), channel_id=1, source_target_pairs={{0,8},{1,5},{2,10},{3,7},{4,12},{5,1},{6,14},{7,3},{8,0},{9,13},{1... | collective-permute-start | bytes 196616 | tf_op jit(solution)/shard_map/ppermute | solution.py:235
  10.8 7.5 %collective-permute-start.5 = (bf16[1,128,128]{2,1,0:T(8,128)(2,1)S(1)}, bf16[1,128,128]{2,1,0:T(8,128)(2,1)S(1)}, u32[]{:S(2)}, u32[]{:S(2)}) collective-permute-start(bf16[1,128,128]{2,1,0:T(8,128)(2,1)S(1)} %get-tuple-element.26), channel_id=1, source_target_pairs={{0,28},{1,29},{2,30},{3,31},{4,24},{5,25},{6,26},{7,27},{8,20},{9,... | collective-permute-start | bytes 98312 | tf_op jit(solution)/shard_map/ppermute | solution.py:235
  18.5 1.4 %collective-permute-start.6 = (bf16[4,128,128]{2,1,0:T(8,128)(2,1)S(1)}, bf16[4,128,128]{2,1,0:T(8,128)(2,1)S(1)}, u32[]{:S(2)}, u32[]{:S(2)}) collective-permute-start(bf16[4,128,128]{2,1,0:T(8,128)(2,1)S(1)} %get-tuple-element.27), channel_id=1, source_target_pairs={{0,1},{1,0},{2,3},{3,2},{4,5},{5,4},{6,7},{7,6},{8,9},{9,8},{10,11... | collective-permute-start | bytes 393224 | tf_op jit(solution)/shard_map/ppermute | solution.py:244
  20.0 4.3 %collective-permute-start.7 = (bf16[2,128,128]{2,1,0:T(8,128)(2,1)S(1)}, bf16[2,128,128]{2,1,0:T(8,128)(2,1)S(1)}, u32[]{:S(2)}, u32[]{:S(2)}) collective-permute-start(bf16[2,128,128]{2,1,0:T(8,128)(2,1)S(1)} %get-tuple-element.30), channel_id=1, source_target_pairs={{0,2},{1,3},{2,0},{3,1},{4,6},{5,7},{6,4},{7,5},{8,10},{9,11},{10,... | collective-permute-start | bytes 196616 | tf_op jit(solution)/shard_map/ppermute | solution.py:245

commit v4 on v3

--- a/solution.py
+++ b/solution.py
@@ -121,11 +121,8 @@
     quarter = (total.shape[0] - 1) // 4
     total[...] = jnp.zeros_like(total)
     total[own_table[0, fixed(0, 0)]] = held[0].astype(jnp.float32)
-    source = flipped(core, 0)
-    total[own_table[0, source]] += received[0].astype(jnp.float32)
-    total[other_table[0, source]] += received[1].astype(jnp.float32)
-    targets = [table[0, flipped(core, i)] for i in (1, 2) for table in (own_table, other_table)]
-    targets.append(own_table[0, fixed(*FAR)])
+    total[own_table[0, fixed(*FAR)]] += received[0].astype(jnp.float32)
+    targets = [table[0, flipped(core, i)] for i in range(3) for table in (own_table, other_table)]
     for side, half in enumerate((1 - core, core)):
         for x in range(2):
             for j in range(quarter):
@@ -137,8 +134,8 @@
                     chosen[s, at] = jnp.full(chosen.shape[2:], one, jnp.float32)
 
 
-def second_kernel(part, chosen, near, nearest, far, give, keep):
-    slots = [near[0], near[1], nearest[0], nearest[1], far[0]]
+def second_kernel(part, chosen, long, near, nearest, give, keep):
+    slots = [long[0], long[1], near[0], near[1], nearest[0], nearest[1]]
     half, states = give.shape[0], give.shape[1]
     for at in range(2 * half):
         tile = part[at].reshape(states // 8, 8, states)
@@ -159,14 +156,15 @@
         first_kernel,
         out_shape=[
             jax.ShapeDtypeStruct(whole, jnp.float32),
-            jax.ShapeDtypeStruct((5, tiles, 8, states), jnp.float32),
+            jax.ShapeDtypeStruct((6, tiles, 8, states), jnp.float32),
         ],
         in_specs=[SMEM] * 2 + [VMEM] * 2,
         out_specs=[VMEM] * 2,
         scratch_shapes=[pltpu.VMEM((tiles + 1, states, states), jnp.float32)],
         compiler_params=pltpu.CompilerParams(vmem_limit_bytes=16 * 1024 * 1024),
         name="first_sums",
-    )(own_table, other_table, longest, held)
+        cost_estimate=pl.CostEstimate(flops=2 * 10**9, bytes_accessed=10**6, transcendentals=0),
+    )(own_table, other_table, far, held)
     return pl.pallas_call(
         second_kernel,
         out_shape=[
@@ -177,7 +175,7 @@
         out_specs=[VMEM] * 2,
         compiler_params=pltpu.CompilerParams(vmem_limit_bytes=16 * 1024 * 1024),
         name="second_sums",
-    )(part, chosen, near, nearest, far)
+    )(part, chosen, longest, near, nearest)
 
 
 def cross_kernel(received, kept, give, keep):
@@ -215,12 +213,13 @@
 
     share = wave.shape[0] // n_mpo
     core = lambda flip: jnp.bitwise_xor(lax.rem(lax.axis_index("mpo"), 2), flip)
-    give, keep, far, held, live = couple(
+    give, rest, live = couple(
         [
             (lambda: [flipped(core(1), i) for i in range(3)], 3),
-            (lambda: [flipped(core(0), i) for i in range(3)], 3),
-            (lambda: [fixed(*FAR)], 1),
-            (lambda: [fixed(0, 0)], 1),
+            (
+                lambda: [flipped(core(0), i) for i in range(3)] + [fixed(*FAR), fixed(0, 0)],
+                5,
+            ),
         ],
         (lambda: lax.axis_index("mpo") * share, share),
         n_left * n_right,
@@ -236,6 +235,7 @@
 
     give, other_table = lax.optimization_barrier((give, other_table))
     got = lax.ppermute(give, "mpo", swap_core)
+    keep, far, held = rest[:3], rest[3:4], rest[4:]
     far = move(far, (FAR, FAR))
     received = [
         move(jnp.stack([keep[i], got[i]]), (SETS[0][i], SETS[1][i])) for i in range(3)

time: 25.1 us -> 24.1 us (0.960)
  waiting for transfers between devices: 7.33 us -> 6.05 us
    ppermute x1, waiting for transfers between devices: 1.24 us -> 0.01 us  [by_permutes(): got = lax.ppermute(give, 'mpo', swap_core)]
    ppermute x4, starting transfers between devices: 10.3 us -> 10.6 us  [move(): return lax.ppermute(x, axes, perm)]
  transfers between devices with their start and end apart: 8 -> 8, of which waited for: 4 -> 4; matrix products, arithmetic and copies ran while one was open for 0% -> 0% of each run, Pallas kernels for 16% -> 17%
where the time goes in v4:
time: 24.1 us; the launch traced here: 24 us
  starting transfers between devices  12.8 us (53%)
  waiting for transfers between devices  6.05 us (25%)
  Pallas kernels  4.32 us (18%)
  other arithmetic  0.69 us (3%)
    ppermute x4, starting transfers between devices, move(): return lax.ppermute(x, axes, perm)  10.6 us
    pallas_call x1, Pallas kernels, couple(): pl.pallas_call(functools.partial(couple_kernel, [g for g, _ in groups], s...  3.41 us
    ppermute x1, waiting for transfers between devices, by_permutes(): summed = keep + lax.ppermute(give, 'mpo', swap_chip).astype(jnp.float32)  2.78 us
    ppermute x4, waiting for transfers between devices, move(): return lax.ppermute(x, axes, perm)  1.93 us
    ppermute x1, starting transfers between devices, by_permutes(): summed = keep + lax.ppermute(give, 'mpo', swap_chip).astype(jnp.float32)  1.55 us
    ppermute x1, waiting for transfers between devices, by_permutes(): give, keep = cross(lax.ppermute(give, 'mpo', swap_core), keep)  1.33 us
    convert_element_type x1, other arithmetic, by_permutes(): return jnp.where(live > 0, summed, 0.0).astype(jnp.bfloat16)  0.66 us
    pallas_call x1, Pallas kernels, gather(): pl.pallas_call(first_kernel, out_shape=[jax.ShapeDtypeStruct(whole, jnp.f...  0.65 us
  transfers between devices with their start and end apart: 8, of which 4 were waited for; matrix products, arithmetic and copies ran while one was open for 0% of the time, Pallas kernels for 17%

profile of v4, /device:TPU:0, one launch (start us, length us, event | category | flops | bytes accessed | tf_op | source)
XLA Modules:
  0.0 24.0 jit_solution(6534297897281365163)
XLA Ops:
  0.0 0.5 %collective-permute-start = (s32[1,8]{1,0:T(1,128)}, s32[1,8]{1,0:T(1,128)S(1)}, u32[]{:S(2)}, u32[]{:S(2)}) collective-permute-start(s32[1,8]{1,0:T(1,128)} %own_table.1), channel_id=1, source_target_pairs={{0,1},{1,0},{2,3},{3,2},{4,5},{5,4},{6,7},{7,6},{8,9},{9,8},{10,11... | collective-permute-start | bytes 104 | tf_op jit(solution)/shard_map/ppermute | solution.py:212
  0.5 0.0 copy-start
  0.5 3.4 %couple.1 = (bf16[3,128,128]{2,1,0:T(8,128)(2,1)S(1)}, bf16[5,128,128]{2,1,0:T(8,128)(2,1)S(1)}, bf16[2,128,128]{2,1,0:T(8,128)(2,1)S(1)}) custom-call(s32[8]{0:T(128)} %refs_0_.1, s32[8]{0:T(128)} %refs_1_.1, s32[4]{0:T(128)} %refs_2_.1, s32[4]{0:T(128)} %refs_3_.1, s32[8,10]{1,0:T(8,128)} %bitcast.1, bf16[8,128,128]{2,1,0:T(8,128)(2,1)} %refs_5_.1, ...), custom_call_target="tpu_custom_call" | custom-call | tf_op jit(solution)/shard_map/couple/pallas_call | solution.py:81
  3.9 0.0 collective-permute-done.other_table
  3.9 0.1 collective-permute-start.2
  4.0 6.1 %collective-permute-start.1 = (bf16[1,128,128]{2,1,0:T(8,128)(2,1)S(1)}, bf16[1,128,128]{2,1,0:T(8,128)(2,1)S(1)}, u32[]{:S(2)}, u32[]{:S(2)}) collective-permute-start(bf16[1,128,128]{2,1,0:T(8,128)(2,1)S(1)} %get-tuple-element.31), channel_id=1, source_target_pairs={{0,28},{1,29},{2,30},{3,31},{4,24},{5,25},{6,26},{7,27},{8,20},{9,... | collective-permute-start | bytes 98312 | tf_op jit(solution)/shard_map/ppermute | solution.py:234
  10.1 0.0 collective-permute-done.2
  10.1 0.3 %collective-permute-start.3 = (bf16[2,128,128]{2,1,0:T(8,128)(2,1)S(1)}, bf16[2,128,128]{2,1,0:T(8,128)(2,1)S(1)}, u32[]{:S(2)}, u32[]{:S(2)}) collective-permute-start(bf16[2,128,128]{2,1,0:T(8,128)(2,1)S(1)} %pad_maximum_fusion), channel_id=1, source_target_pairs={{0,24},{1,21},{2,26},{3,23},{4,28},{5,17},{6,30},{7,19},{8,16},{9,... | collective-permute-start | bytes 196616 | tf_op jit(solution)/shard_map/ppermute | solution.py:234
  10.4 0.9 %collective-permute-start.4 = (bf16[2,128,128]{2,1,0:T(8,128)(2,1)S(1)}, bf16[2,128,128]{2,1,0:T(8,128)(2,1)S(1)}, u32[]{:S(2)}, u32[]{:S(2)}) collective-permute-start(bf16[2,128,128]{2,1,0:T(8,128)(2,1)S(1)} %pad_maximum_fusion.1), channel_id=1, source_target_pairs={{0,16},{1,13},{2,18},{3,15},{4,20},{5,9},{6,22},{7,11},{8,24},{9,5... | collective-permute-start | bytes 196616 | tf_op jit(solution)/shard_map/ppermute | solution.py:234
  11.3 3.4 %collective-permute-start.5 = (bf16[2,128,128]{2,1,0:T(8,128)(2,1)S(1)}, bf16[2,128,128]{2,1,0:T(8,128)(2,1)S(1)}, u32[]{:S(2)}, u32[]{:S(2)}) collective-permute-start(bf16[2,128,128]{2,1,0:T(8,128)(2,1)S(1)} %pad_maximum_fusion.2), channel_id=1, source_target_pairs={{0,8},{1,5},{2,10},{3,7},{4,12},{5,1},{6,14},{7,3},{8,0},{9,13},{1... | collective-permute-start | bytes 196616 | tf_op jit(solution)/shard_map/ppermute | solution.py:234
  14.7 0.0 collective-permute-done.1.received
  14.7 0.0 copy-done
  14.7 0.6 %first_sums.1 = (f32[8,128,128]{2,1,0:T(8,128)S(1)}, f32[6,8,8,128]{3,2,1,0:T(8,128)S(1)}) custom-call(s32[1,8]{1,0:T(1,128)S(1)} %copy-done, s32[1,8]{1,0:T(1,128)S(1)} %collective-permute-done.other_table, bf16[1,128,128]{2,1,0:T(8,128)(2,1)S(1)} %collective-permute-done.1.received, bf16[1,128,128]{2,1,0:T(8,128)(2,1)S(1)} %get-tuple-element.30.held), custom_call_target="tpu_custom_call" | custom-call | flops 2000000000 | bytes 1000000 | tf_op jit(solution)/shard_map/first_sums/pallas_call | solution.py:155
  15.4 1.6 %collective-permute-done.3.long = bf16[2,128,128]{2,1,0:T(8,128)(2,1)S(1)} collective-permute-done((bf16[2,128,128]{2,1,0:T(8,128)(2,1)S(1)}, bf16[2,128,128]{2,1,0:T(8,128)(2,1)S(1)}, u32[]{:S(2)}, u32[]{:S(2)}) %collective-permute-start.3) | collective-permute-done | bytes 65568 | tf_op jit(solution)/shard_map/ppermute | solution.py:234
  16.9 0.0 collective-permute-done.4.near
  16.9 0.4 %collective-permute-done.5.nearest = bf16[2,128,128]{2,1,0:T(8,128)(2,1)S(1)} collective-permute-done((bf16[2,128,128]{2,1,0:T(8,128)(2,1)S(1)}, bf16[2,128,128]{2,1,0:T(8,128)(2,1)S(1)}, u32[]{:S(2)}, u32[]{:S(2)}) %collective-permute-start.5) | collective-permute-done | bytes 65568 | tf_op jit(solution)/shard_map/ppermute | solution.py:234
  17.3 0.2 second_sums.1
  17.5 0.1 collective-permute-start.6
  17.6 1.3 %collective-permute-done.6.received = bf16[4,128,128]{2,1,0:T(8,128)(2,1)S(1)} collective-permute-done((bf16[4,128,128]{2,1,0:T(8,128)(2,1)S(1)}, bf16[4,128,128]{2,1,0:T(8,128)(2,1)S(1)}, u32[]{:S(2)}, u32[]{:S(2)}) %collective-permute-start.6) | collective-permute-done | bytes 131104 | tf_op jit(solution)/shard_map/ppermute | solution.py:244
  19.0 1.6 %collective-permute-start.7 = (bf16[2,128,128]{2,1,0:T(8,128)(2,1)S(1)}, bf16[2,128,128]{2,1,0:T(8,128)(2,1)S(1)}, u32[]{:S(2)}, u32[]{:S(2)}) collective-permute-start(bf16[2,128,128]{2,1,0:T(8,128)(2,1)S(1)} %get-tuple-element.26), channel_id=1, source_target_pairs={{0,2},{1,3},{2,0},{3,1},{4,6},{5,7},{6,4},{7,5},{8,10},{9,11},{10,... | collective-permute-start | bytes 196616 | tf_op jit(solution)/shard_map/ppermute | solution.py:245
  20.5 2.8 %collective-permute-done.7 = bf16[2,128,128]{2,1,0:T(8,128)(2,1)S(1)} collective-permute-done((bf16[2,128,128]{2,1,0:T(8,128)(2,1)S(1)}, bf16[2,128,128]{2,1,0:T(8,128)(2,1)S(1)}, u32[]{:S(2)}, u32[]{:S(2)}) %collective-permute-start.7) | collective-permute-done | bytes 65568 | tf_op jit(solution)/shard_map/ppermute | solution.py:245
  23.3 0.7 %select_convert_fusion = bf16[2,128,128]{2,1,0:T(8,128)(2,1)} fusion(f32[2,128,128]{2,1,0:T(8,128)S(1)} %get-tuple-element.25, bf16[2,128,128]{2,1,0:T(8,128)(2,1)S(1)} %collective-permute-done.7, bf16[2,128,128]{2,1,0:T(8,128)(2,1)S(1)} %get-tuple-element.16), kind=kLoop, calls=%fused_computation | loop fusion | flops 163840 | bytes 327680 | tf_op jit(solution)/shard_map/convert_element_type | solution.py:246
  (6 shorter events, 0.1 us)
Async XLA Ops:
  0.0 3.9 %collective-permute-start = (s32[1,8]{1,0:T(1,128)}, s32[1,8]{1,0:T(1,128)S(1)}, u32[]{:S(2)}, u32[]{:S(2)}) collective-permute-start(s32[1,8]{1,0:T(1,128)} %own_table.1), channel_id=1, source_target_pairs={{0,1},{1,0},{2,3},{3,2},{4,5},{5,4},{6,7},{7,6},{8,9},{9,8},{10,11... | collective-permute-start | bytes 104 | tf_op jit(solution)/shard_map/ppermute | solution.py:212
  0.5 14.3 %copy-start = (s32[1,8]{1,0:T(1,128)S(1)}, s32[1,8]{1,0:T(1,128)}, u32[]{:S(2)}) copy-start(s32[1,8]{1,0:T(1,128)} %own_table.1) | copy-start | bytes 100
  3.9 6.2 %collective-permute-start.2 = (bf16[3,128,128]{2,1,0:T(8,128)(2,1)S(1)}, bf16[3,128,128]{2,1,0:T(8,128)(2,1)S(1)}, u32[]{:S(2)}, u32[]{:S(2)}) collective-permute-start(bf16[3,128,128]{2,1,0:T(8,128)(2,1)S(1)} %get-tuple-element.22), channel_id=1, source_target_pairs={{0,1},{1,0},{2,3},{3,2},{4,5},{5,4},{6,7},{7,6},{8,9},{9,8},{10,11... | collective-permute-start | bytes 294920 | tf_op jit(solution)/shard_map/ppermute | solution.py:237
  4.0 10.7 %collective-permute-start.1 = (bf16[1,128,128]{2,1,0:T(8,128)(2,1)S(1)}, bf16[1,128,128]{2,1,0:T(8,128)(2,1)S(1)}, u32[]{:S(2)}, u32[]{:S(2)}) collective-permute-start(bf16[1,128,128]{2,1,0:T(8,128)(2,1)S(1)} %get-tuple-element.31), channel_id=1, source_target_pairs={{0,28},{1,29},{2,30},{3,31},{4,24},{5,25},{6,26},{7,27},{8,20},{9,... | collective-permute-start | bytes 98312 | tf_op jit(solution)/shard_map/ppermute | solution.py:234
  10.1 6.8 %collective-permute-start.3 = (bf16[2,128,128]{2,1,0:T(8,128)(2,1)S(1)}, bf16[2,128,128]{2,1,0:T(8,128)(2,1)S(1)}, u32[]{:S(2)}, u32[]{:S(2)}) collective-permute-start(bf16[2,128,128]{2,1,0:T(8,128)(2,1)S(1)} %pad_maximum_fusion), channel_id=1, source_target_pairs={{0,24},{1,21},{2,26},{3,23},{4,28},{5,17},{6,30},{7,19},{8,16},{9,... | collective-permute-start | bytes 196616 | tf_op jit(solution)/shard_map/ppermute | solution.py:234
  10.4 6.5 %collective-permute-start.4 = (bf16[2,128,128]{2,1,0:T(8,128)(2,1)S(1)}, bf16[2,128,128]{2,1,0:T(8,128)(2,1)S(1)}, u32[]{:S(2)}, u32[]{:S(2)}) collective-permute-start(bf16[2,128,128]{2,1,0:T(8,128)(2,1)S(1)} %pad_maximum_fusion.1), channel_id=1, source_target_pairs={{0,16},{1,13},{2,18},{3,15},{4,20},{5,9},{6,22},{7,11},{8,24},{9,5... | collective-permute-start | bytes 196616 | tf_op jit(solution)/shard_map/ppermute | solution.py:234
  11.3 6.0 %collective-permute-start.5 = (bf16[2,128,128]{2,1,0:T(8,128)(2,1)S(1)}, bf16[2,128,128]{2,1,0:T(8,128)(2,1)S(1)}, u32[]{:S(2)}, u32[]{:S(2)}) collective-permute-start(bf16[2,128,128]{2,1,0:T(8,128)(2,1)S(1)} %pad_maximum_fusion.2), channel_id=1, source_target_pairs={{0,8},{1,5},{2,10},{3,7},{4,12},{5,1},{6,14},{7,3},{8,0},{9,13},{1... | collective-permute-start | bytes 196616 | tf_op jit(solution)/shard_map/ppermute | solution.py:234
  17.5 1.4 %collective-permute-start.6 = (bf16[4,128,128]{2,1,0:T(8,128)(2,1)S(1)}, bf16[4,128,128]{2,1,0:T(8,128)(2,1)S(1)}, u32[]{:S(2)}, u32[]{:S(2)}) collective-permute-start(bf16[4,128,128]{2,1,0:T(8,128)(2,1)S(1)} %get-tuple-element.23), channel_id=1, source_target_pairs={{0,1},{1,0},{2,3},{3,2},{4,5},{5,4},{6,7},{7,6},{8,9},{9,8},{10,11... | collective-permute-start | bytes 393224 | tf_op jit(solution)/shard_map/ppermute | solution.py:244
  19.0 4.3 %collective-permute-start.7 = (bf16[2,128,128]{2,1,0:T(8,128)(2,1)S(1)}, bf16[2,128,128]{2,1,0:T(8,128)(2,1)S(1)}, u32[]{:S(2)}, u32[]{:S(2)}) collective-permute-start(bf16[2,128,128]{2,1,0:T(8,128)(2,1)S(1)} %get-tuple-element.26), channel_id=1, source_target_pairs={{0,2},{1,3},{2,0},{3,1},{4,6},{5,7},{6,4},{7,5},{8,10},{9,11},{10,... | collective-permute-start | bytes 196616 | tf_op jit(solution)/shard_map/ppermute | solution.py:245

commit v5 on v4

--- a/solution.py
+++ b/solution.py
@@ -101,28 +101,27 @@
     )(*in_hbm(*tables, wave, left, right))
 
 
-SETS = (((3, 0), (2, 0), (1, 0)), ((2, 1), (1, 1), (0, 1)))
-FAR = (3, 1)
-
-
-def flipped(core, i):
-    z, y = lax.axis_index("lsec"), lax.axis_index("rsec")
-    dz, dy = (jnp.where(core == 0, SETS[0][i][d], SETS[1][i][d]) for d in range(2))
-    return jnp.bitwise_xor(z, dz) * 2 + jnp.bitwise_xor(y, dy)
-
-
-def fixed(dz, dy):
-    z, y = lax.axis_index("lsec"), lax.axis_index("rsec")
-    return jnp.bitwise_xor(z, dz) * 2 + jnp.bitwise_xor(y, dy)
+SETS = (((1, 0), (1, 1), (3, 0)), ((2, 0), (2, 1), (3, 1)))
+SHARED = (0, 1)
+
+
+def pair_at(dz, dy, sign):
+    n_left = lax.axis_size("lsec")
+    z = lax.rem(lax.axis_index("lsec") + n_left + sign * dz, n_left)
+    return z * 2 + jnp.bitwise_xor(lax.axis_index("rsec"), dy)
+
+
+def pair_of(core, i, sign):
+    return pair_at(*(jnp.where(core == 0, SETS[0][i][d], SETS[1][i][d]) for d in range(2)), sign)
 
 
 def first_kernel(own_table, other_table, received, held, part, chosen, total):
     core = lax.rem(lax.axis_index("mpo"), 2)
     quarter = (total.shape[0] - 1) // 4
     total[...] = jnp.zeros_like(total)
-    total[own_table[0, fixed(0, 0)]] = held[0].astype(jnp.float32)
-    total[own_table[0, fixed(*FAR)]] += received[0].astype(jnp.float32)
-    targets = [table[0, flipped(core, i)] for i in range(3) for table in (own_table, other_table)]
+    total[own_table[0, pair_at(0, 0, 1)]] = held[0].astype(jnp.float32)
+    total[own_table[0, pair_at(*SHARED, -1)]] += received[0].astype(jnp.float32)
+    targets = [table[0, pair_of(core, i, -1)] for i in range(3) for table in (own_table, other_table)]
     for side, half in enumerate((1 - core, core)):
         for x in range(2):
             for j in range(quarter):
@@ -134,8 +133,8 @@
                     chosen[s, at] = jnp.full(chosen.shape[2:], one, jnp.float32)
 
 
-def second_kernel(part, chosen, long, near, nearest, give, keep):
-    slots = [long[0], long[1], near[0], near[1], nearest[0], nearest[1]]
+def second_kernel(part, chosen, early, near, nearest, give, keep):
+    slots = [early[0], early[1], near[0], near[1], nearest[0], nearest[1]]
     half, states = give.shape[0], give.shape[1]
     for at in range(2 * half):
         tile = part[at].reshape(states // 8, 8, states)
@@ -149,7 +148,7 @@
             keep[at - half] = tile
 
 
-def gather(own_table, other_table, held, longest, near, nearest, far, tiles):
+def gather(own_table, other_table, held, early, near, nearest, shared, tiles):
     states = held.shape[1]
     whole = (tiles, states, states)
     part, chosen = pl.pallas_call(
@@ -164,7 +163,7 @@
         compiler_params=pltpu.CompilerParams(vmem_limit_bytes=16 * 1024 * 1024),
         name="first_sums",
         cost_estimate=pl.CostEstimate(flops=2 * 10**9, bytes_accessed=10**6, transcendentals=0),
-    )(own_table, other_table, far, held)
+    )(own_table, other_table, shared, held)
     return pl.pallas_call(
         second_kernel,
         out_shape=[
@@ -175,7 +174,7 @@
         out_specs=[VMEM] * 2,
         compiler_params=pltpu.CompilerParams(vmem_limit_bytes=16 * 1024 * 1024),
         name="second_sums",
-    )(part, chosen, longest, near, nearest)
+    )(part, chosen, early, near, nearest)
 
 
 def cross_kernel(received, kept, give, keep):
@@ -215,9 +214,9 @@
     core = lambda flip: jnp.bitwise_xor(lax.rem(lax.axis_index("mpo"), 2), flip)
     give, rest, live = couple(
         [
-            (lambda: [flipped(core(1), i) for i in range(3)], 3),
+            (lambda: [pair_of(core(1), i, 1) for i in range(3)], 3),
             (
-                lambda: [flipped(core(0), i) for i in range(3)] + [fixed(*FAR), fixed(0, 0)],
+                lambda: [pair_of(core(0), i, 1) for i in range(3)] + [pair_at(*SHARED, 1), pair_at(0, 0, 1)],
                 5,
             ),
         ],
@@ -226,21 +225,21 @@
         tile_left, tile_right, left_sizes, right_sizes, send_slot, wave, left, right,
     )
 
-    def move(x, flips):
+    def move(x, steps):
         perm = [
-            (place(z, y, m), place(z ^ flips[m % 2][0], y ^ flips[m % 2][1], m))
+            (place(z, y, m), place((z + steps[m % 2][0]) % n_left, y ^ steps[m % 2][1], m))
             for z, y, m in every
         ]
         return lax.ppermute(x, axes, perm)
 
     give, other_table = lax.optimization_barrier((give, other_table))
     got = lax.ppermute(give, "mpo", swap_core)
-    keep, far, held = rest[:3], rest[3:4], rest[4:]
-    far = move(far, (FAR, FAR))
+    keep, shared, held = rest[:3], rest[3:4], rest[4:]
+    shared = move(shared, (SHARED, SHARED))
     received = [
         move(jnp.stack([keep[i], got[i]]), (SETS[0][i], SETS[1][i])) for i in range(3)
     ]
-    give, keep = gather(recv_tile, other_table, held, *received, far, wave.shape[0])
+    give, keep = gather(recv_tile, other_table, held, *received, shared, wave.shape[0])
     give, keep = cross(lax.ppermute(give, "mpo", swap_core), keep)
     summed = keep + lax.ppermute(give, "mpo", swap_chip).astype(jnp.float32)
     return jnp.where(live > 0, summed, 0.0).astype(jnp.bfloat16)

time: 24.1 us -> 23.2 us (0.963)
  starting transfers between devices: 12.8 us -> 11.1 us
  waiting for transfers between devices: 6.05 us -> 6.88 us
    ppermute x4, starting transfers between devices: 10.6 us -> 8.87 us  [move(): return lax.ppermute(x, axes, perm)]
    ppermute x4, waiting for transfers between devices: 1.93 us -> 2.76 us  [move(): return lax.ppermute(x, axes, perm)]
  transfers between devices with their start and end apart: 8 -> 8, of which waited for: 4 -> 3; matrix products, arithmetic and copies ran while one was open for 0% -> 0% of each run, Pallas kernels for 17% -> 18%
where the time goes in v5:
time: 23.2 us; the launch traced here: 23 us
  starting transfers between devices  11.1 us (48%)
  waiting for transfers between devices  6.88 us (30%)
  Pallas kernels  4.31 us (19%)
  other arithmetic  0.69 us (3%)
    ppermute x4, starting transfers between devices, move(): return lax.ppermute(x, axes, perm)  8.87 us
    pallas_call x1, Pallas kernels, couple(): pl.pallas_call(functools.partial(couple_kernel, [g for g, _ in groups], s...  3.41 us
    ppermute x1, waiting for transfers between devices, by_permutes(): summed = keep + lax.ppermute(give, 'mpo', swap_chip).astype(jnp.float32)  2.78 us
    ppermute x4, waiting for transfers between devices, move(): return lax.ppermute(x, axes, perm)  2.76 us
    ppermute x1, starting transfers between devices, by_permutes(): summed = keep + lax.ppermute(give, 'mpo', swap_chip).astype(jnp.float32)  1.55 us
    ppermute x1, waiting for transfers between devices, by_permutes(): give, keep = cross(lax.ppermute(give, 'mpo', swap_core), keep)  1.33 us
    convert_element_type x1, other arithmetic, by_permutes(): return jnp.where(live > 0, summed, 0.0).astype(jnp.bfloat16)  0.66 us
    pallas_call x1, Pallas kernels, gather(): pl.pallas_call(first_kernel, out_shape=[jax.ShapeDtypeStruct(whole, jnp.f...  0.64 us
  transfers between devices with their start and end apart: 8, of which 3 were waited for; matrix products, arithmetic and copies ran while one was open for 0% of the time, Pallas kernels for 18%

profile of v5, /device:TPU:0, one launch (start us, length us, event | category | flops | bytes accessed | tf_op | source)
XLA Modules:
  0.0 23.0 jit_solution(2516451403393755547)
XLA Ops:
  0.0 0.5 %collective-permute-start = (s32[1,8]{1,0:T(1,128)}, s32[1,8]{1,0:T(1,128)S(1)}, u32[]{:S(2)}, u32[]{:S(2)}) collective-permute-start(s32[1,8]{1,0:T(1,128)} %own_table.1), channel_id=1, source_target_pairs={{0,1},{1,0},{2,3},{3,2},{4,5},{5,4},{6,7},{7,6},{8,9},{9,8},{10,11... | collective-permute-start | bytes 104 | tf_op jit(solution)/shard_map/ppermute | solution.py:211
  0.5 0.0 copy-start
  0.5 3.4 %couple.1 = (bf16[3,128,128]{2,1,0:T(8,128)(2,1)S(1)}, bf16[5,128,128]{2,1,0:T(8,128)(2,1)S(1)}, bf16[2,128,128]{2,1,0:T(8,128)(2,1)S(1)}) custom-call(s32[8]{0:T(128)} %refs_0_.1, s32[8]{0:T(128)} %refs_1_.1, s32[4]{0:T(128)} %refs_2_.1, s32[4]{0:T(128)} %refs_3_.1, s32[8,10]{1,0:T(8,128)} %bitcast.1, bf16[8,128,128]{2,1,0:T(8,128)(2,1)} %refs_5_.1, ...), custom_call_target="tpu_custom_call" | custom-call | tf_op jit(solution)/shard_map/couple/pallas_call | solution.py:81
  3.9 0.0 collective-permute-done.other_table
  3.9 0.1 collective-permute-start.2
  4.0 3.0 %collective-permute-start.1 = (bf16[1,128,128]{2,1,0:T(8,128)(2,1)S(1)}, bf16[1,128,128]{2,1,0:T(8,128)(2,1)S(1)}, u32[]{:S(2)}, u32[]{:S(2)}) collective-permute-start(bf16[1,128,128]{2,1,0:T(8,128)(2,1)S(1)} %get-tuple-element.31), channel_id=1, source_target_pairs={{0,4},{1,5},{2,6},{3,7},{4,0},{5,1},{6,2},{7,3},{8,12},{9,13},{10,... | collective-permute-start | bytes 98312 | tf_op jit(solution)/shard_map/ppermute | solution.py:233
  7.1 0.0 collective-permute-done.2
  7.1 1.6 %collective-permute-start.3 = (bf16[2,128,128]{2,1,0:T(8,128)(2,1)S(1)}, bf16[2,128,128]{2,1,0:T(8,128)(2,1)S(1)}, u32[]{:S(2)}, u32[]{:S(2)}) collective-permute-start(bf16[2,128,128]{2,1,0:T(8,128)(2,1)S(1)} %pad_maximum_fusion), channel_id=1, source_target_pairs={{0,8},{1,17},{2,10},{3,19},{4,12},{5,21},{6,14},{7,23},{8,16},{9,2... | collective-permute-start | bytes 196616 | tf_op jit(solution)/shard_map/ppermute | solution.py:233
  8.7 1.9 %collective-permute-start.4 = (bf16[2,128,128]{2,1,0:T(8,128)(2,1)S(1)}, bf16[2,128,128]{2,1,0:T(8,128)(2,1)S(1)}, u32[]{:S(2)}, u32[]{:S(2)}) collective-permute-start(bf16[2,128,128]{2,1,0:T(8,128)(2,1)S(1)} %pad_maximum_fusion.1), channel_id=1, source_target_pairs={{0,12},{1,21},{2,14},{3,23},{4,8},{5,17},{6,10},{7,19},{8,20},{9,2... | collective-permute-start | bytes 196616 | tf_op jit(solution)/shard_map/ppermute | solution.py:233
  10.6 2.3 %collective-permute-start.5 = (bf16[2,128,128]{2,1,0:T(8,128)(2,1)S(1)}, bf16[2,128,128]{2,1,0:T(8,128)(2,1)S(1)}, u32[]{:S(2)}, u32[]{:S(2)}) collective-permute-start(bf16[2,128,128]{2,1,0:T(8,128)(2,1)S(1)} %pad_maximum_fusion.2), channel_id=1, source_target_pairs={{0,24},{1,29},{2,26},{3,31},{4,28},{5,25},{6,30},{7,27},{8,0},{9,5... | collective-permute-start | bytes 196616 | tf_op jit(solution)/shard_map/ppermute | solution.py:233
  12.9 0.0 collective-permute-done.1.received
  12.9 0.0 copy-done
  12.9 0.6 %first_sums.1 = (f32[8,128,128]{2,1,0:T(8,128)S(1)}, f32[6,8,8,128]{3,2,1,0:T(8,128)S(1)}) custom-call(s32[1,8]{1,0:T(1,128)S(1)} %copy-done, s32[1,8]{1,0:T(1,128)S(1)} %collective-permute-done.other_table, bf16[1,128,128]{2,1,0:T(8,128)(2,1)S(1)} %collective-permute-done.1.received, bf16[1,128,128]{2,1,0:T(8,128)(2,1)S(1)} %get-tuple-element.30.held), custom_call_target="tpu_custom_call" | custom-call | flops 2000000000 | bytes 1000000 | tf_op jit(solution)/shard_map/first_sums/pallas_call | solution.py:154
  13.6 0.0 collective-permute-done.3.early
  13.6 2.8 %collective-permute-done.4.near = bf16[2,128,128]{2,1,0:T(8,128)(2,1)S(1)} collective-permute-done((bf16[2,128,128]{2,1,0:T(8,128)(2,1)S(1)}, bf16[2,128,128]{2,1,0:T(8,128)(2,1)S(1)}, u32[]{:S(2)}, u32[]{:S(2)}) %collective-permute-start.4) | collective-permute-done | bytes 65568 | tf_op jit(solution)/shard_map/ppermute | solution.py:233
  16.4 0.0 collective-permute-done.5.nearest
  16.4 0.2 %second_sums.1 = (bf16[4,128,128]{2,1,0:T(8,128)(2,1)S(1)}, f32[4,128,128]{2,1,0:T(8,128)S(1)}) custom-call(f32[8,128,128]{2,1,0:T(8,128)S(1)} %get-tuple-element.20.part, f32[6,8,8,128]{3,2,1,0:T(8,128)S(1)} %get-tuple-element.21.chosen, bf16[2,128,128]{2,1,0:T(8,128)(2,1)S(1)} %collective-permute-done.3.early, ...), custom_call_target="tpu_custom_call" | custom-call | tf_op jit(solution)/shard_map/second_sums/pallas_call | solution.py:167
  16.6 0.1 collective-permute-start.6
  16.7 1.3 %collective-permute-done.6.received = bf16[4,128,128]{2,1,0:T(8,128)(2,1)S(1)} collective-permute-done((bf16[4,128,128]{2,1,0:T(8,128)(2,1)S(1)}, bf16[4,128,128]{2,1,0:T(8,128)(2,1)S(1)}, u32[]{:S(2)}, u32[]{:S(2)}) %collective-permute-start.6) | collective-permute-done | bytes 131104 | tf_op jit(solution)/shard_map/ppermute | solution.py:243
  18.0 1.6 %collective-permute-start.7 = (bf16[2,128,128]{2,1,0:T(8,128)(2,1)S(1)}, bf16[2,128,128]{2,1,0:T(8,128)(2,1)S(1)}, u32[]{:S(2)}, u32[]{:S(2)}) collective-permute-start(bf16[2,128,128]{2,1,0:T(8,128)(2,1)S(1)} %get-tuple-element.26), channel_id=1, source_target_pairs={{0,2},{1,3},{2,0},{3,1},{4,6},{5,7},{6,4},{7,5},{8,10},{9,11},{10,... | collective-permute-start | bytes 196616 | tf_op jit(solution)/shard_map/ppermute | solution.py:244
  19.6 2.8 %collective-permute-done.7 = bf16[2,128,128]{2,1,0:T(8,128)(2,1)S(1)} collective-permute-done((bf16[2,128,128]{2,1,0:T(8,128)(2,1)S(1)}, bf16[2,128,128]{2,1,0:T(8,128)(2,1)S(1)}, u32[]{:S(2)}, u32[]{:S(2)}) %collective-permute-start.7) | collective-permute-done | bytes 65568 | tf_op jit(solution)/shard_map/ppermute | solution.py:244
  22.4 0.7 %select_convert_fusion = bf16[2,128,128]{2,1,0:T(8,128)(2,1)} fusion(f32[2,128,128]{2,1,0:T(8,128)S(1)} %get-tuple-element.25, bf16[2,128,128]{2,1,0:T(8,128)(2,1)S(1)} %collective-permute-done.7, bf16[2,128,128]{2,1,0:T(8,128)(2,1)S(1)} %get-tuple-element.16), kind=kLoop, calls=%fused_computation | loop fusion | flops 163840 | bytes 327680 | tf_op jit(solution)/shard_map/convert_element_type | solution.py:245
  (6 shorter events, 0.1 us)
Async XLA Ops:
  0.0 3.9 %collective-permute-start = (s32[1,8]{1,0:T(1,128)}, s32[1,8]{1,0:T(1,128)S(1)}, u32[]{:S(2)}, u32[]{:S(2)}) collective-permute-start(s32[1,8]{1,0:T(1,128)} %own_table.1), channel_id=1, source_target_pairs={{0,1},{1,0},{2,3},{3,2},{4,5},{5,4},{6,7},{7,6},{8,9},{9,8},{10,11... | collective-permute-start | bytes 104 | tf_op jit(solution)/shard_map/ppermute | solution.py:211
  0.5 12.5 %copy-start = (s32[1,8]{1,0:T(1,128)S(1)}, s32[1,8]{1,0:T(1,128)}, u32[]{:S(2)}) copy-start(s32[1,8]{1,0:T(1,128)} %own_table.1) | copy-start | bytes 100
  3.9 3.2 %collective-permute-start.2 = (bf16[3,128,128]{2,1,0:T(8,128)(2,1)S(1)}, bf16[3,128,128]{2,1,0:T(8,128)(2,1)S(1)}, u32[]{:S(2)}, u32[]{:S(2)}) collective-permute-start(bf16[3,128,128]{2,1,0:T(8,128)(2,1)S(1)} %get-tuple-element.22), channel_id=1, source_target_pairs={{0,1},{1,0},{2,3},{3,2},{4,5},{5,4},{6,7},{7,6},{8,9},{9,8},{10,11... | collective-permute-start | bytes 294920 | tf_op jit(solution)/shard_map/ppermute | solution.py:236
  4.0 8.9 %collective-permute-start.1 = (bf16[1,128,128]{2,1,0:T(8,128)(2,1)S(1)}, bf16[1,128,128]{2,1,0:T(8,128)(2,1)S(1)}, u32[]{:S(2)}, u32[]{:S(2)}) collective-permute-start(bf16[1,128,128]{2,1,0:T(8,128)(2,1)S(1)} %get-tuple-element.31), channel_id=1, source_target_pairs={{0,4},{1,5},{2,6},{3,7},{4,0},{5,1},{6,2},{7,3},{8,12},{9,13},{10,... | collective-permute-start | bytes 98312 | tf_op jit(solution)/shard_map/ppermute | solution.py:233
  7.1 6.5 %collective-permute-start.3 = (bf16[2,128,128]{2,1,0:T(8,128)(2,1)S(1)}, bf16[2,128,128]{2,1,0:T(8,128)(2,1)S(1)}, u32[]{:S(2)}, u32[]{:S(2)}) collective-permute-start(bf16[2,128,128]{2,1,0:T(8,128)(2,1)S(1)} %pad_maximum_fusion), channel_id=1, source_target_pairs={{0,8},{1,17},{2,10},{3,19},{4,12},{5,21},{6,14},{7,23},{8,16},{9,2... | collective-permute-start | bytes 196616 | tf_op jit(solution)/shard_map/ppermute | solution.py:233
  8.7 7.6 %collective-permute-start.4 = (bf16[2,128,128]{2,1,0:T(8,128)(2,1)S(1)}, bf16[2,128,128]{2,1,0:T(8,128)(2,1)S(1)}, u32[]{:S(2)}, u32[]{:S(2)}) collective-permute-start(bf16[2,128,128]{2,1,0:T(8,128)(2,1)S(1)} %pad_maximum_fusion.1), channel_id=1, source_target_pairs={{0,12},{1,21},{2,14},{3,23},{4,8},{5,17},{6,10},{7,19},{8,20},{9,2... | collective-permute-start | bytes 196616 | tf_op jit(solution)/shard_map/ppermute | solution.py:233
  10.6 5.7 %collective-permute-start.5 = (bf16[2,128,128]{2,1,0:T(8,128)(2,1)S(1)}, bf16[2,128,128]{2,1,0:T(8,128)(2,1)S(1)}, u32[]{:S(2)}, u32[]{:S(2)}) collective-permute-start(bf16[2,128,128]{2,1,0:T(8,128)(2,1)S(1)} %pad_maximum_fusion.2), channel_id=1, source_target_pairs={{0,24},{1,29},{2,26},{3,31},{4,28},{5,25},{6,30},{7,27},{8,0},{9,5... | collective-permute-start | bytes 196616 | tf_op jit(solution)/shard_map/ppermute | solution.py:233
  16.6 1.4 %collective-permute-start.6 = (bf16[4,128,128]{2,1,0:T(8,128)(2,1)S(1)}, bf16[4,128,128]{2,1,0:T(8,128)(2,1)S(1)}, u32[]{:S(2)}, u32[]{:S(2)}) collective-permute-start(bf16[4,128,128]{2,1,0:T(8,128)(2,1)S(1)} %get-tuple-element.23), channel_id=1, source_target_pairs={{0,1},{1,0},{2,3},{3,2},{4,5},{5,4},{6,7},{7,6},{8,9},{9,8},{10,11... | collective-permute-start | bytes 393224 | tf_op jit(solution)/shard_map/ppermute | solution.py:243
  18.0 4.3 %collective-permute-start.7 = (bf16[2,128,128]{2,1,0:T(8,128)(2,1)S(1)}, bf16[2,128,128]{2,1,0:T(8,128)(2,1)S(1)}, u32[]{:S(2)}, u32[]{:S(2)}) collective-permute-start(bf16[2,128,128]{2,1,0:T(8,128)(2,1)S(1)} %get-tuple-element.26), channel_id=1, source_target_pairs={{0,2},{1,3},{2,0},{3,1},{4,6},{5,7},{6,4},{7,5},{8,10},{9,11},{10,... | collective-permute-start | bytes 196616 | tf_op jit(solution)/shard_map/ppermute | solution.py:244

commit v6 on v5

--- a/solution.py
+++ b/solution.py
@@ -101,14 +101,15 @@
     )(*in_hbm(*tables, wave, left, right))
 
 
-SETS = (((1, 0), (1, 1), (3, 0)), ((2, 0), (2, 1), (3, 1)))
-SHARED = (0, 1)
-
-
-def pair_at(dz, dy, sign):
-    n_left = lax.axis_size("lsec")
-    z = lax.rem(lax.axis_index("lsec") + n_left + sign * dz, n_left)
-    return z * 2 + jnp.bitwise_xor(lax.axis_index("rsec"), dy)
+SETS = (((1, 1), (0, 1), (3, 1)), ((2, 0), (2, 1), (3, 0)))
+SHARED = (1, 0)
+
+
+def pair_at(step, flip, sign):
+    z, n_left = lax.axis_index("lsec"), lax.axis_size("lsec")
+    shifted = lax.rem(z + n_left + sign * step, n_left)
+    to = jnp.where(flip == 0, jnp.bitwise_xor(z, step), shifted)
+    return to * 2 + jnp.bitwise_xor(lax.axis_index("rsec"), flip)
 
 
 def pair_of(core, i, sign):
@@ -225,9 +226,12 @@
         tile_left, tile_right, left_sizes, right_sizes, send_slot, wave, left, right,
     )
 
+    def goes(z, y, step, flip):
+        return ((z + step) % n_left if flip else z ^ step), y ^ flip
+
     def move(x, steps):
         perm = [
-            (place(z, y, m), place((z + steps[m % 2][0]) % n_left, y ^ steps[m % 2][1], m))
+            (place(z, y, m), place(*goes(z, y, *steps[m % 2]), m))
             for z, y, m in every
         ]
         return lax.ppermute(x, axes, perm)

time: 23.2 us -> 22.8 us (0.983)
  waiting for transfers between devices: 6.88 us -> 5.08 us
  starting transfers between devices: 11.1 us -> 12.5 us
    ppermute x4, waiting for transfers between devices: 2.76 us -> 1.23 us  [move(): return lax.ppermute(x, axes, perm)]
    ppermute x1, starting transfers between devices: 0.07 us -> 0.86 us  [by_permutes(): give, keep = cross(lax.ppermute(give, 'mpo', swap_core), keep)]
    ppermute x4, starting transfers between devices: 8.87 us -> 9.5 us  [move(): return lax.ppermute(x, axes, perm)]
    ppermute x1, waiting for transfers between devices: 1.33 us -> 0.99 us  [by_permutes(): give, keep = cross(lax.ppermute(give, 'mpo', swap_core), keep)]
where the time goes in v6:
time: 22.8 us; the launch traced here: 22.7 us
  starting transfers between devices  12.5 us (55%)
  waiting for transfers between devices  5.08 us (22%)
  Pallas kernels  4.32 us (19%)
  other arithmetic  0.69 us (3%)
    ppermute x4, starting transfers between devices, move(): return lax.ppermute(x, axes, perm)  9.5 us
    pallas_call x1, Pallas kernels, couple(): pl.pallas_call(functools.partial(couple_kernel, [g for g, _ in groups], s...  3.41 us
    ppermute x1, waiting for transfers between devices, by_permutes(): summed = keep + lax.ppermute(give, 'mpo', swap_chip).astype(jnp.float32)  2.86 us
    ppermute x1, starting transfers between devices, by_permutes(): summed = keep + lax.ppermute(give, 'mpo', swap_chip).astype(jnp.float32)  1.57 us
    ppermute x4, waiting for transfers between devices, move(): return lax.ppermute(x, axes, perm)  1.23 us
    ppermute x1, waiting for transfers between devices, by_permutes(): give, keep = cross(lax.ppermute(give, 'mpo', swap_core), keep)  0.99 us
    ppermute x1, starting transfers between devices, by_permutes(): give, keep = cross(lax.ppermute(give, 'mpo', swap_core), keep)  0.86 us
    convert_element_type x1, other arithmetic, by_permutes(): return jnp.where(live > 0, summed, 0.0).astype(jnp.bfloat16)  0.66 us
  transfers between devices with their start and end apart: 8, of which 3 were waited for; matrix products, arithmetic and copies ran while one was open for 0% of the time, Pallas kernels for 18%

profile of v6, /device:TPU:0, one launch (start us, length us, event | category | flops | bytes accessed | tf_op | source)
XLA Modules:
  0.0 22.7 jit_solution(11989285608325146933)
XLA Ops:
  0.0 0.5 %collective-permute-start = (s32[1,8]{1,0:T(1,128)}, s32[1,8]{1,0:T(1,128)S(1)}, u32[]{:S(2)}, u32[]{:S(2)}) collective-permute-start(s32[1,8]{1,0:T(1,128)} %own_table.1), channel_id=1, source_target_pairs={{0,1},{1,0},{2,3},{3,2},{4,5},{5,4},{6,7},{7,6},{8,9},{9,8},{10,11... | collective-permute-start | bytes 104 | tf_op jit(solution)/shard_map/ppermute | solution.py:212
  0.5 0.0 copy-start
  0.5 3.4 %couple.1 = (bf16[3,128,128]{2,1,0:T(8,128)(2,1)S(1)}, bf16[5,128,128]{2,1,0:T(8,128)(2,1)S(1)}, bf16[2,128,128]{2,1,0:T(8,128)(2,1)S(1)}) custom-call(s32[8]{0:T(128)} %refs_0_.1, s32[8]{0:T(128)} %refs_1_.1, s32[4]{0:T(128)} %refs_2_.1, s32[4]{0:T(128)} %refs_3_.1, s32[8,10]{1,0:T(8,128)} %bitcast.1, bf16[8,128,128]{2,1,0:T(8,128)(2,1)} %refs_5_.1, ...), custom_call_target="tpu_custom_call" | custom-call | tf_op jit(solution)/shard_map/couple/pallas_call | solution.py:81
  3.9 0.0 collective-permute-done.other_table
  3.9 0.1 collective-permute-start.2
  4.0 3.1 %collective-permute-start.1 = (bf16[1,128,128]{2,1,0:T(8,128)(2,1)S(1)}, bf16[1,128,128]{2,1,0:T(8,128)(2,1)S(1)}, u32[]{:S(2)}, u32[]{:S(2)}) collective-permute-start(bf16[1,128,128]{2,1,0:T(8,128)(2,1)S(1)} %get-tuple-element.31), channel_id=1, source_target_pairs={{0,8},{1,9},{2,10},{3,11},{4,12},{5,13},{6,14},{7,15},{8,0},{9,1},... | collective-permute-start | bytes 98312 | tf_op jit(solution)/shard_map/ppermute | solution.py:237
  7.1 0.0 collective-permute-done.2
  7.1 1.9 %collective-permute-start.3 = (bf16[2,128,128]{2,1,0:T(8,128)(2,1)S(1)}, bf16[2,128,128]{2,1,0:T(8,128)(2,1)S(1)}, u32[]{:S(2)}, u32[]{:S(2)}) collective-permute-start(bf16[2,128,128]{2,1,0:T(8,128)(2,1)S(1)} %pad_maximum_fusion), channel_id=1, source_target_pairs={{0,12},{1,17},{2,14},{3,19},{4,8},{5,21},{6,10},{7,23},{8,20},{9,2... | collective-permute-start | bytes 196616 | tf_op jit(solution)/shard_map/ppermute | solution.py:237
  9.0 0.6 %collective-permute-start.4 = (bf16[2,128,128]{2,1,0:T(8,128)(2,1)S(1)}, bf16[2,128,128]{2,1,0:T(8,128)(2,1)S(1)}, u32[]{:S(2)}, u32[]{:S(2)}) collective-permute-start(bf16[2,128,128]{2,1,0:T(8,128)(2,1)S(1)} %pad_maximum_fusion.1), channel_id=1, source_target_pairs={{0,4},{1,21},{2,6},{3,23},{4,0},{5,17},{6,2},{7,19},{8,12},{9,29},... | collective-permute-start | bytes 196616 | tf_op jit(solution)/shard_map/ppermute | solution.py:237
  9.6 4.0 %collective-permute-start.5 = (bf16[2,128,128]{2,1,0:T(8,128)(2,1)S(1)}, bf16[2,128,128]{2,1,0:T(8,128)(2,1)S(1)}, u32[]{:S(2)}, u32[]{:S(2)}) collective-permute-start(bf16[2,128,128]{2,1,0:T(8,128)(2,1)S(1)} %pad_maximum_fusion.2), channel_id=1, source_target_pairs={{0,28},{1,25},{2,30},{3,27},{4,24},{5,29},{6,26},{7,31},{8,4},{9,1... | collective-permute-start | bytes 196616 | tf_op jit(solution)/shard_map/ppermute | solution.py:237
  13.6 0.0 collective-permute-done.1.received
  13.6 0.0 copy-done
  13.6 0.6 %first_sums.1 = (f32[8,128,128]{2,1,0:T(8,128)S(1)}, f32[6,8,8,128]{3,2,1,0:T(8,128)S(1)}) custom-call(s32[1,8]{1,0:T(1,128)S(1)} %copy-done, s32[1,8]{1,0:T(1,128)S(1)} %collective-permute-done.other_table, bf16[1,128,128]{2,1,0:T(8,128)(2,1)S(1)} %collective-permute-done.1.received, bf16[1,128,128]{2,1,0:T(8,128)(2,1)S(1)} %get-tuple-element.30.held), custom_call_target="tpu_custom_call" | custom-call | flops 2000000000 | bytes 1000000 | tf_op jit(solution)/shard_map/first_sums/pallas_call | solution.py:155
  14.2 0.0 collective-permute-done.3.early
  14.2 0.0 collective-permute-done.4.near
  14.2 1.2 %collective-permute-done.5.nearest = bf16[2,128,128]{2,1,0:T(8,128)(2,1)S(1)} collective-permute-done((bf16[2,128,128]{2,1,0:T(8,128)(2,1)S(1)}, bf16[2,128,128]{2,1,0:T(8,128)(2,1)S(1)}, u32[]{:S(2)}, u32[]{:S(2)}) %collective-permute-start.5) | collective-permute-done | bytes 65568 | tf_op jit(solution)/shard_map/ppermute | solution.py:237
  15.5 0.2 %second_sums.1 = (bf16[4,128,128]{2,1,0:T(8,128)(2,1)S(1)}, f32[4,128,128]{2,1,0:T(8,128)S(1)}) custom-call(f32[8,128,128]{2,1,0:T(8,128)S(1)} %get-tuple-element.20.part, f32[6,8,8,128]{3,2,1,0:T(8,128)S(1)} %get-tuple-element.21.chosen, bf16[2,128,128]{2,1,0:T(8,128)(2,1)S(1)} %collective-permute-done.3.early, ...), custom_call_target="tpu_custom_call" | custom-call | tf_op jit(solution)/shard_map/second_sums/pallas_call | solution.py:168
  15.7 0.9 %collective-permute-start.6 = (bf16[4,128,128]{2,1,0:T(8,128)(2,1)S(1)}, bf16[4,128,128]{2,1,0:T(8,128)(2,1)S(1)}, u32[]{:S(2)}, u32[]{:S(2)}) collective-permute-start(bf16[4,128,128]{2,1,0:T(8,128)(2,1)S(1)} %get-tuple-element.23), channel_id=1, source_target_pairs={{0,1},{1,0},{2,3},{3,2},{4,5},{5,4},{6,7},{7,6},{8,9},{9,8},{10,11... | collective-permute-start | bytes 393224 | tf_op jit(solution)/shard_map/ppermute | solution.py:247
  16.6 1.0 %collective-permute-done.6.received = bf16[4,128,128]{2,1,0:T(8,128)(2,1)S(1)} collective-permute-done((bf16[4,128,128]{2,1,0:T(8,128)(2,1)S(1)}, bf16[4,128,128]{2,1,0:T(8,128)(2,1)S(1)}, u32[]{:S(2)}, u32[]{:S(2)}) %collective-permute-start.6) | collective-permute-done | bytes 131104 | tf_op jit(solution)/shard_map/ppermute | solution.py:247
  17.6 1.6 %collective-permute-start.7 = (bf16[2,128,128]{2,1,0:T(8,128)(2,1)S(1)}, bf16[2,128,128]{2,1,0:T(8,128)(2,1)S(1)}, u32[]{:S(2)}, u32[]{:S(2)}) collective-permute-start(bf16[2,128,128]{2,1,0:T(8,128)(2,1)S(1)} %get-tuple-element.26), channel_id=1, source_target_pairs={{0,2},{1,3},{2,0},{3,1},{4,6},{5,7},{6,4},{7,5},{8,10},{9,11},{10,... | collective-permute-start | bytes 196616 | tf_op jit(solution)/shard_map/ppermute | solution.py:248
  19.1 2.9 %collective-permute-done.7 = bf16[2,128,128]{2,1,0:T(8,128)(2,1)S(1)} collective-permute-done((bf16[2,128,128]{2,1,0:T(8,128)(2,1)S(1)}, bf16[2,128,128]{2,1,0:T(8,128)(2,1)S(1)}, u32[]{:S(2)}, u32[]{:S(2)}) %collective-permute-start.7) | collective-permute-done | bytes 65568 | tf_op jit(solution)/shard_map/ppermute | solution.py:248
  22.0 0.7 %select_convert_fusion = bf16[2,128,128]{2,1,0:T(8,128)(2,1)} fusion(f32[2,128,128]{2,1,0:T(8,128)S(1)} %get-tuple-element.25, bf16[2,128,128]{2,1,0:T(8,128)(2,1)S(1)} %collective-permute-done.7, bf16[2,128,128]{2,1,0:T(8,128)(2,1)S(1)} %get-tuple-element.16), kind=kLoop, calls=%fused_computation | loop fusion | flops 163840 | bytes 327680 | tf_op jit(solution)/shard_map/convert_element_type | solution.py:249
  (6 shorter events, 0.1 us)
Async XLA Ops:
  0.0 3.9 %collective-permute-start = (s32[1,8]{1,0:T(1,128)}, s32[1,8]{1,0:T(1,128)S(1)}, u32[]{:S(2)}, u32[]{:S(2)}) collective-permute-start(s32[1,8]{1,0:T(1,128)} %own_table.1), channel_id=1, source_target_pairs={{0,1},{1,0},{2,3},{3,2},{4,5},{5,4},{6,7},{7,6},{8,9},{9,8},{10,11... | collective-permute-start | bytes 104 | tf_op jit(solution)/shard_map/ppermute | solution.py:212
  0.5 13.1 %copy-start = (s32[1,8]{1,0:T(1,128)S(1)}, s32[1,8]{1,0:T(1,128)}, u32[]{:S(2)}) copy-start(s32[1,8]{1,0:T(1,128)} %own_table.1) | copy-start | bytes 100
  3.9 3.2 %collective-permute-start.2 = (bf16[3,128,128]{2,1,0:T(8,128)(2,1)S(1)}, bf16[3,128,128]{2,1,0:T(8,128)(2,1)S(1)}, u32[]{:S(2)}, u32[]{:S(2)}) collective-permute-start(bf16[3,128,128]{2,1,0:T(8,128)(2,1)S(1)} %get-tuple-element.22), channel_id=1, source_target_pairs={{0,1},{1,0},{2,3},{3,2},{4,5},{5,4},{6,7},{7,6},{8,9},{9,8},{10,11... | collective-permute-start | bytes 294920 | tf_op jit(solution)/shard_map/ppermute | solution.py:240
  4.0 9.5 %collective-permute-start.1 = (bf16[1,128,128]{2,1,0:T(8,128)(2,1)S(1)}, bf16[1,128,128]{2,1,0:T(8,128)(2,1)S(1)}, u32[]{:S(2)}, u32[]{:S(2)}) collective-permute-start(bf16[1,128,128]{2,1,0:T(8,128)(2,1)S(1)} %get-tuple-element.31), channel_id=1, source_target_pairs={{0,8},{1,9},{2,10},{3,11},{4,12},{5,13},{6,14},{7,15},{8,0},{9,1},... | collective-permute-start | bytes 98312 | tf_op jit(solution)/shard_map/ppermute | solution.py:237
  7.1 7.1 %collective-permute-start.3 = (bf16[2,128,128]{2,1,0:T(8,128)(2,1)S(1)}, bf16[2,128,128]{2,1,0:T(8,128)(2,1)S(1)}, u32[]{:S(2)}, u32[]{:S(2)}) collective-permute-start(bf16[2,128,128]{2,1,0:T(8,128)(2,1)S(1)} %pad_maximum_fusion), channel_id=1, source_target_pairs={{0,12},{1,17},{2,14},{3,19},{4,8},{5,21},{6,10},{7,23},{8,20},{9,2... | collective-permute-start | bytes 196616 | tf_op jit(solution)/shard_map/ppermute | solution.py:237
  9.0 5.2 %collective-permute-start.4 = (bf16[2,128,128]{2,1,0:T(8,128)(2,1)S(1)}, bf16[2,128,128]{2,1,0:T(8,128)(2,1)S(1)}, u32[]{:S(2)}, u32[]{:S(2)}) collective-permute-start(bf16[2,128,128]{2,1,0:T(8,128)(2,1)S(1)} %pad_maximum_fusion.1), channel_id=1, source_target_pairs={{0,4},{1,21},{2,6},{3,23},{4,0},{5,17},{6,2},{7,19},{8,12},{9,29},... | collective-permute-start | bytes 196616 | tf_op jit(solution)/shard_map/ppermute | solution.py:237
  9.6 5.9 %collective-permute-start.5 = (bf16[2,128,128]{2,1,0:T(8,128)(2,1)S(1)}, bf16[2,128,128]{2,1,0:T(8,128)(2,1)S(1)}, u32[]{:S(2)}, u32[]{:S(2)}) collective-permute-start(bf16[2,128,128]{2,1,0:T(8,128)(2,1)S(1)} %pad_maximum_fusion.2), channel_id=1, source_target_pairs={{0,28},{1,25},{2,30},{3,27},{4,24},{5,29},{6,26},{7,31},{8,4},{9,1... | collective-permute-start | bytes 196616 | tf_op jit(solution)/shard_map/ppermute | solution.py:237
  15.7 1.8 %collective-permute-start.6 = (bf16[4,128,128]{2,1,0:T(8,128)(2,1)S(1)}, bf16[4,128,128]{2,1,0:T(8,128)(2,1)S(1)}, u32[]{:S(2)}, u32[]{:S(2)}) collective-permute-start(bf16[4,128,128]{2,1,0:T(8,128)(2,1)S(1)} %get-tuple-element.23), channel_id=1, source_target_pairs={{0,1},{1,0},{2,3},{3,2},{4,5},{5,4},{6,7},{7,6},{8,9},{9,8},{10,11... | collective-permute-start | bytes 393224 | tf_op jit(solution)/shard_map/ppermute | solution.py:247
  17.6 4.4 %collective-permute-start.7 = (bf16[2,128,128]{2,1,0:T(8,128)(2,1)S(1)}, bf16[2,128,128]{2,1,0:T(8,128)(2,1)S(1)}, u32[]{:S(2)}, u32[]{:S(2)}) collective-permute-start(bf16[2,128,128]{2,1,0:T(8,128)(2,1)S(1)} %get-tuple-element.26), channel_id=1, source_target_pairs={{0,2},{1,3},{2,0},{3,1},{4,6},{5,7},{6,4},{7,5},{8,10},{9,11},{10,... | collective-permute-start | bytes 196616 | tf_op jit(solution)/shard_map/ppermute | solution.py:248

commit v7 on v6

--- a/solution.py
+++ b/solution.py
@@ -123,10 +123,11 @@
     total[own_table[0, pair_at(0, 0, 1)]] = held[0].astype(jnp.float32)
     total[own_table[0, pair_at(*SHARED, -1)]] += received[0].astype(jnp.float32)
     targets = [table[0, pair_of(core, i, -1)] for i in range(3) for table in (own_table, other_table)]
+    chip = lax.axis_index("mpo") // 2
     for side, half in enumerate((1 - core, core)):
-        for x in range(2):
+        for here, x in enumerate((1 - chip, chip)):
             for j in range(quarter):
-                at = (side * 2 + x) * quarter + j
+                at = (side * 2 + here) * quarter + j
                 tile = (2 * x + half) * quarter + j
                 part[at] = total[tile]
                 for s, target in enumerate(targets):
@@ -134,19 +135,16 @@
                     chosen[s, at] = jnp.full(chosen.shape[2:], one, jnp.float32)
 
 
-def second_kernel(part, chosen, early, near, nearest, give, keep):
+def second_kernel(part, chosen, early, near, nearest, *outs):
     slots = [early[0], early[1], near[0], near[1], nearest[0], nearest[1]]
-    half, states = give.shape[0], give.shape[1]
-    for at in range(2 * half):
+    quarter, states = outs[0].shape[0], outs[0].shape[1]
+    for at in range(4 * quarter):
         tile = part[at].reshape(states // 8, 8, states)
         for s, slot in enumerate(slots):
             rows = slot.astype(jnp.float32).reshape(states // 8, 8, states)
             tile += rows * chosen[s, at][None]
-        tile = tile.reshape(states, states)
-        if at < half:
-            give[at] = tile.astype(jnp.bfloat16)
-        else:
-            keep[at - half] = tile
+        out = outs[at // quarter]
+        out[at % quarter] = tile.reshape(states, states).astype(out.dtype)
 
 
 def gather(own_table, other_table, held, early, near, nearest, shared, tiles):
@@ -168,38 +166,14 @@
     return pl.pallas_call(
         second_kernel,
         out_shape=[
-            jax.ShapeDtypeStruct((tiles // 2, states, states), jnp.bfloat16),
-            jax.ShapeDtypeStruct((tiles // 2, states, states), jnp.float32),
+            jax.ShapeDtypeStruct((tiles // 4, states, states), kind)
+            for kind in (jnp.bfloat16, jnp.bfloat16, jnp.bfloat16, jnp.float32)
         ],
         in_specs=[VMEM] * 5,
-        out_specs=[VMEM] * 2,
+        out_specs=[VMEM] * 4,
         compiler_params=pltpu.CompilerParams(vmem_limit_bytes=16 * 1024 * 1024),
         name="second_sums",
     )(part, chosen, early, near, nearest)
-
-
-def cross_kernel(received, kept, give, keep):
-    half = give.shape[0]
-    x = lax.axis_index("mpo") // 2
-    for j in range(half):
-        away, here = (1 - x) * half + j, x * half + j
-        give[j] = (kept[away] + received[away].astype(jnp.float32)).astype(jnp.bfloat16)
-        keep[j] = kept[here] + received[here].astype(jnp.float32)
-
-
-def cross(received, kept):
-    half, states = kept.shape[0] // 2, kept.shape[1]
-    return pl.pallas_call(
-        cross_kernel,
-        out_shape=[
-            jax.ShapeDtypeStruct((half, states, states), jnp.bfloat16),
-            jax.ShapeDtypeStruct((half, states, states), jnp.float32),
-        ],
-        in_specs=[VMEM] * 2,
-        out_specs=[VMEM] * 2,
-        compiler_params=pltpu.CompilerParams(vmem_limit_bytes=8 * 1024 * 1024),
-        name="cross",
-    )(received, kept)
 
 
 def by_permutes(sizes, wave, left, right, left_sizes, right_sizes, tile_left, tile_right, send_slot, recv_tile):
@@ -243,9 +217,12 @@
     received = [
         move(jnp.stack([keep[i], got[i]]), (SETS[0][i], SETS[1][i])) for i in range(3)
     ]
-    give, keep = gather(recv_tile, other_table, held, *received, shared, wave.shape[0])
-    give, keep = cross(lax.ppermute(give, "mpo", swap_core), keep)
-    summed = keep + lax.ppermute(give, "mpo", swap_chip).astype(jnp.float32)
+    swap_both = [(m, m ^ 3) for m in range(n_mpo)]
+    to_both, to_core, to_chip, summed = gather(
+        recv_tile, other_table, held, *received, shared, wave.shape[0]
+    )
+    for send, swap in ((to_chip, swap_chip), (to_both, swap_both), (to_core, swap_core)):
+        summed += lax.ppermute(send, "mpo", swap).astype(jnp.float32)
     return jnp.where(live > 0, summed, 0.0).astype(jnp.bfloat16)
 
 

time: 22.8 us -> 22.4 us (0.982)
  waiting for transfers between devices: 5.08 us -> 4.85 us
    ppermute x2 -> x3, waiting for transfers between devices: 3.84 us -> 3.61 us  [by_permutes(): summed += lax.ppermute(send, 'mpo', swap).astype(jnp.float32)]
    ppermute x2 -> x3, starting transfers between devices: 2.42 us -> 2.21 us  [by_permutes(): summed += lax.ppermute(send, 'mpo', swap).astype(jnp.float32)]
  transfers between devices with their start and end apart: 8 -> 9, of which waited for: 3 -> 3; matrix products, arithmetic and copies ran while one was open for 0% -> 0% of each run, Pallas kernels for 18% -> 18%
where the time goes in v7:
time: 22.4 us; the launch traced here: 22.2 us
  starting transfers between devices  12.3 us (55%)
  waiting for transfers between devices  4.85 us (22%)
  Pallas kernels  4.3 us (19%)
  other arithmetic  0.7 us (3%)
    ppermute x4, starting transfers between devices, move(): return lax.ppermute(x, axes, perm)  9.5 us
    ppermute x3, waiting for transfers between devices, by_permutes(): summed += lax.ppermute(send, 'mpo', swap).astype(jnp.float32)  3.61 us
    pallas_call x1, Pallas kernels, couple(): pl.pallas_call(functools.partial(couple_kernel, [g for g, _ in groups], s...  3.41 us
    ppermute x3, starting transfers between devices, by_permutes(): summed += lax.ppermute(send, 'mpo', swap).astype(jnp.float32)  2.21 us
    ppermute x4, waiting for transfers between devices, move(): return lax.ppermute(x, axes, perm)  1.24 us
    convert_element_type x1, other arithmetic, by_permutes(): return jnp.where(live > 0, summed, 0.0).astype(jnp.bfloat16)  0.68 us
    pallas_call x1, Pallas kernels, gather(): pl.pallas_call(first_kernel, out_shape=[jax.ShapeDtypeStruct(whole, jnp.f...  0.64 us
    ppermute x1, starting transfers between devices, by_permutes(): other_table = lax.ppermute(recv_tile, 'mpo', swap_core)  0.45 us
  transfers between devices with their start and end apart: 9, of which 3 were waited for; matrix products, arithmetic and copies ran while one was open for 0% of the time, Pallas kernels for 18%

profile of v7, /device:TPU:0, one launch (start us, length us, event | category | flops | bytes accessed | tf_op | source)
XLA Modules:
  0.0 22.2 jit_solution(18302140939809886482)
XLA Ops:
  0.0 0.5 %collective-permute-start = (s32[1,8]{1,0:T(1,128)}, s32[1,8]{1,0:T(1,128)S(1)}, u32[]{:S(2)}, u32[]{:S(2)}) collective-permute-start(s32[1,8]{1,0:T(1,128)} %own_table.1), channel_id=1, source_target_pairs={{0,1},{1,0},{2,3},{3,2},{4,5},{5,4},{6,7},{7,6},{8,9},{9,8},{10,11... | collective-permute-start | bytes 104 | tf_op jit(solution)/shard_map/ppermute | solution.py:186
  0.5 0.0 copy-start
  0.5 3.4 %couple.1 = (bf16[3,128,128]{2,1,0:T(8,128)(2,1)S(1)}, bf16[5,128,128]{2,1,0:T(8,128)(2,1)S(1)}, bf16[2,128,128]{2,1,0:T(8,128)(2,1)S(1)}) custom-call(s32[8]{0:T(128)} %refs_0_.1, s32[8]{0:T(128)} %refs_1_.1, s32[4]{0:T(128)} %refs_2_.1, s32[4]{0:T(128)} %refs_3_.1, s32[8,10]{1,0:T(8,128)} %bitcast.1, bf16[8,128,128]{2,1,0:T(8,128)(2,1)} %refs_5_.1, ...), custom_call_target="tpu_custom_call" | custom-call | tf_op jit(solution)/shard_map/couple/pallas_call | solution.py:81
  3.9 0.0 collective-permute-done.other_table
  3.9 0.1 collective-permute-start.2
  4.0 3.1 %collective-permute-start.1 = (bf16[1,128,128]{2,1,0:T(8,128)(2,1)S(1)}, bf16[1,128,128]{2,1,0:T(8,128)(2,1)S(1)}, u32[]{:S(2)}, u32[]{:S(2)}) collective-permute-start(bf16[1,128,128]{2,1,0:T(8,128)(2,1)S(1)} %get-tuple-element.31), channel_id=1, source_target_pairs={{0,8},{1,9},{2,10},{3,11},{4,12},{5,13},{6,14},{7,15},{8,0},{9,1},... | collective-permute-start | bytes 98312 | tf_op jit(solution)/shard_map/ppermute | solution.py:211
  7.1 0.0 collective-permute-done.2
  7.1 1.9 %collective-permute-start.3 = (bf16[2,128,128]{2,1,0:T(8,128)(2,1)S(1)}, bf16[2,128,128]{2,1,0:T(8,128)(2,1)S(1)}, u32[]{:S(2)}, u32[]{:S(2)}) collective-permute-start(bf16[2,128,128]{2,1,0:T(8,128)(2,1)S(1)} %pad_maximum_fusion), channel_id=1, source_target_pairs={{0,12},{1,17},{2,14},{3,19},{4,8},{5,21},{6,10},{7,23},{8,20},{9,2... | collective-permute-start | bytes 196616 | tf_op jit(solution)/shard_map/ppermute | solution.py:211
  9.0 0.6 %collective-permute-start.4 = (bf16[2,128,128]{2,1,0:T(8,128)(2,1)S(1)}, bf16[2,128,128]{2,1,0:T(8,128)(2,1)S(1)}, u32[]{:S(2)}, u32[]{:S(2)}) collective-permute-start(bf16[2,128,128]{2,1,0:T(8,128)(2,1)S(1)} %pad_maximum_fusion.1), channel_id=1, source_target_pairs={{0,4},{1,21},{2,6},{3,23},{4,0},{5,17},{6,2},{7,19},{8,12},{9,29},... | collective-permute-start | bytes 196616 | tf_op jit(solution)/shard_map/ppermute | solution.py:211
  9.6 4.0 %collective-permute-start.5 = (bf16[2,128,128]{2,1,0:T(8,128)(2,1)S(1)}, bf16[2,128,128]{2,1,0:T(8,128)(2,1)S(1)}, u32[]{:S(2)}, u32[]{:S(2)}) collective-permute-start(bf16[2,128,128]{2,1,0:T(8,128)(2,1)S(1)} %pad_maximum_fusion.2), channel_id=1, source_target_pairs={{0,28},{1,25},{2,30},{3,27},{4,24},{5,29},{6,26},{7,31},{8,4},{9,1... | collective-permute-start | bytes 196616 | tf_op jit(solution)/shard_map/ppermute | solution.py:211
  13.6 0.0 collective-permute-done.1.received
  13.6 0.0 copy-done
  13.6 0.6 %first_sums.1 = (f32[8,128,128]{2,1,0:T(8,128)S(1)}, f32[6,8,8,128]{3,2,1,0:T(8,128)S(1)}) custom-call(s32[1,8]{1,0:T(1,128)S(1)} %copy-done, s32[1,8]{1,0:T(1,128)S(1)} %collective-permute-done.other_table, bf16[1,128,128]{2,1,0:T(8,128)(2,1)S(1)} %collective-permute-done.1.received, bf16[1,128,128]{2,1,0:T(8,128)(2,1)S(1)} %get-tuple-element.30.held), custom_call_target="tpu_custom_call" | custom-call | flops 2000000000 | bytes 1000000 | tf_op jit(solution)/shard_map/first_sums/pallas_call | solution.py:153
  14.2 0.0 collective-permute-done.3.early
  14.2 0.0 collective-permute-done.4.near
  14.2 1.2 %collective-permute-done.5.nearest = bf16[2,128,128]{2,1,0:T(8,128)(2,1)S(1)} collective-permute-done((bf16[2,128,128]{2,1,0:T(8,128)(2,1)S(1)}, bf16[2,128,128]{2,1,0:T(8,128)(2,1)S(1)}, u32[]{:S(2)}, u32[]{:S(2)}) %collective-permute-start.5) | collective-permute-done | bytes 65568 | tf_op jit(solution)/shard_map/ppermute | solution.py:211
  15.5 0.2 %second_sums.1 = (bf16[2,128,128]{2,1,0:T(8,128)(2,1)S(1)}, bf16[2,128,128]{2,1,0:T(8,128)(2,1)S(1)}, bf16[2,128,128]{2,1,0:T(8,128)(2,1)S(1)}, f32[2,128,128]{2,1,0:T(8,128)S(1)}) custom-call(f32[8,128,128]{2,1,0:T(8,128)S(1)} %get-tuple-element.20.part, f32[6,8,8,128]{3,2,1,0:T(8,128)S(1)} %get-tuple-element.21.chosen, ...), custom_call_target="tpu_custom_call" | custom-call | tf_op jit(solution)/shard_map/second_sums/pallas_call | solution.py:166
  15.7 1.5 %collective-permute-start.6 = (bf16[2,128,128]{2,1,0:T(8,128)(2,1)S(1)}, bf16[2,128,128]{2,1,0:T(8,128)(2,1)S(1)}, u32[]{:S(2)}, u32[]{:S(2)}) collective-permute-start(bf16[2,128,128]{2,1,0:T(8,128)(2,1)S(1)} %get-tuple-element.24), channel_id=1, source_target_pairs={{0,2},{1,3},{2,0},{3,1},{4,6},{5,7},{6,4},{7,5},{8,10},{9,11},{10,... | collective-permute-start | bytes 196616 | tf_op jit(solution)/shard_map/ppermute | solution.py:225
  17.3 0.7 %collective-permute-start.7 = (bf16[2,128,128]{2,1,0:T(8,128)(2,1)S(1)}, bf16[2,128,128]{2,1,0:T(8,128)(2,1)S(1)}, u32[]{:S(2)}, u32[]{:S(2)}) collective-permute-start(bf16[2,128,128]{2,1,0:T(8,128)(2,1)S(1)} %get-tuple-element.25), channel_id=1, source_target_pairs={{0,3},{1,2},{2,1},{3,0},{4,7},{5,6},{6,5},{7,4},{8,11},{9,10},{10,... | collective-permute-start | bytes 196616 | tf_op jit(solution)/shard_map/ppermute | solution.py:225
  17.9 0.0 collective-permute-start.8
  17.9 2.8 %collective-permute-done.6 = bf16[2,128,128]{2,1,0:T(8,128)(2,1)S(1)} collective-permute-done((bf16[2,128,128]{2,1,0:T(8,128)(2,1)S(1)}, bf16[2,128,128]{2,1,0:T(8,128)(2,1)S(1)}, u32[]{:S(2)}, u32[]{:S(2)}) %collective-permute-start.6) | collective-permute-done | bytes 65568 | tf_op jit(solution)/shard_map/ppermute | solution.py:225
  20.7 0.8 %collective-permute-done.7 = bf16[2,128,128]{2,1,0:T(8,128)(2,1)S(1)} collective-permute-done((bf16[2,128,128]{2,1,0:T(8,128)(2,1)S(1)}, bf16[2,128,128]{2,1,0:T(8,128)(2,1)S(1)}, u32[]{:S(2)}, u32[]{:S(2)}) %collective-permute-start.7) | collective-permute-done | bytes 65568 | tf_op jit(solution)/shard_map/ppermute | solution.py:225
  21.5 0.0 collective-permute-done.8
  21.5 0.7 %select_convert_fusion = bf16[2,128,128]{2,1,0:T(8,128)(2,1)} fusion(bf16[2,128,128]{2,1,0:T(8,128)(2,1)S(1)} %collective-permute-done.8, bf16[2,128,128]{2,1,0:T(8,128)(2,1)S(1)} %collective-permute-done.7, f32[2,128,128]{2,1,0:T(8,128)S(1)} %get-tuple-element.23, bf16[2,128,128]{2,1,0:T(8,128)(2,1)S(1)} %collective-permute-done.6, ...), kind=kLoop, calls=%fused_computation | loop fusion | flops 294912 | bytes 458752 | tf_op jit(solution)/shard_map/convert_element_type | solution.py:226
  (5 shorter events, 0.0 us)
Async XLA Ops:
  0.0 3.9 %collective-permute-start = (s32[1,8]{1,0:T(1,128)}, s32[1,8]{1,0:T(1,128)S(1)}, u32[]{:S(2)}, u32[]{:S(2)}) collective-permute-start(s32[1,8]{1,0:T(1,128)} %own_table.1), channel_id=1, source_target_pairs={{0,1},{1,0},{2,3},{3,2},{4,5},{5,4},{6,7},{7,6},{8,9},{9,8},{10,11... | collective-permute-start | bytes 104 | tf_op jit(solution)/shard_map/ppermute | solution.py:186
  0.5 13.1 %copy-start = (s32[1,8]{1,0:T(1,128)S(1)}, s32[1,8]{1,0:T(1,128)}, u32[]{:S(2)}) copy-start(s32[1,8]{1,0:T(1,128)} %own_table.1) | copy-start | bytes 100
  3.9 3.2 %collective-permute-start.2 = (bf16[3,128,128]{2,1,0:T(8,128)(2,1)S(1)}, bf16[3,128,128]{2,1,0:T(8,128)(2,1)S(1)}, u32[]{:S(2)}, u32[]{:S(2)}) collective-permute-start(bf16[3,128,128]{2,1,0:T(8,128)(2,1)S(1)} %get-tuple-element.22), channel_id=1, source_target_pairs={{0,1},{1,0},{2,3},{3,2},{4,5},{5,4},{6,7},{7,6},{8,9},{9,8},{10,11... | collective-permute-start | bytes 294920 | tf_op jit(solution)/shard_map/ppermute | solution.py:214
  4.0 9.5 %collective-permute-start.1 = (bf16[1,128,128]{2,1,0:T(8,128)(2,1)S(1)}, bf16[1,128,128]{2,1,0:T(8,128)(2,1)S(1)}, u32[]{:S(2)}, u32[]{:S(2)}) collective-permute-start(bf16[1,128,128]{2,1,0:T(8,128)(2,1)S(1)} %get-tuple-element.31), channel_id=1, source_target_pairs={{0,8},{1,9},{2,10},{3,11},{4,12},{5,13},{6,14},{7,15},{8,0},{9,1},... | collective-permute-start | bytes 98312 | tf_op jit(solution)/shard_map/ppermute | solution.py:211
  7.1 7.1 %collective-permute-start.3 = (bf16[2,128,128]{2,1,0:T(8,128)(2,1)S(1)}, bf16[2,128,128]{2,1,0:T(8,128)(2,1)S(1)}, u32[]{:S(2)}, u32[]{:S(2)}) collective-permute-start(bf16[2,128,128]{2,1,0:T(8,128)(2,1)S(1)} %pad_maximum_fusion), channel_id=1, source_target_pairs={{0,12},{1,17},{2,14},{3,19},{4,8},{5,21},{6,10},{7,23},{8,20},{9,2... | collective-permute-start | bytes 196616 | tf_op jit(solution)/shard_map/ppermute | solution.py:211
  9.0 5.2 %collective-permute-start.4 = (bf16[2,128,128]{2,1,0:T(8,128)(2,1)S(1)}, bf16[2,128,128]{2,1,0:T(8,128)(2,1)S(1)}, u32[]{:S(2)}, u32[]{:S(2)}) collective-permute-start(bf16[2,128,128]{2,1,0:T(8,128)(2,1)S(1)} %pad_maximum_fusion.1), channel_id=1, source_target_pairs={{0,4},{1,21},{2,6},{3,23},{4,0},{5,17},{6,2},{7,19},{8,12},{9,29},... | collective-permute-start | bytes 196616 | tf_op jit(solution)/shard_map/ppermute | solution.py:211
  9.6 5.9 %collective-permute-start.5 = (bf16[2,128,128]{2,1,0:T(8,128)(2,1)S(1)}, bf16[2,128,128]{2,1,0:T(8,128)(2,1)S(1)}, u32[]{:S(2)}, u32[]{:S(2)}) collective-permute-start(bf16[2,128,128]{2,1,0:T(8,128)(2,1)S(1)} %pad_maximum_fusion.2), channel_id=1, source_target_pairs={{0,28},{1,25},{2,30},{3,27},{4,24},{5,29},{6,26},{7,31},{8,4},{9,1... | collective-permute-start | bytes 196616 | tf_op jit(solution)/shard_map/ppermute | solution.py:211
  15.7 5.0 %collective-permute-start.6 = (bf16[2,128,128]{2,1,0:T(8,128)(2,1)S(1)}, bf16[2,128,128]{2,1,0:T(8,128)(2,1)S(1)}, u32[]{:S(2)}, u32[]{:S(2)}) collective-permute-start(bf16[2,128,128]{2,1,0:T(8,128)(2,1)S(1)} %get-tuple-element.24), channel_id=1, source_target_pairs={{0,2},{1,3},{2,0},{3,1},{4,6},{5,7},{6,4},{7,5},{8,10},{9,11},{10,... | collective-permute-start | bytes 196616 | tf_op jit(solution)/shard_map/ppermute | solution.py:225
  17.3 4.3 %collective-permute-start.7 = (bf16[2,128,128]{2,1,0:T(8,128)(2,1)S(1)}, bf16[2,128,128]{2,1,0:T(8,128)(2,1)S(1)}, u32[]{:S(2)}, u32[]{:S(2)}) collective-permute-start(bf16[2,128,128]{2,1,0:T(8,128)(2,1)S(1)} %get-tuple-element.25), channel_id=1, source_target_pairs={{0,3},{1,2},{2,1},{3,0},{4,7},{5,6},{6,5},{7,4},{8,11},{9,10},{10,... | collective-permute-start | bytes 196616 | tf_op jit(solution)/shard_map/ppermute | solution.py:225
  17.9 3.6 %collective-permute-start.8 = (bf16[2,128,128]{2,1,0:T(8,128)(2,1)S(1)}, bf16[2,128,128]{2,1,0:T(8,128)(2,1)S(1)}, u32[]{:S(2)}, u32[]{:S(2)}) collective-permute-start(bf16[2,128,128]{2,1,0:T(8,128)(2,1)S(1)} %get-tuple-element.26), channel_id=1, source_target_pairs={{0,1},{1,0},{2,3},{3,2},{4,5},{5,4},{6,7},{7,6},{8,9},{9,8},{10,11... | collective-permute-start | bytes 196616 | tf_op jit(solution)/shard_map/ppermute | solution.py:225

commit v8 on v7

--- a/solution.py
+++ b/solution.py
@@ -35,10 +35,10 @@
     ]
     for copy in table_copies:
         copy.start()
+    right_copy = pltpu.make_async_copy(right_hbm, right, right_sem)
+    right_copy.start()
     wave_copy = pltpu.make_async_copy(wave_hbm, wave, wave_sem)
     wave_copy.start()
-    right_copy = pltpu.make_async_copy(right_hbm, right, right_sem)
-    right_copy.start()
     total[...] = jnp.zeros_like(total)
     for copy in table_copies:
         copy.wait()
@@ -210,7 +210,6 @@
         ]
         return lax.ppermute(x, axes, perm)
 
-    give, other_table = lax.optimization_barrier((give, other_table))
     got = lax.ppermute(give, "mpo", swap_core)
     keep, shared, held = rest[:3], rest[3:4], rest[4:]
     shared = move(shared, (SHARED, SHARED))

time: 22.4 us -> 22.4 us (level)
  no operation moved by 1% of the time
where the time goes in v8:
time: 22.4 us; the launch traced here: 22.2 us
  starting transfers between devices  12.3 us (55%)
  waiting for transfers between devices  4.84 us (22%)
  Pallas kernels  4.3 us (19%)
  other arithmetic  0.7 us (3%)
    ppermute x4, starting transfers between devices, move(): return lax.ppermute(x, axes, perm)  9.49 us
    ppermute x3, waiting for transfers between devices, by_permutes(): summed += lax.ppermute(send, 'mpo', swap).astype(jnp.float32)  3.61 us
    pallas_call x1, Pallas kernels, couple(): pl.pallas_call(functools.partial(couple_kernel, [g for g, _ in groups], s...  3.41 us
    ppermute x3, starting transfers between devices, by_permutes(): summed += lax.ppermute(send, 'mpo', swap).astype(jnp.float32)  2.21 us
    ppermute x4, waiting for transfers between devices, move(): return lax.ppermute(x, axes, perm)  1.23 us
    convert_element_type x1, other arithmetic, by_permutes(): return jnp.where(live > 0, summed, 0.0).astype(jnp.bfloat16)  0.68 us
    pallas_call x1, Pallas kernels, gather(): pl.pallas_call(first_kernel, out_shape=[jax.ShapeDtypeStruct(whole, jnp.f...  0.64 us
    ppermute x1, starting transfers between devices, by_permutes(): other_table = lax.ppermute(recv_tile, 'mpo', swap_core)  0.45 us
  transfers between devices with their start and end apart: 9, of which 3 were waited for; matrix products, arithmetic and copies ran while one was open for 0% of the time, Pallas kernels for 18%

profile of v8, /device:TPU:0, one launch (start us, length us, event | category | flops | bytes accessed | tf_op | source)
XLA Modules:
  0.0 22.2 jit_solution(11254793380175511867)
XLA Ops:
  0.0 0.5 %collective-permute-start = (s32[1,8]{1,0:T(1,128)}, s32[1,8]{1,0:T(1,128)S(1)}, u32[]{:S(2)}, u32[]{:S(2)}) collective-permute-start(s32[1,8]{1,0:T(1,128)} %own_table.1), channel_id=1, source_target_pairs={{0,1},{1,0},{2,3},{3,2},{4,5},{5,4},{6,7},{7,6},{8,9},{9,8},{10,11... | collective-permute-start | bytes 104 | tf_op jit(solution)/shard_map/ppermute | solution.py:186
  0.5 0.0 copy-start
  0.5 3.4 %couple.1 = (bf16[3,128,128]{2,1,0:T(8,128)(2,1)S(1)}, bf16[5,128,128]{2,1,0:T(8,128)(2,1)S(1)}, bf16[2,128,128]{2,1,0:T(8,128)(2,1)S(1)}) custom-call(s32[8]{0:T(128)} %refs_0_.1, s32[8]{0:T(128)} %refs_1_.1, s32[4]{0:T(128)} %refs_2_.1, s32[4]{0:T(128)} %refs_3_.1, s32[8,10]{1,0:T(8,128)} %bitcast.1, bf16[8,128,128]{2,1,0:T(8,128)(2,1)} %refs_5_.1, ...), custom_call_target="tpu_custom_call" | custom-call | tf_op jit(solution)/shard_map/couple/pallas_call | solution.py:81
  3.9 0.1 collective-permute-start.2
  4.0 3.1 %collective-permute-start.1 = (bf16[1,128,128]{2,1,0:T(8,128)(2,1)S(1)}, bf16[1,128,128]{2,1,0:T(8,128)(2,1)S(1)}, u32[]{:S(2)}, u32[]{:S(2)}) collective-permute-start(bf16[1,128,128]{2,1,0:T(8,128)(2,1)S(1)} %get-tuple-element.27), channel_id=1, source_target_pairs={{0,8},{1,9},{2,10},{3,11},{4,12},{5,13},{6,14},{7,15},{8,0},{9,1},... | collective-permute-start | bytes 98312 | tf_op jit(solution)/shard_map/ppermute | solution.py:211
  7.1 0.0 collective-permute-done.2
  7.1 1.9 %collective-permute-start.3 = (bf16[2,128,128]{2,1,0:T(8,128)(2,1)S(1)}, bf16[2,128,128]{2,1,0:T(8,128)(2,1)S(1)}, u32[]{:S(2)}, u32[]{:S(2)}) collective-permute-start(bf16[2,128,128]{2,1,0:T(8,128)(2,1)S(1)} %pad_maximum_fusion), channel_id=1, source_target_pairs={{0,12},{1,17},{2,14},{3,19},{4,8},{5,21},{6,10},{7,23},{8,20},{9,2... | collective-permute-start | bytes 196616 | tf_op jit(solution)/shard_map/ppermute | solution.py:211
  9.0 0.6 %collective-permute-start.4 = (bf16[2,128,128]{2,1,0:T(8,128)(2,1)S(1)}, bf16[2,128,128]{2,1,0:T(8,128)(2,1)S(1)}, u32[]{:S(2)}, u32[]{:S(2)}) collective-permute-start(bf16[2,128,128]{2,1,0:T(8,128)(2,1)S(1)} %pad_maximum_fusion.1), channel_id=1, source_target_pairs={{0,4},{1,21},{2,6},{3,23},{4,0},{5,17},{6,2},{7,19},{8,12},{9,29},... | collective-permute-start | bytes 196616 | tf_op jit(solution)/shard_map/ppermute | solution.py:211
  9.6 4.0 %collective-permute-start.5 = (bf16[2,128,128]{2,1,0:T(8,128)(2,1)S(1)}, bf16[2,128,128]{2,1,0:T(8,128)(2,1)S(1)}, u32[]{:S(2)}, u32[]{:S(2)}) collective-permute-start(bf16[2,128,128]{2,1,0:T(8,128)(2,1)S(1)} %pad_maximum_fusion.2), channel_id=1, source_target_pairs={{0,28},{1,25},{2,30},{3,27},{4,24},{5,29},{6,26},{7,31},{8,4},{9,1... | collective-permute-start | bytes 196616 | tf_op jit(solution)/shard_map/ppermute | solution.py:211
  13.6 0.0 collective-permute-done.other_table
  13.6 0.0 collective-permute-done.1.received
  13.6 0.0 copy-done
  13.6 0.6 %first_sums.1 = (f32[8,128,128]{2,1,0:T(8,128)S(1)}, f32[6,8,8,128]{3,2,1,0:T(8,128)S(1)}) custom-call(s32[1,8]{1,0:T(1,128)S(1)} %copy-done, s32[1,8]{1,0:T(1,128)S(1)} %collective-permute-done.other_table, bf16[1,128,128]{2,1,0:T(8,128)(2,1)S(1)} %collective-permute-done.1.received, bf16[1,128,128]{2,1,0:T(8,128)(2,1)S(1)} %get-tuple-element.26.held), custom_call_target="tpu_custom_call" | custom-call | flops 2000000000 | bytes 1000000 | tf_op jit(solution)/shard_map/first_sums/pallas_call | solution.py:153
  14.2 0.0 collective-permute-done.3.early
  14.2 0.0 collective-permute-done.4.near
  14.2 1.2 %collective-permute-done.5.nearest = bf16[2,128,128]{2,1,0:T(8,128)(2,1)S(1)} collective-permute-done((bf16[2,128,128]{2,1,0:T(8,128)(2,1)S(1)}, bf16[2,128,128]{2,1,0:T(8,128)(2,1)S(1)}, u32[]{:S(2)}, u32[]{:S(2)}) %collective-permute-start.5) | collective-permute-done | bytes 65568 | tf_op jit(solution)/shard_map/ppermute | solution.py:211
  15.5 0.2 %second_sums.1 = (bf16[2,128,128]{2,1,0:T(8,128)(2,1)S(1)}, bf16[2,128,128]{2,1,0:T(8,128)(2,1)S(1)}, bf16[2,128,128]{2,1,0:T(8,128)(2,1)S(1)}, f32[2,128,128]{2,1,0:T(8,128)S(1)}) custom-call(f32[8,128,128]{2,1,0:T(8,128)S(1)} %get-tuple-element.16.part, f32[6,8,8,128]{3,2,1,0:T(8,128)S(1)} %get-tuple-element.17.chosen, ...), custom_call_target="tpu_custom_call" | custom-call | tf_op jit(solution)/shard_map/second_sums/pallas_call | solution.py:166
  15.7 1.6 %collective-permute-start.6 = (bf16[2,128,128]{2,1,0:T(8,128)(2,1)S(1)}, bf16[2,128,128]{2,1,0:T(8,128)(2,1)S(1)}, u32[]{:S(2)}, u32[]{:S(2)}) collective-permute-start(bf16[2,128,128]{2,1,0:T(8,128)(2,1)S(1)} %get-tuple-element.20), channel_id=1, source_target_pairs={{0,2},{1,3},{2,0},{3,1},{4,6},{5,7},{6,4},{7,5},{8,10},{9,11},{10,... | collective-permute-start | bytes 196616 | tf_op jit(solution)/shard_map/ppermute | solution.py:224
  17.3 0.6 %collective-permute-start.7 = (bf16[2,128,128]{2,1,0:T(8,128)(2,1)S(1)}, bf16[2,128,128]{2,1,0:T(8,128)(2,1)S(1)}, u32[]{:S(2)}, u32[]{:S(2)}) collective-permute-start(bf16[2,128,128]{2,1,0:T(8,128)(2,1)S(1)} %get-tuple-element.21), channel_id=1, source_target_pairs={{0,3},{1,2},{2,1},{3,0},{4,7},{5,6},{6,5},{7,4},{8,11},{9,10},{10,... | collective-permute-start | bytes 196616 | tf_op jit(solution)/shard_map/ppermute | solution.py:224
  17.9 0.0 collective-permute-start.8
  17.9 2.8 %collective-permute-done.6 = bf16[2,128,128]{2,1,0:T(8,128)(2,1)S(1)} collective-permute-done((bf16[2,128,128]{2,1,0:T(8,128)(2,1)S(1)}, bf16[2,128,128]{2,1,0:T(8,128)(2,1)S(1)}, u32[]{:S(2)}, u32[]{:S(2)}) %collective-permute-start.6) | collective-permute-done | bytes 65568 | tf_op jit(solution)/shard_map/ppermute | solution.py:224
  20.7 0.8 %collective-permute-done.7 = bf16[2,128,128]{2,1,0:T(8,128)(2,1)S(1)} collective-permute-done((bf16[2,128,128]{2,1,0:T(8,128)(2,1)S(1)}, bf16[2,128,128]{2,1,0:T(8,128)(2,1)S(1)}, u32[]{:S(2)}, u32[]{:S(2)}) %collective-permute-start.7) | collective-permute-done | bytes 65568 | tf_op jit(solution)/shard_map/ppermute | solution.py:224
  21.5 0.0 collective-permute-done.8
  21.5 0.7 %select_convert_fusion = bf16[2,128,128]{2,1,0:T(8,128)(2,1)} fusion(bf16[2,128,128]{2,1,0:T(8,128)(2,1)S(1)} %collective-permute-done.8, bf16[2,128,128]{2,1,0:T(8,128)(2,1)S(1)} %collective-permute-done.7, f32[2,128,128]{2,1,0:T(8,128)S(1)} %get-tuple-element.19, bf16[2,128,128]{2,1,0:T(8,128)(2,1)S(1)} %collective-permute-done.6, ...), kind=kLoop, calls=%fused_computation | loop fusion | flops 294912 | bytes 458752 | tf_op jit(solution)/shard_map/convert_element_type | solution.py:225
  (5 shorter events, 0.0 us)
Async XLA Ops:
  0.0 13.6 %collective-permute-start = (s32[1,8]{1,0:T(1,128)}, s32[1,8]{1,0:T(1,128)S(1)}, u32[]{:S(2)}, u32[]{:S(2)}) collective-permute-start(s32[1,8]{1,0:T(1,128)} %own_table.1), channel_id=1, source_target_pairs={{0,1},{1,0},{2,3},{3,2},{4,5},{5,4},{6,7},{7,6},{8,9},{9,8},{10,11... | collective-permute-start | bytes 104 | tf_op jit(solution)/shard_map/ppermute | solution.py:186
  0.5 13.1 %copy-start = (s32[1,8]{1,0:T(1,128)S(1)}, s32[1,8]{1,0:T(1,128)}, u32[]{:S(2)}) copy-start(s32[1,8]{1,0:T(1,128)} %own_table.1) | copy-start | bytes 100
  3.9 3.2 %collective-permute-start.2 = (bf16[3,128,128]{2,1,0:T(8,128)(2,1)S(1)}, bf16[3,128,128]{2,1,0:T(8,128)(2,1)S(1)}, u32[]{:S(2)}, u32[]{:S(2)}) collective-permute-start(bf16[3,128,128]{2,1,0:T(8,128)(2,1)S(1)} %get-tuple-element.18), channel_id=1, source_target_pairs={{0,1},{1,0},{2,3},{3,2},{4,5},{5,4},{6,7},{7,6},{8,9},{9,8},{10,11... | collective-permute-start | bytes 294920 | tf_op jit(solution)/shard_map/ppermute | solution.py:213
  4.0 9.5 %collective-permute-start.1 = (bf16[1,128,128]{2,1,0:T(8,128)(2,1)S(1)}, bf16[1,128,128]{2,1,0:T(8,128)(2,1)S(1)}, u32[]{:S(2)}, u32[]{:S(2)}) collective-permute-start(bf16[1,128,128]{2,1,0:T(8,128)(2,1)S(1)} %get-tuple-element.27), channel_id=1, source_target_pairs={{0,8},{1,9},{2,10},{3,11},{4,12},{5,13},{6,14},{7,15},{8,0},{9,1},... | collective-permute-start | bytes 98312 | tf_op jit(solution)/shard_map/ppermute | solution.py:211
  7.1 7.1 %collective-permute-start.3 = (bf16[2,128,128]{2,1,0:T(8,128)(2,1)S(1)}, bf16[2,128,128]{2,1,0:T(8,128)(2,1)S(1)}, u32[]{:S(2)}, u32[]{:S(2)}) collective-permute-start(bf16[2,128,128]{2,1,0:T(8,128)(2,1)S(1)} %pad_maximum_fusion), channel_id=1, source_target_pairs={{0,12},{1,17},{2,14},{3,19},{4,8},{5,21},{6,10},{7,23},{8,20},{9,2... | collective-permute-start | bytes 196616 | tf_op jit(solution)/shard_map/ppermute | solution.py:211
  9.0 5.2 %collective-permute-start.4 = (bf16[2,128,128]{2,1,0:T(8,128)(2,1)S(1)}, bf16[2,128,128]{2,1,0:T(8,128)(2,1)S(1)}, u32[]{:S(2)}, u32[]{:S(2)}) collective-permute-start(bf16[2,128,128]{2,1,0:T(8,128)(2,1)S(1)} %pad_maximum_fusion.1), channel_id=1, source_target_pairs={{0,4},{1,21},{2,6},{3,23},{4,0},{5,17},{6,2},{7,19},{8,12},{9,29},... | collective-permute-start | bytes 196616 | tf_op jit(solution)/shard_map/ppermute | solution.py:211
  9.6 5.9 %collective-permute-start.5 = (bf16[2,128,128]{2,1,0:T(8,128)(2,1)S(1)}, bf16[2,128,128]{2,1,0:T(8,128)(2,1)S(1)}, u32[]{:S(2)}, u32[]{:S(2)}) collective-permute-start(bf16[2,128,128]{2,1,0:T(8,128)(2,1)S(1)} %pad_maximum_fusion.2), channel_id=1, source_target_pairs={{0,28},{1,25},{2,30},{3,27},{4,24},{5,29},{6,26},{7,31},{8,4},{9,1... | collective-permute-start | bytes 196616 | tf_op jit(solution)/shard_map/ppermute | solution.py:211
  15.7 5.0 %collective-permute-start.6 = (bf16[2,128,128]{2,1,0:T(8,128)(2,1)S(1)}, bf16[2,128,128]{2,1,0:T(8,128)(2,1)S(1)}, u32[]{:S(2)}, u32[]{:S(2)}) collective-permute-start(bf16[2,128,128]{2,1,0:T(8,128)(2,1)S(1)} %get-tuple-element.20), channel_id=1, source_target_pairs={{0,2},{1,3},{2,0},{3,1},{4,6},{5,7},{6,4},{7,5},{8,10},{9,11},{10,... | collective-permute-start | bytes 196616 | tf_op jit(solution)/shard_map/ppermute | solution.py:224
  17.3 4.3 %collective-permute-start.7 = (bf16[2,128,128]{2,1,0:T(8,128)(2,1)S(1)}, bf16[2,128,128]{2,1,0:T(8,128)(2,1)S(1)}, u32[]{:S(2)}, u32[]{:S(2)}) collective-permute-start(bf16[2,128,128]{2,1,0:T(8,128)(2,1)S(1)} %get-tuple-element.21), channel_id=1, source_target_pairs={{0,3},{1,2},{2,1},{3,0},{4,7},{5,6},{6,5},{7,4},{8,11},{9,10},{10,... | collective-permute-start | bytes 196616 | tf_op jit(solution)/shard_map/ppermute | solution.py:224
  17.9 3.6 %collective-permute-start.8 = (bf16[2,128,128]{2,1,0:T(8,128)(2,1)S(1)}, bf16[2,128,128]{2,1,0:T(8,128)(2,1)S(1)}, u32[]{:S(2)}, u32[]{:S(2)}) collective-permute-start(bf16[2,128,128]{2,1,0:T(8,128)(2,1)S(1)} %get-tuple-element.22), channel_id=1, source_target_pairs={{0,1},{1,0},{2,3},{3,2},{4,5},{5,4},{6,7},{7,6},{8,9},{9,8},{10,11... | collective-permute-start | bytes 196616 | tf_op jit(solution)/shard_map/ppermute | solution.py:224

commit v9 on v7

--- a/solution.py
+++ b/solution.py
@@ -101,7 +101,7 @@
     )(*in_hbm(*tables, wave, left, right))
 
 
-SETS = (((1, 1), (0, 1), (3, 1)), ((2, 0), (2, 1), (3, 0)))
+SETS = (((1, 1), (0, 1), (3, 1)), ((2, 1), (2, 0), (3, 0)))
 SHARED = (1, 0)
 
 

time: 22.4 us -> 22.4 us (level)
  no operation moved by 1% of the time
where the time goes in v9:
time: 22.4 us; the launch traced here: 22.3 us
  starting transfers between devices  12.3 us (55%)
  waiting for transfers between devices  4.85 us (22%)
  Pallas kernels  4.29 us (19%)
  other arithmetic  0.7 us (3%)
    ppermute x4, starting transfers between devices, move(): return lax.ppermute(x, axes, perm)  9.49 us
    ppermute x3, waiting for transfers between devices, by_permutes(): summed += lax.ppermute(send, 'mpo', swap).astype(jnp.float32)  3.61 us
    pallas_call x1, Pallas kernels, couple(): pl.pallas_call(functools.partial(couple_kernel, [g for g, _ in groups], s...  3.41 us
    ppermute x3, starting transfers between devices, by_permutes(): summed += lax.ppermute(send, 'mpo', swap).astype(jnp.float32)  2.26 us
    ppermute x4, waiting for transfers between devices, move(): return lax.ppermute(x, axes, perm)  1.24 us
    convert_element_type x1, other arithmetic, by_permutes(): return jnp.where(live > 0, summed, 0.0).astype(jnp.bfloat16)  0.68 us
    pallas_call x1, Pallas kernels, gather(): pl.pallas_call(first_kernel, out_shape=[jax.ShapeDtypeStruct(whole, jnp.f...  0.64 us
    ppermute x1, starting transfers between devices, by_permutes(): other_table = lax.ppermute(recv_tile, 'mpo', swap_core)  0.45 us
  transfers between devices with their start and end apart: 9, of which 3 were waited for; matrix products, arithmetic and copies ran while one was open for 0% of the time, Pallas kernels for 18%

profile of v9, /device:TPU:0, one launch (start us, length us, event | category | flops | bytes accessed | tf_op | source)
XLA Modules:
  0.0 22.3 jit_solution(1420198495894727134)
XLA Ops:
  0.0 0.5 %collective-permute-start = (s32[1,8]{1,0:T(1,128)}, s32[1,8]{1,0:T(1,128)S(1)}, u32[]{:S(2)}, u32[]{:S(2)}) collective-permute-start(s32[1,8]{1,0:T(1,128)} %own_table.1), channel_id=1, source_target_pairs={{0,1},{1,0},{2,3},{3,2},{4,5},{5,4},{6,7},{7,6},{8,9},{9,8},{10,11... | collective-permute-start | bytes 104 | tf_op jit(solution)/shard_map/ppermute | solution.py:186
  0.5 0.0 copy-start
  0.5 3.4 %couple.1 = (bf16[3,128,128]{2,1,0:T(8,128)(2,1)S(1)}, bf16[5,128,128]{2,1,0:T(8,128)(2,1)S(1)}, bf16[2,128,128]{2,1,0:T(8,128)(2,1)S(1)}) custom-call(s32[8]{0:T(128)} %refs_0_.1, s32[8]{0:T(128)} %refs_1_.1, s32[4]{0:T(128)} %refs_2_.1, s32[4]{0:T(128)} %refs_3_.1, s32[8,10]{1,0:T(8,128)} %bitcast.1, bf16[8,128,128]{2,1,0:T(8,128)(2,1)} %refs_5_.1, ...), custom_call_target="tpu_custom_call" | custom-call | tf_op jit(solution)/shard_map/couple/pallas_call | solution.py:81
  3.9 0.0 collective-permute-done.other_table
  3.9 0.1 collective-permute-start.2
  4.0 3.1 %collective-permute-start.1 = (bf16[1,128,128]{2,1,0:T(8,128)(2,1)S(1)}, bf16[1,128,128]{2,1,0:T(8,128)(2,1)S(1)}, u32[]{:S(2)}, u32[]{:S(2)}) collective-permute-start(bf16[1,128,128]{2,1,0:T(8,128)(2,1)S(1)} %get-tuple-element.31), channel_id=1, source_target_pairs={{0,8},{1,9},{2,10},{3,11},{4,12},{5,13},{6,14},{7,15},{8,0},{9,1},... | collective-permute-start | bytes 98312 | tf_op jit(solution)/shard_map/ppermute | solution.py:211
  7.1 0.0 collective-permute-done.2
  7.1 1.9 %collective-permute-start.3 = (bf16[2,128,128]{2,1,0:T(8,128)(2,1)S(1)}, bf16[2,128,128]{2,1,0:T(8,128)(2,1)S(1)}, u32[]{:S(2)}, u32[]{:S(2)}) collective-permute-start(bf16[2,128,128]{2,1,0:T(8,128)(2,1)S(1)} %pad_maximum_fusion), channel_id=1, source_target_pairs={{0,12},{1,21},{2,14},{3,23},{4,8},{5,17},{6,10},{7,19},{8,20},{9,2... | collective-permute-start | bytes 196616 | tf_op jit(solution)/shard_map/ppermute | solution.py:211
  9.0 0.6 %collective-permute-start.4 = (bf16[2,128,128]{2,1,0:T(8,128)(2,1)S(1)}, bf16[2,128,128]{2,1,0:T(8,128)(2,1)S(1)}, u32[]{:S(2)}, u32[]{:S(2)}) collective-permute-start(bf16[2,128,128]{2,1,0:T(8,128)(2,1)S(1)} %pad_maximum_fusion.1), channel_id=1, source_target_pairs={{0,4},{1,17},{2,6},{3,19},{4,0},{5,21},{6,2},{7,23},{8,12},{9,25},... | collective-permute-start | bytes 196616 | tf_op jit(solution)/shard_map/ppermute | solution.py:211
  9.6 4.0 %collective-permute-start.5 = (bf16[2,128,128]{2,1,0:T(8,128)(2,1)S(1)}, bf16[2,128,128]{2,1,0:T(8,128)(2,1)S(1)}, u32[]{:S(2)}, u32[]{:S(2)}) collective-permute-start(bf16[2,128,128]{2,1,0:T(8,128)(2,1)S(1)} %pad_maximum_fusion.2), channel_id=1, source_target_pairs={{0,28},{1,25},{2,30},{3,27},{4,24},{5,29},{6,26},{7,31},{8,4},{9,1... | collective-permute-start | bytes 196616 | tf_op jit(solution)/shard_map/ppermute | solution.py:211
  13.6 0.0 collective-permute-done.1.received
  13.6 0.0 copy-done
  13.6 0.6 %first_sums.1 = (f32[8,128,128]{2,1,0:T(8,128)S(1)}, f32[6,8,8,128]{3,2,1,0:T(8,128)S(1)}) custom-call(s32[1,8]{1,0:T(1,128)S(1)} %copy-done, s32[1,8]{1,0:T(1,128)S(1)} %collective-permute-done.other_table, bf16[1,128,128]{2,1,0:T(8,128)(2,1)S(1)} %collective-permute-done.1.received, bf16[1,128,128]{2,1,0:T(8,128)(2,1)S(1)} %get-tuple-element.30.held), custom_call_target="tpu_custom_call" | custom-call | flops 2000000000 | bytes 1000000 | tf_op jit(solution)/shard_map/first_sums/pallas_call | solution.py:153
  14.2 0.0 collective-permute-done.3.early
  14.2 0.0 collective-permute-done.4.near
  14.2 1.2 %collective-permute-done.5.nearest = bf16[2,128,128]{2,1,0:T(8,128)(2,1)S(1)} collective-permute-done((bf16[2,128,128]{2,1,0:T(8,128)(2,1)S(1)}, bf16[2,128,128]{2,1,0:T(8,128)(2,1)S(1)}, u32[]{:S(2)}, u32[]{:S(2)}) %collective-permute-start.5) | collective-permute-done | bytes 65568 | tf_op jit(solution)/shard_map/ppermute | solution.py:211
  15.5 0.2 %second_sums.1 = (bf16[2,128,128]{2,1,0:T(8,128)(2,1)S(1)}, bf16[2,128,128]{2,1,0:T(8,128)(2,1)S(1)}, bf16[2,128,128]{2,1,0:T(8,128)(2,1)S(1)}, f32[2,128,128]{2,1,0:T(8,128)S(1)}) custom-call(f32[8,128,128]{2,1,0:T(8,128)S(1)} %get-tuple-element.20.part, f32[6,8,8,128]{3,2,1,0:T(8,128)S(1)} %get-tuple-element.21.chosen, ...), custom_call_target="tpu_custom_call" | custom-call | tf_op jit(solution)/shard_map/second_sums/pallas_call | solution.py:166
  15.7 1.6 %collective-permute-start.6 = (bf16[2,128,128]{2,1,0:T(8,128)(2,1)S(1)}, bf16[2,128,128]{2,1,0:T(8,128)(2,1)S(1)}, u32[]{:S(2)}, u32[]{:S(2)}) collective-permute-start(bf16[2,128,128]{2,1,0:T(8,128)(2,1)S(1)} %get-tuple-element.24), channel_id=1, source_target_pairs={{0,2},{1,3},{2,0},{3,1},{4,6},{5,7},{6,4},{7,5},{8,10},{9,11},{10,... | collective-permute-start | bytes 196616 | tf_op jit(solution)/shard_map/ppermute | solution.py:225
  17.3 0.7 %collective-permute-start.7 = (bf16[2,128,128]{2,1,0:T(8,128)(2,1)S(1)}, bf16[2,128,128]{2,1,0:T(8,128)(2,1)S(1)}, u32[]{:S(2)}, u32[]{:S(2)}) collective-permute-start(bf16[2,128,128]{2,1,0:T(8,128)(2,1)S(1)} %get-tuple-element.25), channel_id=1, source_target_pairs={{0,3},{1,2},{2,1},{3,0},{4,7},{5,6},{6,5},{7,4},{8,11},{9,10},{10,... | collective-permute-start | bytes 196616 | tf_op jit(solution)/shard_map/ppermute | solution.py:225
  18.0 0.0 collective-permute-start.8
  18.0 2.8 %collective-permute-done.6 = bf16[2,128,128]{2,1,0:T(8,128)(2,1)S(1)} collective-permute-done((bf16[2,128,128]{2,1,0:T(8,128)(2,1)S(1)}, bf16[2,128,128]{2,1,0:T(8,128)(2,1)S(1)}, u32[]{:S(2)}, u32[]{:S(2)}) %collective-permute-start.6) | collective-permute-done | bytes 65568 | tf_op jit(solution)/shard_map/ppermute | solution.py:225
  20.7 0.8 %collective-permute-done.7 = bf16[2,128,128]{2,1,0:T(8,128)(2,1)S(1)} collective-permute-done((bf16[2,128,128]{2,1,0:T(8,128)(2,1)S(1)}, bf16[2,128,128]{2,1,0:T(8,128)(2,1)S(1)}, u32[]{:S(2)}, u32[]{:S(2)}) %collective-permute-start.7) | collective-permute-done | bytes 65568 | tf_op jit(solution)/shard_map/ppermute | solution.py:225
  21.6 0.0 collective-permute-done.8
  21.6 0.7 %select_convert_fusion = bf16[2,128,128]{2,1,0:T(8,128)(2,1)} fusion(bf16[2,128,128]{2,1,0:T(8,128)(2,1)S(1)} %collective-permute-done.8, bf16[2,128,128]{2,1,0:T(8,128)(2,1)S(1)} %collective-permute-done.7, f32[2,128,128]{2,1,0:T(8,128)S(1)} %get-tuple-element.23, bf16[2,128,128]{2,1,0:T(8,128)(2,1)S(1)} %collective-permute-done.6, ...), kind=kLoop, calls=%fused_computation | loop fusion | flops 294912 | bytes 458752 | tf_op jit(solution)/shard_map/convert_element_type | solution.py:226
  (5 shorter events, 0.0 us)
Async XLA Ops:
  0.0 3.9 %collective-permute-start = (s32[1,8]{1,0:T(1,128)}, s32[1,8]{1,0:T(1,128)S(1)}, u32[]{:S(2)}, u32[]{:S(2)}) collective-permute-start(s32[1,8]{1,0:T(1,128)} %own_table.1), channel_id=1, source_target_pairs={{0,1},{1,0},{2,3},{3,2},{4,5},{5,4},{6,7},{7,6},{8,9},{9,8},{10,11... | collective-permute-start | bytes 104 | tf_op jit(solution)/shard_map/ppermute | solution.py:186
  0.5 13.1 %copy-start = (s32[1,8]{1,0:T(1,128)S(1)}, s32[1,8]{1,0:T(1,128)}, u32[]{:S(2)}) copy-start(s32[1,8]{1,0:T(1,128)} %own_table.1) | copy-start | bytes 100
  3.9 3.2 %collective-permute-start.2 = (bf16[3,128,128]{2,1,0:T(8,128)(2,1)S(1)}, bf16[3,128,128]{2,1,0:T(8,128)(2,1)S(1)}, u32[]{:S(2)}, u32[]{:S(2)}) collective-permute-start(bf16[3,128,128]{2,1,0:T(8,128)(2,1)S(1)} %get-tuple-element.22), channel_id=1, source_target_pairs={{0,1},{1,0},{2,3},{3,2},{4,5},{5,4},{6,7},{7,6},{8,9},{9,8},{10,11... | collective-permute-start | bytes 294920 | tf_op jit(solution)/shard_map/ppermute | solution.py:214
  4.0 9.5 %collective-permute-start.1 = (bf16[1,128,128]{2,1,0:T(8,128)(2,1)S(1)}, bf16[1,128,128]{2,1,0:T(8,128)(2,1)S(1)}, u32[]{:S(2)}, u32[]{:S(2)}) collective-permute-start(bf16[1,128,128]{2,1,0:T(8,128)(2,1)S(1)} %get-tuple-element.31), channel_id=1, source_target_pairs={{0,8},{1,9},{2,10},{3,11},{4,12},{5,13},{6,14},{7,15},{8,0},{9,1},... | collective-permute-start | bytes 98312 | tf_op jit(solution)/shard_map/ppermute | solution.py:211
  7.1 7.1 %collective-permute-start.3 = (bf16[2,128,128]{2,1,0:T(8,128)(2,1)S(1)}, bf16[2,128,128]{2,1,0:T(8,128)(2,1)S(1)}, u32[]{:S(2)}, u32[]{:S(2)}) collective-permute-start(bf16[2,128,128]{2,1,0:T(8,128)(2,1)S(1)} %pad_maximum_fusion), channel_id=1, source_target_pairs={{0,12},{1,21},{2,14},{3,23},{4,8},{5,17},{6,10},{7,19},{8,20},{9,2... | collective-permute-start | bytes 196616 | tf_op jit(solution)/shard_map/ppermute | solution.py:211
  9.0 5.2 %collective-permute-start.4 = (bf16[2,128,128]{2,1,0:T(8,128)(2,1)S(1)}, bf16[2,128,128]{2,1,0:T(8,128)(2,1)S(1)}, u32[]{:S(2)}, u32[]{:S(2)}) collective-permute-start(bf16[2,128,128]{2,1,0:T(8,128)(2,1)S(1)} %pad_maximum_fusion.1), channel_id=1, source_target_pairs={{0,4},{1,17},{2,6},{3,19},{4,0},{5,21},{6,2},{7,23},{8,12},{9,25},... | collective-permute-start | bytes 196616 | tf_op jit(solution)/shard_map/ppermute | solution.py:211
  9.6 5.9 %collective-permute-start.5 = (bf16[2,128,128]{2,1,0:T(8,128)(2,1)S(1)}, bf16[2,128,128]{2,1,0:T(8,128)(2,1)S(1)}, u32[]{:S(2)}, u32[]{:S(2)}) collective-permute-start(bf16[2,128,128]{2,1,0:T(8,128)(2,1)S(1)} %pad_maximum_fusion.2), channel_id=1, source_target_pairs={{0,28},{1,25},{2,30},{3,27},{4,24},{5,29},{6,26},{7,31},{8,4},{9,1... | collective-permute-start | bytes 196616 | tf_op jit(solution)/shard_map/ppermute | solution.py:211
  15.7 5.0 %collective-permute-start.6 = (bf16[2,128,128]{2,1,0:T(8,128)(2,1)S(1)}, bf16[2,128,128]{2,1,0:T(8,128)(2,1)S(1)}, u32[]{:S(2)}, u32[]{:S(2)}) collective-permute-start(bf16[2,128,128]{2,1,0:T(8,128)(2,1)S(1)} %get-tuple-element.24), channel_id=1, source_target_pairs={{0,2},{1,3},{2,0},{3,1},{4,6},{5,7},{6,4},{7,5},{8,10},{9,11},{10,... | collective-permute-start | bytes 196616 | tf_op jit(solution)/shard_map/ppermute | solution.py:225
  17.3 4.3 %collective-permute-start.7 = (bf16[2,128,128]{2,1,0:T(8,128)(2,1)S(1)}, bf16[2,128,128]{2,1,0:T(8,128)(2,1)S(1)}, u32[]{:S(2)}, u32[]{:S(2)}) collective-permute-start(bf16[2,128,128]{2,1,0:T(8,128)(2,1)S(1)} %get-tuple-element.25), channel_id=1, source_target_pairs={{0,3},{1,2},{2,1},{3,0},{4,7},{5,6},{6,5},{7,4},{8,11},{9,10},{10,... | collective-permute-start | bytes 196616 | tf_op jit(solution)/shard_map/ppermute | solution.py:225
  18.0 3.6 %collective-permute-start.8 = (bf16[2,128,128]{2,1,0:T(8,128)(2,1)S(1)}, bf16[2,128,128]{2,1,0:T(8,128)(2,1)S(1)}, u32[]{:S(2)}, u32[]{:S(2)}) collective-permute-start(bf16[2,128,128]{2,1,0:T(8,128)(2,1)S(1)} %get-tuple-element.26), channel_id=1, source_target_pairs={{0,1},{1,0},{2,3},{3,2},{4,5},{5,4},{6,7},{7,6},{8,9},{9,8},{10,11... | collective-permute-start | bytes 196616 | tf_op jit(solution)/shard_map/ppermute | solution.py:225
